TPU v7x, 32 devices: a whole 2x2x4 slice. The times are simulated.
32 devices in a mesh: tm: 16 (over z, y, x), run: 2 (over core).
Axes of the slice: x: 2, y: 2, z: 4, core: 2. Of those that a mesh axis runs over, the one named last changes fastest.
Arguments:
- signal: bfloat16 [2, 16384, 256], P('run', 'tm'), may hold values from -6 to 6
- conv_weight: bfloat16 [768, 512], replicated, may hold values from -0.21875 to 0.21875
- conv_bias: float32 [512], replicated, may hold values from -3 to 3
- out_weight: bfloat16 [256, 256], replicated, may hold values from -0.375 to 0.375
- out_bias: float32 [256], replicated, may hold values from -3 to 3
- cotangent: bfloat16 [2, 16384, 256], P('run', 'tm'), may hold values from -8 to 8
Outputs:
- output: bfloat16 [2, 16384, 256], P('run', 'tm')
- grad_signal: bfloat16 [2, 16384, 256], P('run', 'tm')
- grad_conv_weight: float32 [768, 512], replicated
- grad_conv_bias: float32 [512], replicated
- grad_out_weight: float32 [256, 256], replicated
- grad_out_bias: float32 [256], replicated
All inputs are finite; a program needn't handle non-finite values.
Results may differ from a plain program's by a relative error of at most 0.0034.
Values may be sent and summed in bfloat16 or wider, within the bound.
No kernel may reach another device: no remote copies, remote signals or barrier semaphores. Data moves between devices by JAX's collectives and lax.ppermute only.
A program may use at most 64 MiB of HBM per device.

v0:
```python
import jax
import jax.numpy as jnp
from jax import lax
from jax.sharding import PartitionSpec as P

DILATION_STEPS = 256
KERNEL_TAPS = 3


def passed_along(array, axis, by):
    size = lax.axis_size(axis)
    pairs = [(i, i + by) for i in range(size) if 0 <= i + by < size]
    return lax.ppermute(array, axis, pairs)


def local(signal, conv_weight, conv_bias, out_weight, out_bias, cotangent):
    device_rows = signal.shape[1]
    channels = signal.shape[2]
    receptive_span = (KERNEL_TAPS - 1) * DILATION_STEPS
    history = passed_along(signal[:, device_rows - receptive_span :, :], "tm", 1)
    padded_input = jnp.concatenate([history, signal], 1)
    tap_stack = jnp.concatenate(
        [
            padded_input[
                :,
                receptive_span
                - kernel_tap_index * DILATION_STEPS : receptive_span
                - kernel_tap_index * DILATION_STEPS
                + device_rows,
            ]
            for kernel_tap_index in range(KERNEL_TAPS)
        ],
        2,
    )
    preact = (
        jnp.einsum("bsk,kn->bsn", tap_stack, conv_weight, preferred_element_type=jnp.float32)
        + conv_bias
    )
    filtered = jnp.tanh(preact[..., :channels])
    gated = jax.nn.sigmoid(preact[..., channels:])
    mixed = (filtered * gated).astype(jnp.bfloat16)
    hidden = (
        jnp.einsum("bsc,cd->bsd", mixed, out_weight, preferred_element_type=jnp.float32) + out_bias
    )
    output = (signal.astype(jnp.float32) + hidden).astype(jnp.bfloat16)
    dmixed = jnp.einsum("bsd,cd->bsc", cotangent, out_weight, preferred_element_type=jnp.float32)
    dpre = jnp.concatenate(
        [dmixed * gated * (1.0 - filtered * filtered), dmixed * filtered * gated * (1.0 - gated)], 2
    ).astype(jnp.bfloat16)
    dstacked = jnp.einsum("bsn,kn->bsk", dpre, conv_weight, preferred_element_type=jnp.float32)
    local_grad = jnp.zeros((signal.shape[0], receptive_span + device_rows, channels), jnp.float32)
    for kernel_tap_index in range(KERNEL_TAPS):
        shifted_slice = dstacked[
            ..., kernel_tap_index * channels : (kernel_tap_index + 1) * channels
        ]
        local_grad = local_grad + jnp.pad(
            shifted_slice,
            (
                (0, 0),
                (
                    receptive_span - kernel_tap_index * DILATION_STEPS,
                    kernel_tap_index * DILATION_STEPS,
                ),
                (0, 0),
            ),
        )
    incoming = passed_along(local_grad[:, :receptive_span].astype(jnp.bfloat16), "tm", -1).astype(
        jnp.float32
    )
    grad_signal = (
        cotangent.astype(jnp.float32)
        + local_grad[:, receptive_span:]
        + jnp.pad(incoming, ((0, 0), (device_rows - receptive_span, 0), (0, 0)))
    )
    grad_signal = grad_signal.astype(jnp.bfloat16)
    grad_conv = jnp.einsum("bsk,bsn->kn", tap_stack, dpre, preferred_element_type=jnp.float32)
    grad_cbias = jnp.sum(dpre.astype(jnp.float32), (0, 1))
    grad_proj = jnp.einsum("bsc,bsd->cd", mixed, cotangent, preferred_element_type=jnp.float32)
    grad_pbias = jnp.sum(cotangent.astype(jnp.float32), (0, 1))
    scale = float(signal.shape[0] * lax.axis_size("run") * device_rows * lax.axis_size("tm")) ** (
        -0.5
    )
    summed = lax.psum((grad_conv, grad_cbias, grad_proj, grad_pbias), ("tm", "run"))
    return (
        output,
        grad_signal,
        summed[0] * scale,
        summed[1] * scale,
        summed[2] * scale,
        summed[3] * scale,
    )


def solution(mesh):
    placed = (P("run", "tm", None), P(), P(), P(), P(), P("run", "tm", None))
    return jax.shard_map(
        local,
        mesh=mesh,
        in_specs=placed,
        out_specs=(P("run", "tm", None), P("run", "tm", None), P(), P(), P(), P()),
        check_vma=False,
    )
```

profile of v0, /device:TPU:0, one launch (start us, length us, event | category | flops | bytes accessed | tf_op | source)
XLA Modules:
  0.0 180.7 jit_solution(2866281760604464369)
XLA Ops:
  7.2 0.0 copy-start
  7.2 0.0 copy-start.2
  7.2 0.0 copy-start.6
  7.2 0.0 all-reduce.8.cloned.1.call-start
  7.2 1.1 slice.31
  8.3 4.9 %collective-permute-start = (bf16[1,512,256]{2,1,0:T(8,128)(2,1)S(1)}, bf16[1,512,256]{2,1,0:T(8,128)(2,1)S(1)}, u32[]{:S(2)}, u32[]{:S(2)}) collective-permute-start(bf16[1,512,256]{2,1,0:T(8,128)(2,1)S(1)} %slice.31), channel_id=1, source_target_pairs={{0,2},{2,4},{4,6},{6,8},{8,10},{10,12},{12,14},{14,16},{16,18},{18... | collective-permute-start | bytes 786440 | tf_op jit(solution)/shard_map/ppermute | solution.py:13
  13.2 5.5 %collective-permute-done = bf16[1,512,256]{2,1,0:T(8,128)(2,1)S(1)} collective-permute-done((bf16[1,512,256]{2,1,0:T(8,128)(2,1)S(1)}, bf16[1,512,256]{2,1,0:T(8,128)(2,1)S(1)}, u32[]{:S(2)}, u32[]{:S(2)}) %collective-permute-start) | collective-permute-done | bytes 262176 | tf_op jit(solution)/shard_map/ppermute | solution.py:13
  18.7 1.1 constant_dynamic-update-slice_fusion
  19.8 0.1 fusion.17
  19.9 0.0 copy-done
  19.9 0.0 copy-done.2
  19.9 0.0 copy-done.6
  19.9 0.0 copy-start.1
  19.9 0.0 copy-start.5
  19.9 1.0 add_bitcast_fusion
  21.0 0.0 copy-done.1
  21.0 0.0 copy-done.5
  21.0 0.8 multiply_convert_fusion.1
  21.8 0.0 copy-start.3
  21.8 0.2 convert_reduce_fusion
  22.0 2.2 %fusion.8 = f32[768,512]{1,0:T(8,128)} fusion(bf16[1024,256]{0,1:T(8,128)(2,1)S(1)} %bitcast.37, bf16[1024,256]{0,1:T(8,128)(2,1)S(1)} %bitcast.35, bf16[1,1024,256]{2,1,0:T(8,128)(2,1)S(1)} %get-tuple-element.17, bf16[1,1024,256]{2,1,0:T(8,128)(2,1)S(1)} %get-tuple-element.16, bf16[1,1024,256]{2,1,0:T(8,128)(2,1)S(1)} %copy-done.2), kind=kOutput, calls=%fused_computation.24 | convolution fusion | flops 812122112 | bytes 4194304 | tf_op jit(solution)/shard_map/bsk,bsn->kn/dot_general | solution.py:76
  24.2 2.7 %convolution_bitcast_fusion = f32[1,1024,768]{2,1,0:T(8,128)} fusion(bf16[768,512]{1,0:T(8,128)(2,1)S(1)} %copy-done, bf16[1024,256]{0,1:T(8,128)(2,1)S(1)} %bitcast.38, bf16[1024,256]{0,1:T(8,128)(2,1)S(1)} %bitcast.36), kind=kOutput, calls=%fused_computation.2 | convolution fusion | flops 807403520 | bytes 4980736 | tf_op jit(solution)/shard_map/bsn,kn->bsk/dot_general | solution.py:50
  26.9 0.0 copy-done.3
  26.9 1.0 fusion.10
  27.9 2.1 %fusion.16 = (f32[1,1024,256]{2,1,0:T(8,128)S(1)}, f32[1,1024,256]{2,1,0:T(8,128)S(1)}, f32[1,1024,256]{2,1,0:T(8,128)S(1)}) fusion(f32[1,1024,768]{2,1,0:T(8,128)} %convolution_bitcast_fusion), kind=kLoop, calls=%fused_computation.38 | loop fusion | bytes 6291456 | tf_op jit(solution)/shard_map/slice | solution.py:53
  30.0 0.2 pad_add_fusion
  30.2 0.0 copy-start.7
  30.2 0.7 slice.74
  30.9 1.3 collective-permute-start.1
  32.2 0.0 all-reduce.8.cloned.1.call-update
  32.2 0.0 copy-done.7
  32.2 2.2 %fusion.2 = bf16[1,1024,256]{2,1,0:T(8,128)(2,1)} fusion(bf16[1024,256]{0,1:T(8,128)(2,1)} %copy-done.3, bf16[256,256]{1,0:T(8,128)(2,1)S(1)} %copy-done.5, bf16[1,1024,256]{2,1,0:T(8,128)(2,1)S(1)} %copy-done.2, f32[256]{0:T(256)S(1)} %copy-done.7), kind=kOutput, calls=%fused_computation.11 | convolution fusion | flops 135266304 | bytes 1704960 | tf_op jit(solution)/shard_map/bsc,cd->bsd/dot_general | solution.py:43
  34.4 6.6 %collective-permute-done.1 = bf16[1,512,256]{2,1,0:T(8,128)(2,1)} collective-permute-done((bf16[1,512,256]{2,1,0:T(8,128)(2,1)}, bf16[1,512,256]{2,1,0:T(8,128)(2,1)}, u32[]{:S(2)}, u32[]{:S(2)}) %collective-permute-start.1) | collective-permute-done | bytes 262176 | tf_op jit(solution)/shard_map/ppermute | solution.py:13
  41.0 2.0 %convert_reduce_fusion.1 = (f32[256]{0:T(256)S(1)}, bf16[1,1024,256]{2,1,0:T(8,128)(2,1)}) fusion(bf16[1,1024,256]{2,1,0:T(8,128)(2,1)S(1)} %copy-done.1, bf16[1,512,256]{2,1,0:T(8,128)(2,1)} %collective-permute-done.1, f32[1,1536,256]{2,1,0:T(8,128)S(1)} %pad_add_fusion), kind=kLoop, calls=%fused_computation.8 | loop fusion | flops 1572608 | bytes 2360320 | tf_op jit(solution)/shard_map/reduce_sum | solution.py:79
  43.0 42.5 %all-reduce.4 = (f32[512]{0:T(512)S(1)}, f32[256]{0:T(256)S(1)}) all-reduce(f32[512]{0:T(512)S(1)} %convert_reduce_fusion, f32[256]{0:T(256)S(1)} %get-tuple-element.18), channel_id=1, replica_groups=mesh['tm'=16,'run'=2] {'tm','run'}, use_global_device_ids=true, to_apply=%region_2.3 | all-reduce | flops 768 | bytes 6144 | tf_op jit(solution)/shard_map/psum | solution.py:83
  85.6 0.6 broadcast_multiply_fusion.3
  86.1 0.6 broadcast_multiply_fusion.2
  86.7 83.7 %all-reduce.8.cloned.1.call-done = (f32[768,512]{1,0:T(8,128)}, f32[256,256]{1,0:T(8,128)}) async-done(((f32[768,512]{1,0:T(8,128)}, f32[256,256]{1,0:T(8,128)}), (f32[768,512]{1,0:T(8,128)}, f32[256,256]{1,0:T(8,128)})) %all-reduce.8.cloned.1.call-update) | async-done | bytes 1835024 | tf_op jit(solution)/shard_map/psum | solution.py:83
  170.4 0.0 copy-start.4
  170.4 2.8 %broadcast_multiply_fusion = f32[768,512]{1,0:T(8,128)} fusion(f32[768,512]{1,0:T(8,128)} %get-tuple-element.8), kind=kLoop, calls=%fused_computation.23 | loop fusion | flops 393216 | bytes 3145728 | tf_op jit(solution)/shard_map/mul | solution.py:87
  173.1 0.0 copy-done.4
  173.1 0.7 broadcast_multiply_fusion.1
  (1 shorter events, 0.0 us)
Async XLA Ops:
  7.2 12.7 %copy-start = (bf16[768,512]{1,0:T(8,128)(2,1)S(1)}, bf16[768,512]{1,0:T(8,128)(2,1)}, u32[]{:S(2)}) copy-start(bf16[768,512]{1,0:T(8,128)(2,1)} %param.7) | copy-start | bytes 2359300
  7.2 12.7 %copy-start.2 = (bf16[1,1024,256]{2,1,0:T(8,128)(2,1)S(1)}, bf16[1,1024,256]{2,1,0:T(8,128)(2,1)}, u32[]{:S(2)}) copy-start(bf16[1,1024,256]{2,1,0:T(8,128)(2,1)} %param.6) | copy-start | bytes 1572868
  7.2 12.7 %copy-start.6 = (f32[512]{0:T(512)S(1)}, f32[512]{0:T(512)}, u32[]{:S(2)}) copy-start(f32[512]{0:T(512)} %param.8) | copy-start | bytes 6148
  7.2 163.2 %all-reduce.8.cloned.1.call-start = ((), (), s32[]{:S(2)}) async-start(), calls=%async_computation | async-start | bytes 3670016 | tf_op jit(solution)/shard_map/psum | solution.py:83
  8.3 10.4 %collective-permute-start = (bf16[1,512,256]{2,1,0:T(8,128)(2,1)S(1)}, bf16[1,512,256]{2,1,0:T(8,128)(2,1)S(1)}, u32[]{:S(2)}, u32[]{:S(2)}) collective-permute-start(bf16[1,512,256]{2,1,0:T(8,128)(2,1)S(1)} %slice.31), channel_id=1, source_target_pairs={{0,2},{2,4},{4,6},{6,8},{8,10},{10,12},{12,14},{14,16},{16,18},{18... | collective-permute-start | bytes 786440 | tf_op jit(solution)/shard_map/ppermute | solution.py:13
  19.9 1.1 copy-start.1
  19.9 1.1 copy-start.5
  21.8 5.1 %copy-start.3 = (bf16[1024,256]{0,1:T(8,128)(2,1)}, bf16[1024,256]{0,1:T(8,128)(2,1)S(1)}, u32[]{:S(2)}) copy-start(bf16[1024,256]{0,1:T(8,128)(2,1)S(1)} %get-tuple-element.15) | copy-start | bytes 1572868
  30.2 2.1 %copy-start.7 = (f32[256]{0:T(256)S(1)}, f32[256]{0:T(256)}, u32[]{:S(2)}) copy-start(f32[256]{0:T(256)} %param.10) | copy-start | bytes 3076
  30.9 10.1 %collective-permute-start.1 = (bf16[1,512,256]{2,1,0:T(8,128)(2,1)}, bf16[1,512,256]{2,1,0:T(8,128)(2,1)}, u32[]{:S(2)}, u32[]{:S(2)}) collective-permute-start(bf16[1,512,256]{2,1,0:T(8,128)(2,1)} %slice.74), channel_id=1, source_target_pairs={{2,0},{4,2},{6,4},{8,6},{10,8},{12,10},{14,12},{16,14},{18,16},{20... | collective-permute-start | bytes 786440 | tf_op jit(solution)/shard_map/ppermute | solution.py:13
  170.4 2.8 %copy-start.4 = (f32[256,256]{1,0:T(8,128)S(1)}, f32[256,256]{1,0:T(8,128)}, u32[]{:S(2)}) copy-start(f32[256,256]{1,0:T(8,128)} %get-tuple-element.9) | copy-start | bytes 786436
Sparse Core Ops, SparseCore 0:
  32.4 137.9 all-reduce.7
where the time goes:
time: 181 us
  waiting for transfers between devices  95.8 us (53%)
  blocking collectives  42.5 us (23%)
  between operations  14.2 us (8%)
  matrix products  9.88 us (5%)
  other arithmetic  7.02 us (4%)
  starting transfers between devices  6.18 us (3%)
  local copies, waits for them, and re-layouts  5.08 us (3%)
    psum x1, waiting for transfers between devices, local(): lax.psum((grad_conv, grad_cbias, grad_proj, grad_pbias), ('tm', 'run'))  83.7 us
    psum x1, blocking collectives, local(): lax.psum((grad_conv, grad_cbias, grad_proj, grad_pbias), ('tm', 'run'))  42.5 us
    ppermute x2, waiting for transfers between devices, passed_along(): return lax.ppermute(array, axis, pairs)  12.1 us
    ppermute x2, starting transfers between devices, passed_along(): return lax.ppermute(array, axis, pairs)  6.14 us
  transfers between devices with their start and end apart: 3, of which 3 were waited for; matrix products, arithmetic and copies ran while one was open for 3% of the time, Pallas kernels for 0%

commit v1 on v0

v1 whole, which is shorter than its diff:
```python
import functools

import jax
import jax.numpy as jnp
from jax import lax
from jax.experimental import pallas as pl
from jax.experimental.pallas import tpu as pltpu
from jax.sharding import PartitionSpec as P

STEP = 256
TAPS = 3
SPAN = (TAPS - 1) * STEP
BOTH = ("tm", "run")
LANES = 128
SUBLANES = 8
BIAS_ROWS = 2 * SUBLANES
F32 = jnp.float32
BF16 = jnp.bfloat16
VMEM = pl.BlockSpec(memory_space=pltpu.VMEM)
SMEM = pl.BlockSpec(memory_space=pltpu.SMEM)
LIMIT = 24 * 1024 * 1024


def call(kernel, out_shape, args, scalars=0, flops=0, scratch=()):
    moved = sum(a.size * a.dtype.itemsize for a in args)
    return pl.pallas_call(
        kernel,
        out_shape=out_shape,
        in_specs=[SMEM] * scalars + [VMEM] * (len(args) - scalars),
        out_specs=[VMEM] * len(out_shape),
        scratch_shapes=list(scratch),
        cost_estimate=pl.CostEstimate(flops=flops, bytes_accessed=moved, transcendentals=0),
        compiler_params=pltpu.CompilerParams(vmem_limit_bytes=LIMIT),
    )(*args)


def shape(dtype, *dims):
    return jax.ShapeDtypeStruct(dims, dtype)


def dot(a, b):
    return jnp.dot(a, b, preferred_element_type=F32)


def dot_rows(a, b):
    return lax.dot_general(a, b, (((0,), (0,)), ((), ())), preferred_element_type=F32)


def dot_columns(a, b):
    return lax.dot_general(a, b, (((1,), (1,)), ((), ())), preferred_element_type=F32)


def gates(preact, dmixed):
    channels = dmixed.shape[1]
    filtered = jnp.tanh(preact[:, :channels])
    gated = jax.nn.sigmoid(preact[:, channels:])
    mixed = filtered * gated
    dfiltered = dmixed * gated * (1.0 - filtered * filtered)
    dgated = dmixed * mixed * (1.0 - gated)
    return mixed.astype(BF16), dfiltered.astype(BF16), dgated.astype(BF16)


def late_kernel(
    signal, weight, bias, out_weight, cot,
    preact_out, dmixed_out, mixed_out, dpre_out, grad_conv, grad_proj, grad_bias,
):
    rows, channels = signal.shape
    tap = lambda k: weight[k * channels : (k + 1) * channels, :]
    preact_out[...] = dot(signal[:SPAN, :], tap(0)) + bias[...]
    for k in range(1, TAPS - 1):
        preact_out[k * STEP :, :] += dot(signal[: SPAN - k * STEP, :], tap(k))
    dmixed_out[...] = dot_columns(cot[:SPAN, :], out_weight[...])
    for begin in range(SPAN, rows, STEP):
        here = slice(begin, begin + STEP)
        at = slice(begin - SPAN, begin - SPAN + STEP)
        preact = bias[...]
        for k in range(TAPS):
            preact = preact + dot(signal[begin - k * STEP : begin - k * STEP + STEP, :], tap(k))
        mixed, dfiltered, dgated = gates(preact, dot_columns(cot[here, :], out_weight[...]))
        mixed_out[at, :] = mixed
        dpre_out[at, :channels] = dfiltered
        dpre_out[at, channels:] = dgated
    dpre = dpre_out[...]
    for k in range(TAPS):
        grad_conv[k * channels : (k + 1) * channels, :] = dot_rows(
            signal[SPAN - k * STEP : rows - k * STEP, :], dpre
        )
    grad_proj[...] = dot_rows(mixed_out[...], cot[SPAN:, :])
    ones = jnp.ones((BIAS_ROWS, rows), BF16)
    grad_bias[:, : 2 * channels] = dot(ones[:, : rows - SPAN], dpre)[:SUBLANES]
    grad_bias[:, 2 * channels :] = dot(ones, cot[...])[:SUBLANES]


def early_kernel(
    fine, first, history, signal, weight, cot, preact_in, dmixed_in, conv_in, proj_in, bias_in,
    mixed_out, dpre_out, main_out, bias_out, message, past, grad_conv, grad_proj,
):
    rows, channels = signal.shape
    tap = lambda k: weight[k * channels : (k + 1) * channels, :]
    past[...] = jnp.where(first[0] == 1, jnp.zeros_like(history), history[...])
    for begin in range(0, SPAN, STEP):
        here = slice(begin, begin + STEP)
        preact = preact_in[here, :]
        for k in range(begin // STEP + 1, TAPS):
            source = SPAN + begin - k * STEP
            preact = preact + dot(past[source : source + STEP, :], tap(k))
        mixed, dfiltered, dgated = gates(preact, dmixed_in[here, :])
        mixed_out[here, :] = mixed
        dpre_out[here, :channels] = dfiltered
        dpre_out[here, channels:] = dgated
    dpre = dpre_out[...]
    for k in range(TAPS):
        at = slice(k * channels, (k + 1) * channels)
        total = conv_in[at, :] + dot_rows(past[SPAN - k * STEP :, :], dpre[: k * STEP, :]) if k else conv_in[at, :]
        if k < TAPS - 1:
            total = total + dot_rows(signal[: SPAN - k * STEP, :], dpre[k * STEP :, :])
        grad_conv[at, :] = total
    grad_proj[...] = proj_in[...] + dot_rows(mixed_out[...], cot[:SPAN, :])
    ones = jnp.ones((BIAS_ROWS, SPAN), BF16)
    columns = dot(ones, dpre)[:SUBLANES]
    bias = bias_in[...]
    bias = jnp.concatenate([bias[:, : 2 * channels] + columns, bias[:, 2 * channels :]], 1)
    lines = [bias[:1, c : c + LANES] for c in range(0, bias.shape[1], LANES)]
    lines += [jnp.zeros((1, LANES), F32)] * (SUBLANES - len(lines))
    bias = jnp.concatenate(lines, 0)
    bias_out[...] = bias
    pieces = main_out.shape[0] // fine
    for piece in range(pieces):
        at = piece * fine
        for grad in (grad_conv, grad_proj):
            height = piece_height(grad.shape[0], pieces)
            begin = piece * height
            count = min(height, grad.shape[0] - begin)
            for column in range(0, grad.shape[1], LANES):
                if count > 0:
                    block = grad[begin : begin + count, column : column + LANES]
                    main_out[at : at + count, :] = block
                    message[at : at + count, :] = block.astype(BF16)
                    padded = at + count
                else:
                    padded = at
                if count < height:
                    blank = jnp.zeros((at + height - padded, LANES), F32)
                    main_out[padded : at + height, :] = blank
                    message[padded : at + height, :] = blank.astype(BF16)
                at += height
    message[pieces * fine :, :] = narrowed(bias)


def back_kernel(dpre, weight, out):
    channels = out.shape[1]
    tap = lambda k: weight[k * channels : (k + 1) * channels, :]
    for begin in range(0, SPAN, STEP):
        total = dot_columns(dpre[begin : begin + STEP, :], tap(TAPS - 1))
        for k in range(1, TAPS - 1):
            source = begin - SPAN + k * STEP
            if source >= 0:
                total = total + dot_columns(dpre[source : source + STEP, :], tap(k))
        out[begin : begin + STEP, :] = total.astype(BF16)


def own_kernel(signal, weight, out_weight, out_bias, cot, mixed_early, mixed_late, dpre_early, dpre_late, output, partial):
    rows, channels = signal.shape
    tap = lambda k: weight[k * channels : (k + 1) * channels, :]

    def part(early, late, begin):
        ref, at = (early, begin) if begin < SPAN else (late, begin - SPAN)
        return ref[at : at + STEP, :]

    for begin in range(0, rows, STEP):
        here = slice(begin, begin + STEP)
        hidden = dot(part(mixed_early, mixed_late, begin), out_weight[...]) + out_bias[...]
        output[here, :] = (signal[here, :].astype(F32) + hidden).astype(BF16)
        total = cot[here, :].astype(F32)
        for k in range(TAPS):
            if begin + k * STEP < rows:
                total = total + dot_columns(part(dpre_early, dpre_late, begin + k * STEP), tap(k))
        partial[here, :] = total


def join_kernel(last, partial, incoming, out):
    rows = partial.shape[0]
    out[: rows - SPAN, :] = partial[: rows - SPAN, :].astype(BF16)
    more = jnp.where(last[0] == 1, jnp.zeros(incoming.shape, F32), incoming[...].astype(F32))
    out[rows - SPAN :, :] = (partial[rows - SPAN :, :] + more).astype(BF16)


def piece_height(rows, pieces):
    return -(-rows // (pieces * 16)) * 16


def widened(block):
    wide = block.astype(F32)
    return wide[:SUBLANES] + wide[SUBLANES:]


def narrowed(total):
    high = total.astype(BF16).astype(F32)
    return jnp.concatenate([high, total - high], 0).astype(BF16)


def split_kernel(radix, more, *refs):
    digit, main, bias, received = refs[0], refs[1], refs[2], refs[3 : 3 + more]
    sends, keep = refs[3 + more : -1], refs[-1]
    rows, end = sends[0].shape[0] - BIAS_ROWS, main.shape[0]
    total = bias[...]
    for ref in received:
        total = total + widened(ref[end:, :])
    for k in range(radix):
        start = pl.multiple_of((digit[0] ^ k) * rows, 16)
        block = main[pl.ds(start, rows), :]
        for ref in received:
            block = block + ref[pl.ds(start, rows), :].astype(F32)
        if k:
            sends[k - 1][:rows, :] = block.astype(BF16)
            sends[k - 1][rows:, :] = narrowed(total)
        else:
            keep[:rows, :] = block
            keep[rows:, :] = total


def finish_kernel(scale, *refs):
    keep, received, out = refs[0], refs[1:-1], refs[-1]
    rows = out.shape[0] - BIAS_ROWS
    block, total = keep[:rows, :], keep[rows:, :]
    for ref in received:
        block = block + ref[:rows, :].astype(F32)
        total = total + widened(ref[rows:, :])
    out[:rows, :] = (block * scale).astype(BF16)
    out[rows:, :] = narrowed(total * scale)


def place_kernel(radix, taker, scalars, given, *refs):
    parts, out = refs[:radix], refs[radix]
    rows = parts[0].shape[0] - BIAS_ROWS
    own = jnp.where(scalars[1] == taker, given[...], parts[0][...])
    for k in range(radix):
        block = parts[k][...] if k else own
        index = scalars[0] ^ k
        out[pl.ds(pl.multiple_of(index * rows, 16), rows), :] = block[:rows]

        @pl.when(index == 0)
        def _():
            out[radix * rows :, :] = block[rows:]


def spread_kernel(radix, taker, pieces, scalars, given, *refs):
    parts, forwarded = refs[:radix], refs[radix : 2 * radix - 1]
    conv, proj, biases, whole = refs[2 * radix - 1 :]
    rows = parts[0].shape[0] - BIAS_ROWS
    for k in range(radix):
        other = forwarded[k - 1] if k else given
        block = jnp.where((scalars[1] == taker) == (k > 0), parts[k][...], other[...])
        index = scalars[0] ^ k
        whole[pl.ds(pl.multiple_of(index * rows, 16), rows), :] = block[:rows]

        @pl.when(index == 0)
        def _():
            biases[...] = widened(block[rows:])

    at = 0
    for piece in range(pieces):
        for out in (conv, proj):
            height = piece_height(out.shape[0], pieces)
            begin = piece * height
            count = min(height, out.shape[0] - begin)
            for column in range(0, out.shape[1], LANES):
                if count > 0:
                    out[begin : begin + count, column : column + LANES] = whole[
                        at : at + count, :
                    ].astype(F32)
                at += height


def digits_of(count):
    digits = []
    while count > 1:
        digits.append(4 if count % 4 == 0 else 2)
        count //= digits[-1]
    return digits


def place_of():
    runs = lax.axis_size("run")
    chips = lax.axis_size("tm") * runs // 2
    flat = lax.axis_index("tm") * runs + lax.axis_index("run")
    return chips, flat // 2, flat % 2


def swapped(array):
    chips = place_of()[0]
    return lax.ppermute(array, BOTH, [(i, i ^ 1) for i in range(2 * chips)])


def crossed(array, source, step):
    chips = place_of()[0]
    pairs = [(2 * c + source, 2 * (c ^ step) + 1 - source) for c in range(chips)]
    pairs += [(2 * c + 1 - source, 2 * c + source) for c in range(chips)]
    return lax.ppermute(array, BOTH, pairs)


def summed_everywhere(main, bias, message, scale, shapes):
    chips, chip, core = place_of()
    digits = digits_of(chips)
    received = [swapped(message)]
    weight, source, levels = 1, 0, []
    for level, radix in enumerate(digits):
        digit = (chip // weight) % radix
        rows = main.shape[0] // radix
        *sends, keep = call(
            functools.partial(split_kernel, radix, len(received)),
            [shape(BF16, rows + BIAS_ROWS, LANES)] * (radix - 1) + [shape(F32, rows + SUBLANES, LANES)],
            (digit.reshape(1), main, bias, *received),
            1,
        )
        if level:
            keep = swapped(keep)
        received = [crossed(sends[k - 1], source, k * weight) for k in range(1, radix)]
        main, bias = keep[:rows], keep[rows:]
        levels.append((radix, weight, digit, source))
        weight *= radix
        source = 1 - source
    (part,) = call(
        functools.partial(finish_kernel, scale),
        [shape(BF16, rows + BIAS_ROWS, LANES)],
        (keep, *received),
    )
    for level in reversed(range(len(levels))):
        radix, weight, digit, _ = levels[level]
        given = swapped(part)
        parts = [part] + [crossed(part, source, k * weight) for k in range(1, radix)]
        scalars = jnp.stack([digit, core])
        if level:
            rows = part.shape[0] - BIAS_ROWS
            (part,) = call(
                functools.partial(place_kernel, radix, 1 - source),
                [shape(BF16, radix * rows + BIAS_ROWS, LANES)],
                (scalars, given, *parts),
                1,
            )
            source = 1 - source
    forwarded = [swapped(p) for p in parts[1:]]
    return call(
        functools.partial(spread_kernel, radix, 1 - source, chips),
        list(shapes) + [shape(F32, SUBLANES, LANES)],
        (scalars, given, *parts, *forwarded),
        1,
        scratch=[pltpu.VMEM((main_rows(shapes, chips), LANES), BF16)],
    )


def main_rows(shapes, pieces):
    return pieces * sum(piece_height(s.shape[0], pieces) * s.shape[1] // LANES for s in shapes)


def local(signal, conv_weight, conv_bias, out_weight, out_bias, cotangent):
    rows, channels = signal.shape[1:]
    wide = 2 * channels
    size = lax.axis_size("tm")
    index = lax.axis_index("tm")
    x, cot = signal[0], cotangent[0]
    history = lax.ppermute(x[rows - SPAN :], "tm", [(i, (i + 1) % size) for i in range(size)])
    late = rows - SPAN
    preact, dmixed, mixed_late, dpre_late, conv, proj, bias = call(
        late_kernel,
        [
            shape(F32, SPAN, wide), shape(F32, SPAN, channels), shape(BF16, late, channels),
            shape(BF16, late, wide), shape(F32, TAPS * channels, wide), shape(F32, channels, channels),
            shape(F32, SUBLANES, wide + channels),
        ],
        (x, conv_weight, conv_bias.reshape(1, -1), out_weight, cot),
        flops=3 * rows * channels * channels * 8,
    )
    chips = place_of()[0]
    shapes = [shape(F32, TAPS * channels, wide), shape(F32, channels, channels)]
    total = main_rows(shapes, chips)
    mixed_early, dpre_early, main, bias, message = call(
        functools.partial(early_kernel, total // chips),
        [
            shape(BF16, SPAN, channels), shape(BF16, SPAN, wide), shape(F32, total, LANES),
            shape(F32, SUBLANES, LANES), shape(BF16, total + BIAS_ROWS, LANES),
        ],
        (
            (index == 0).astype(jnp.int32).reshape(1), history, x, conv_weight, cot,
            preact, dmixed, conv, proj, bias,
        ),
        1,
        flops=2 * rows * channels * channels * 8,
        scratch=[pltpu.VMEM((SPAN, channels), BF16)] + [pltpu.VMEM(s.shape, F32) for s in shapes],
    )
    (back,) = call(back_kernel, [shape(BF16, SPAN, channels)], (dpre_early, conv_weight))
    output, partial = call(
        own_kernel,
        [shape(BF16, rows, channels), shape(F32, rows, channels)],
        (
            x, conv_weight, out_weight, out_bias.reshape(1, -1), cot,
            mixed_early, mixed_late, dpre_early, dpre_late,
        ),
        flops=2 * rows * channels * channels * 8,
    )
    incoming = lax.ppermute(back, "tm", [((i + 1) % size, i) for i in range(size)])
    (grad_signal,) = call(
        join_kernel,
        [shape(BF16, rows, channels)],
        ((index == size - 1).astype(jnp.int32).reshape(1), partial, incoming),
        1,
    )
    scale = float(signal.shape[0] * lax.axis_size("run") * rows * size) ** -0.5
    grad_conv, grad_proj, biases = summed_everywhere(main, bias, message, scale, shapes)
    biases = biases.reshape(-1)
    return (
        output[None],
        grad_signal[None],
        grad_conv,
        biases[:wide],
        grad_proj,
        biases[wide : wide + channels],
    )


def solution(mesh):
    placed = (P("run", "tm", None), P(), P(), P(), P(), P("run", "tm", None))
    return jax.shard_map(
        local,
        mesh=mesh,
        in_specs=placed,
        out_specs=(P("run", "tm", None), P("run", "tm", None), P(), P(), P(), P()),
        check_vma=False,
    )
```

time: 181 us -> 67.3 us (0.37)
  waiting for transfers between devices: 95.8 us -> 21.7 us
  blocking collectives: 42.5 us -> 0 us
  between operations: 14.2 us -> 0.78 us
  starting transfers between devices: 6.18 us -> 18.5 us
  Pallas kernels: 0 us -> 12 us
  matrix products: 9.88 us -> 0 us
  local copies, waits for them, and re-layouts: 5.08 us -> 13.2 us
  other arithmetic: 7.02 us -> 0.15 us
    psum x1 -> x0, waiting for transfers between devices: 83.7 us -> none  [local(): lax.psum((grad_conv, grad_cbias, grad_proj, grad_pbias), ('tm', 'run'))]
    psum x1 -> x0, blocking collectives: 42.5 us -> none  [local(): lax.psum((grad_conv, grad_cbias, grad_proj, grad_pbias), ('tm', 'run'))]
    ppermute x2 -> x21, starting transfers between devices: 6.14 us -> 18.5 us  [the longest x12 7.47 us: crossed(): return lax.ppermute(array, BOTH, pairs)]
    pallas_call x0 -> x10, Pallas kernels: none -> 12 us  [call(): pl.pallas_call(kernel, out_shape=out_shape, in_specs=[SMEM] * scalars + [...]
    dot_general x6 -> x0, matrix products: 9.88 us -> none  [the longest x1 2.67 us: local(): jnp.einsum('bsn,kn->bsk', dpre, conv_weight, preferred_element_type=jnp.f...]
    ppermute x2 -> x21, waiting for transfers between devices: 12.1 us -> 21.7 us  [the longest x12 15.3 us: crossed(): return lax.ppermute(array, BOTH, pairs)]
    unnamed x17 -> x36, local copies, waits for them, and re-layouts: 0.07 us -> 9.24 us
    mul x4 -> x0, other arithmetic: 4.64 us -> none  [the longest x1 2.77 us: local(): summed[0] * scale]
  transfers between devices with their start and end apart: 3 -> 21, of which waited for: 3 -> 10; matrix products, arithmetic and copies ran while one was open for 3% -> 3% of each run, Pallas kernels for 0% -> 7%
where the time goes in v1:
time: 67.3 us; the launch traced here: 66.4 us
  waiting for transfers between devices  21.7 us (32%)
  starting transfers between devices  18.5 us (27%)
  local copies, waits for them, and re-layouts  13.2 us (20%)
  Pallas kernels  12 us (18%)
  between operations  0.78 us (1%)
    ppermute x12, waiting for transfers between devices, crossed(): return lax.ppermute(array, BOTH, pairs)  15.3 us
    pallas_call x10, Pallas kernels, call(): pl.pallas_call(kernel, out_shape=out_shape, in_specs=[SMEM] * scalars + [...  12 us
    unnamed x36, local copies, waits for them, and re-layouts  9.24 us
    ppermute x12, starting transfers between devices, crossed(): return lax.ppermute(array, BOTH, pairs)  7.47 us
    ppermute x7, starting transfers between devices, swapped(): return lax.ppermute(array, BOTH, [(i, i ^ 1) for i in range(2 * chips)])  6.24 us
    ppermute x1, waiting for transfers between devices, local(): lax.ppermute(x[rows - SPAN:], 'tm', [(i, (i + 1) % size) for i in range(s...  3.72 us
    ppermute x1, starting transfers between devices, local(): lax.ppermute(x[rows - SPAN:], 'tm', [(i, (i + 1) % size) for i in range(s...  2.99 us
    ppermute x7, waiting for transfers between devices, swapped(): return lax.ppermute(array, BOTH, [(i, i ^ 1) for i in range(2 * chips)])  2.7 us
  transfers between devices with their start and end apart: 21, of which 10 were waited for; matrix products, arithmetic and copies ran while one was open for 3% of the time, Pallas kernels for 7%

profile of v1, /device:TPU:0, one launch (start us, length us, event | category | flops | bytes accessed | tf_op | source)
XLA Modules:
  0.0 66.4 jit_solution(6361965695670350998)
XLA Ops:
  0.6 1.0 %slice_bitcast_fusion = bf16[512,256]{1,0:T(8,128)(2,1)S(1)} fusion(bf16[1,1024,256]{2,1,0:T(8,128)(2,1)} %param.6), kind=kLoop, calls=%fused_computation | loop fusion | bytes 524288 | tf_op jit(solution)/shard_map/slice | solution.py:362
  1.6 3.0 %collective-permute-start = (bf16[512,256]{1,0:T(8,128)(2,1)S(1)}, bf16[512,256]{1,0:T(8,128)(2,1)S(1)}, u32[]{:S(2)}, u32[]{:S(2)}) collective-permute-start(bf16[512,256]{1,0:T(8,128)(2,1)S(1)} %slice_bitcast_fusion), channel_id=1, source_target_pairs={{0,2},{2,4},{4,6},{6,8},{8,10},{10,12},{12,14},{14,16},{16,18},{18... | collective-permute-start | bytes 786440 | tf_op jit(solution)/shard_map/ppermute | solution.py:362
  4.6 1.1 %copy-done = bf16[768,512]{1,0:T(8,128)(2,1)S(1)} copy-done((bf16[768,512]{1,0:T(8,128)(2,1)S(1)}, bf16[768,512]{1,0:T(8,128)(2,1)}, u32[]{:S(2)}) %copy-start) | copy-done | bytes 786456
  5.7 1.0 %copy-done.2 = bf16[1,1024,256]{2,1,0:T(8,128)(2,1)S(1)} copy-done((bf16[1,1024,256]{2,1,0:T(8,128)(2,1)S(1)}, bf16[1,1024,256]{2,1,0:T(8,128)(2,1)}, u32[]{:S(2)}) %copy-start.2) | copy-done | bytes 524312
  6.8 1.0 %copy-done.4 = bf16[1,1024,256]{2,1,0:T(8,128)(2,1)S(1)} copy-done((bf16[1,1024,256]{2,1,0:T(8,128)(2,1)S(1)}, bf16[1,1024,256]{2,1,0:T(8,128)(2,1)}, u32[]{:S(2)}) %copy-start.4) | copy-done | bytes 524312
  7.8 0.9 %copy-done.10 = bf16[256,256]{1,0:T(8,128)(2,1)S(1)} copy-done((bf16[256,256]{1,0:T(8,128)(2,1)S(1)}, bf16[256,256]{1,0:T(8,128)(2,1)}, u32[]{:S(2)}) %copy-start.10) | copy-done | bytes 131096
  8.7 0.7 %copy-done.12 = f32[512]{0:T(512)S(1)} copy-done((f32[512]{0:T(512)S(1)}, f32[512]{0:T(512)}, u32[]{:S(2)}) %copy-start.12) | copy-done | bytes 2072
  9.4 1.8 %shard_map.109 = (f32[512,512]{1,0:T(8,128)S(1)}, f32[512,256]{1,0:T(8,128)S(1)}, bf16[512,256]{1,0:T(8,128)(2,1)S(1)}, bf16[512,512]{1,0:T(8,128)(2,1)S(1)}, f3...) custom-call(bf16[1024,256]{1,0:T(8,128)(2,1)S(1)} %bitcast.17, bf16[768,512]{1,0:T(8,128)(2,1)S(1)} %copy-done, ...), custom_call_target="tpu_custom_call" | custom-call | flops 1610612736 | bytes 1968128 | tf_op jit(solution)/shard_map/pallas_call | solution.py:26
  11.2 3.7 %collective-permute-done.history = bf16[512,256]{1,0:T(8,128)(2,1)S(1)} collective-permute-done((bf16[512,256]{1,0:T(8,128)(2,1)S(1)}, bf16[512,256]{1,0:T(8,128)(2,1)S(1)}, u32[]{:S(2)}, u32[]{:S(2)}) %collective-permute-start) | collective-permute-done | bytes 262176 | tf_op jit(solution)/shard_map/ppermute | solution.py:362
  14.9 2.2 %shard_map.110 = (bf16[512,256]{1,0:T(8,128)(2,1)S(1)}, bf16[512,512]{1,0:T(8,128)(2,1)S(1)}, f32[3584,128]{1,0:T(8,128)S(1)}, f32[8,128]{1,0:T(8,128)S(1)}, bf16[3600,128]{1,0:T(8,128)(2,1)}) custom-call(s32[1]{0:T(128)} %bitcast.3.first, bf16[512,256]{1,0:T(8,128)(2,1)S(1)} %collective-permute-done.history, bf16[1024,256]{1,0:T(8,128)(2,1)S(1)} %bitcast.18, ...), custom_call_target="tpu_custom_call" | custom-call | flops 1073741824 | bytes 5529604 | tf_op jit(solution)/shard_map/pallas_call | solution.py:26
  17.1 0.7 %copy-done.8 = bf16[512,256]{1,0:T(8,128)(2,1)} copy-done((bf16[512,256]{1,0:T(8,128)(2,1)}, bf16[512,256]{1,0:T(8,128)(2,1)S(1)}, u32[]{:S(2)}) %copy-start.8) | copy-done | bytes 262168
  17.8 2.7 %collective-permute-done.2.refs_3_ = bf16[3600,128]{1,0:T(8,128)(2,1)S(1)} collective-permute-done((bf16[3600,128]{1,0:T(8,128)(2,1)}, bf16[3600,128]{1,0:T(8,128)(2,1)S(1)}, u32[]{:S(2)}, u32[]{:S(2)}) %collective-permute-start.2) | collective-permute-done | bytes 921632 | tf_op jit(solution)/shard_map/ppermute | solution.py:292
  20.5 0.9 %shard_map.114 = (bf16[912,128]{1,0:T(8,128)(2,1)}, bf16[912,128]{1,0:T(8,128)(2,1)}, bf16[912,128]{1,0:T(8,128)(2,1)S(1)}, f32[904,128]{1,0:T(8,128)S(1)}) custom-call(s32[1]{0:T(128)} %bitcast.9.refs_0_, f32[3584,128]{1,0:T(8,128)S(1)} %get-tuple-element.42.refs_1_, f32[8,128]{1,0:T(8,128)S(1)} %get-tuple-element.43.refs_2_, ...), custom_call_target="tpu_custom_call" | custom-call | bytes 2760708 | tf_op jit(solution)/shard_map/pallas_call | solution.py:26
  21.3 0.8 %copy-done.7 = f32[904,128]{1,0:T(8,128)} copy-done((f32[904,128]{1,0:T(8,128)}, f32[904,128]{1,0:T(8,128)S(1)}, u32[]{:S(2)}) %copy-start.7) | copy-done | bytes 462872
  22.2 1.1 %slice.26.refs_1_ = f32[896,128]{1,0:T(8,128)S(1)} slice(f32[904,128]{1,0:T(8,128)} %copy-done.7), slice={[0:896], [0:128]} | slice | bytes 917504 | tf_op jit(solution)/shard_map/slice | solution.py:319
  23.3 0.7 %slice.27.refs_2_ = f32[8,128]{1,0:T(8,128)S(1)} slice(f32[904,128]{1,0:T(8,128)} %copy-done.7), slice={[896:904], [0:128]} | slice | bytes 8192 | tf_op jit(solution)/shard_map/slice | solution.py:319
  24.0 2.0 %collective-permute-done.3.refs_3_ = bf16[912,128]{1,0:T(8,128)(2,1)S(1)} collective-permute-done((bf16[912,128]{1,0:T(8,128)(2,1)}, bf16[912,128]{1,0:T(8,128)(2,1)S(1)}, u32[]{:S(2)}, u32[]{:S(2)}) %collective-permute-start.3) | collective-permute-done | bytes 233504 | tf_op jit(solution)/shard_map/ppermute | solution.py:299
  26.0 2.4 %collective-permute-done.5.refs_5_ = bf16[912,128]{1,0:T(8,128)(2,1)S(1)} collective-permute-done((bf16[912,128]{1,0:T(8,128)(2,1)S(1)}, bf16[912,128]{1,0:T(8,128)(2,1)S(1)}, u32[]{:S(2)}, u32[]{:S(2)}) %collective-permute-start.5) | collective-permute-done | bytes 233504 | tf_op jit(solution)/shard_map/ppermute | solution.py:299
  28.5 0.7 %shard_map.115 = (bf16[240,128]{1,0:T(8,128)(2,1)}, bf16[240,128]{1,0:T(8,128)(2,1)S(1)}, bf16[240,128]{1,0:T(8,128)(2,1)S(1)}, f32[232,128]{1,0:T(8,128)S(1)}) custom-call(s32[1]{0:T(128)} %bitcast.11.refs_0_, f32[896,128]{1,0:T(8,128)S(1)} %slice.26.refs_1_, f32[8,128]{1,0:T(8,128)S(1)} %slice.27.refs_2_, ...), custom_call_target="tpu_custom_call" | custom-call | bytes 1163268 | tf_op jit(solution)/shard_map/pallas_call | solution.py:26
  29.1 2.4 %collective-permute-start.6 = (f32[232,128]{1,0:T(8,128)S(1)}, f32[232,128]{1,0:T(8,128)S(1)}, u32[]{:S(2)}, u32[]{:S(2)}) collective-permute-start(f32[232,128]{1,0:T(8,128)S(1)} %get-tuple-element.49), channel_id=1, source_target_pairs={{0,1},{1,0},{2,3},{3,2},{4,5},{5,4},{6,7},{7,6},{8,9},{9,8},{10,11... | collective-permute-start | bytes 356360 | tf_op jit(solution)/shard_map/ppermute | solution.py:292
  31.5 0.8 %collective-permute-start.9 = (bf16[240,128]{1,0:T(8,128)(2,1)S(1)}, bf16[240,128]{1,0:T(8,128)(2,1)S(1)}, u32[]{:S(2)}, u32[]{:S(2)}) collective-permute-start(bf16[240,128]{1,0:T(8,128)(2,1)S(1)} %get-tuple-element.52), channel_id=1, source_target_pairs={{1,24},{3,26},{5,28},{7,30},{9,16},{11,18},{13,20},{15,22},{17,8},... | collective-permute-start | bytes 184328 | tf_op jit(solution)/shard_map/ppermute | solution.py:299
  32.3 3.1 %collective-permute-done.7.refs_1_ = bf16[240,128]{1,0:T(8,128)(2,1)S(1)} collective-permute-done((bf16[240,128]{1,0:T(8,128)(2,1)}, bf16[240,128]{1,0:T(8,128)(2,1)S(1)}, u32[]{:S(2)}, u32[]{:S(2)}) %collective-permute-start.7) | collective-permute-done | bytes 61472 | tf_op jit(solution)/shard_map/ppermute | solution.py:299
  35.4 2.0 %collective-permute-done.8.refs_2_ = bf16[240,128]{1,0:T(8,128)(2,1)S(1)} collective-permute-done((bf16[240,128]{1,0:T(8,128)(2,1)S(1)}, bf16[240,128]{1,0:T(8,128)(2,1)S(1)}, u32[]{:S(2)}, u32[]{:S(2)}) %collective-permute-start.8) | collective-permute-done | bytes 61472 | tf_op jit(solution)/shard_map/ppermute | solution.py:299
  37.5 0.1 collective-permute-start.10
  37.5 1.3 %collective-permute-start.11 = (bf16[240,128]{1,0:T(8,128)(2,1)S(1)}, bf16[240,128]{1,0:T(8,128)(2,1)S(1)}, u32[]{:S(2)}, u32[]{:S(2)}) collective-permute-start(bf16[240,128]{1,0:T(8,128)(2,1)S(1)} %shard_map.116.refs_0_), channel_id=1, source_target_pairs={{0,9},{2,11},{4,13},{6,15},{8,1},{10,3},{12,5},{14,7},{16,25},{18,... | collective-permute-start | bytes 184328 | tf_op jit(solution)/shard_map/ppermute | solution.py:299
  38.9 0.3 collective-permute-start.12
  39.1 1.5 %collective-permute-start.13 = (bf16[240,128]{1,0:T(8,128)(2,1)S(1)}, bf16[240,128]{1,0:T(8,128)(2,1)S(1)}, u32[]{:S(2)}, u32[]{:S(2)}) collective-permute-start(bf16[240,128]{1,0:T(8,128)(2,1)S(1)} %shard_map.116.refs_0_), channel_id=1, source_target_pairs={{0,25},{2,27},{4,29},{6,31},{8,17},{10,19},{12,21},{14,23},{16,9},... | collective-permute-start | bytes 184328 | tf_op jit(solution)/shard_map/ppermute | solution.py:299
  40.6 0.1 pad_add_fusion.1.scalars
  40.7 0.6 collective-permute-done.12.refs_2_
  41.3 1.2 %collective-permute-done.13.refs_3_ = bf16[240,128]{1,0:T(8,128)(2,1)S(1)} collective-permute-done((bf16[240,128]{1,0:T(8,128)(2,1)S(1)}, bf16[240,128]{1,0:T(8,128)(2,1)S(1)}, u32[]{:S(2)}, u32[]{:S(2)}) %collective-permute-start.13) | collective-permute-done | bytes 61472 | tf_op jit(solution)/shard_map/ppermute | solution.py:299
  42.5 0.6 shard_map.117.refs_0_
  43.1 2.4 %collective-permute-start.15 = (bf16[912,128]{1,0:T(8,128)(2,1)S(1)}, bf16[912,128]{1,0:T(8,128)(2,1)S(1)}, u32[]{:S(2)}, u32[]{:S(2)}) collective-permute-start(bf16[912,128]{1,0:T(8,128)(2,1)S(1)} %shard_map.117.refs_0_), channel_id=1, source_target_pairs={{1,2},{3,0},{5,6},{7,4},{9,10},{11,8},{13,14},{15,12},{17,18},{19,... | collective-permute-start | bytes 700424 | tf_op jit(solution)/shard_map/ppermute | solution.py:299
  45.5 1.1 %collective-permute-start.17 = (bf16[912,128]{1,0:T(8,128)(2,1)S(1)}, bf16[912,128]{1,0:T(8,128)(2,1)}, u32[]{:S(2)}, u32[]{:S(2)}) collective-permute-start(bf16[912,128]{1,0:T(8,128)(2,1)S(1)} %shard_map.117.refs_0_), channel_id=1, source_target_pairs={{1,6},{3,4},{5,2},{7,0},{9,14},{11,12},{13,10},{15,8},{17,22},{19,... | collective-permute-start | bytes 700424 | tf_op jit(solution)/shard_map/ppermute | solution.py:299
  46.6 0.4 shard_map.112
  47.1 1.8 %collective-permute-start.1 = (bf16[512,256]{1,0:T(8,128)(2,1)S(1)}, bf16[512,256]{1,0:T(8,128)(2,1)S(1)}, u32[]{:S(2)}, u32[]{:S(2)}) collective-permute-start(bf16[512,256]{1,0:T(8,128)(2,1)S(1)} %shard_map.112), channel_id=1, source_target_pairs={{2,0},{4,2},{6,4},{8,6},{10,8},{12,10},{14,12},{16,14},{18,16},{20... | collective-permute-start | bytes 786440 | tf_op jit(solution)/shard_map/ppermute | solution.py:401
  48.9 1.0 %collective-permute-start.14 = (bf16[912,128]{1,0:T(8,128)(2,1)S(1)}, bf16[912,128]{1,0:T(8,128)(2,1)}, u32[]{:S(2)}, u32[]{:S(2)}) collective-permute-start(bf16[912,128]{1,0:T(8,128)(2,1)S(1)} %shard_map.117.refs_0_), channel_id=1, source_target_pairs={{0,1},{1,0},{2,3},{3,2},{4,5},{5,4},{6,7},{7,6},{8,9},{9,8},{10,11... | collective-permute-start | bytes 700424 | tf_op jit(solution)/shard_map/ppermute | solution.py:292
  49.9 3.3 %collective-permute-done.16.refs_2_ = bf16[912,128]{1,0:T(8,128)(2,1)} collective-permute-done((bf16[912,128]{1,0:T(8,128)(2,1)S(1)}, bf16[912,128]{1,0:T(8,128)(2,1)}, u32[]{:S(2)}, u32[]{:S(2)}) %collective-permute-start.16) | collective-permute-done | bytes 233504 | tf_op jit(solution)/shard_map/ppermute | solution.py:299
  53.2 0.6 collective-permute-done.17.refs_3_
  53.9 2.8 %collective-permute-start.20 = (bf16[912,128]{1,0:T(8,128)(2,1)}, bf16[912,128]{1,0:T(8,128)(2,1)}, u32[]{:S(2)}, u32[]{:S(2)}) collective-permute-start(bf16[912,128]{1,0:T(8,128)(2,1)} %collective-permute-done.17.refs_3_), channel_id=1, source_target_pairs={{0,1},{1,0},{2,3},{3,2},{4,5},{5,4},{6,7},{7,6},{8,9},{9,8},{10,11... | collective-permute-start | bytes 700424 | tf_op jit(solution)/shard_map/ppermute | solution.py:292
  56.6 0.1 pad_add_fusion.scalars
  56.7 0.9 %copy-done.9 = bf16[512,256]{1,0:T(8,128)(2,1)S(1)} copy-done((bf16[512,256]{1,0:T(8,128)(2,1)S(1)}, bf16[512,256]{1,0:T(8,128)(2,1)}, u32[]{:S(2)}) %copy-start.9) | copy-done | bytes 262168
  57.7 1.0 %copy-done.15 = bf16[512,512]{1,0:T(8,128)(2,1)S(1)} copy-done((bf16[512,512]{1,0:T(8,128)(2,1)S(1)}, bf16[512,512]{1,0:T(8,128)(2,1)}, u32[]{:S(2)}) %copy-start.15) | copy-done | bytes 524312
  58.7 0.9 %copy-done.17 = bf16[512,256]{1,0:T(8,128)(2,1)S(1)} copy-done((bf16[512,256]{1,0:T(8,128)(2,1)S(1)}, bf16[512,256]{1,0:T(8,128)(2,1)}, u32[]{:S(2)}) %copy-start.17) | copy-done | bytes 262168
  59.7 1.6 %shard_map.111 = (bf16[1024,256]{1,0:T(8,128)(2,1)}, f32[1024,256]{1,0:T(8,128)S(1)}) custom-call(bf16[1024,256]{1,0:T(8,128)(2,1)S(1)} %bitcast.19, bf16[768,512]{1,0:T(8,128)(2,1)S(1)} %copy-done.1, bf16[256,256]{1,0:T(8,128)(2,1)S(1)} %copy-done.11, f32[1,256]{1,0:T(1,128)S(1)} %bitcast.24, bf16[1024,256]{1,0:T(8,128)(2,1)S(1)} %bitcast.22, ...), custom_call_target="tpu_custom_call" | custom-call | flops 1073741824 | bytes 3539968 | tf_op jit(solution)/shard_map/pallas_call | solution.py:26
  61.3 0.9 %shard_map.113 = bf16[1024,256]{1,0:T(8,128)(2,1)} custom-call(s32[1]{0:T(128)} %bitcast.7.last, f32[1024,256]{1,0:T(8,128)S(1)} %get-tuple-element.41.partial, bf16[512,256]{1,0:T(8,128)(2,1)S(1)} %collective-permute-done.1.incoming), custom_call_target="tpu_custom_call" | custom-call | bytes 1310724 | tf_op jit(solution)/shard_map/pallas_call | solution.py:26
  62.2 3.0 %shard_map.118 = (f32[768,512]{1,0:T(8,128)}, f32[256,256]{1,0:T(8,128)}, f32[8,128]{1,0:T(8,128)S(1)}) custom-call(s32[2]{0:T(128)S(1)} %pad_add_fusion.scalars, bf16[912,128]{1,0:T(8,128)(2,1)} %collective-permute-done.14.given, bf16[912,128]{1,0:T(8,128)(2,1)S(1)} %shard_map.117.refs_0_, bf16[912,128]{1,0:T(8,128)(2,1)S(1)} %collective-permute-done.15.refs_1_, ...), custom_call_target="tpu_custom_call" | custom-call | bytes 1867784 | tf_op jit(solution)/shard_map/pallas_call | solution.py:26
  65.2 0.6 slice_bitcast_fusion.1
  65.8 0.6 slice_bitcast_fusion.2
  (47 shorter events, 0.3 us)
Async XLA Ops:
  1.6 13.3 %collective-permute-start = (bf16[512,256]{1,0:T(8,128)(2,1)S(1)}, bf16[512,256]{1,0:T(8,128)(2,1)S(1)}, u32[]{:S(2)}, u32[]{:S(2)}) collective-permute-start(bf16[512,256]{1,0:T(8,128)(2,1)S(1)} %slice_bitcast_fusion), channel_id=1, source_target_pairs={{0,2},{2,4},{4,6},{6,8},{8,10},{10,12},{12,14},{14,16},{16,18},{18... | collective-permute-start | bytes 786440 | tf_op jit(solution)/shard_map/ppermute | solution.py:362
  4.6 1.1 %copy-start = (bf16[768,512]{1,0:T(8,128)(2,1)S(1)}, bf16[768,512]{1,0:T(8,128)(2,1)}, u32[]{:S(2)}) copy-start(bf16[768,512]{1,0:T(8,128)(2,1)} %weight.7) | copy-start | bytes 2359300
  5.7 1.0 %copy-start.2 = (bf16[1,1024,256]{2,1,0:T(8,128)(2,1)S(1)}, bf16[1,1024,256]{2,1,0:T(8,128)(2,1)}, u32[]{:S(2)}) copy-start(bf16[1,1024,256]{2,1,0:T(8,128)(2,1)} %param.6) | copy-start | bytes 1572868
  6.8 1.0 %copy-start.4 = (bf16[1,1024,256]{2,1,0:T(8,128)(2,1)S(1)}, bf16[1,1024,256]{2,1,0:T(8,128)(2,1)}, u32[]{:S(2)}) copy-start(bf16[1,1024,256]{2,1,0:T(8,128)(2,1)} %param.11) | copy-start | bytes 1572868
  7.8 0.9 %copy-start.10 = (bf16[256,256]{1,0:T(8,128)(2,1)S(1)}, bf16[256,256]{1,0:T(8,128)(2,1)}, u32[]{:S(2)}) copy-start(bf16[256,256]{1,0:T(8,128)(2,1)} %out_weight.3) | copy-start | bytes 393220
  8.7 0.7 %copy-start.12 = (f32[512]{0:T(512)S(1)}, f32[512]{0:T(512)}, u32[]{:S(2)}) copy-start(f32[512]{0:T(512)} %param.8) | copy-start | bytes 6148
  9.4 5.5 %copy-start.5 = (bf16[1,1024,256]{2,1,0:T(8,128)(2,1)S(1)}, bf16[1,1024,256]{2,1,0:T(8,128)(2,1)}, u32[]{:S(2)}) copy-start(bf16[1,1024,256]{2,1,0:T(8,128)(2,1)} %param.11) | copy-start | bytes 1572868
  11.2 5.9 %copy-start.14 = (bf16[512,512]{1,0:T(8,128)(2,1)}, bf16[512,512]{1,0:T(8,128)(2,1)S(1)}, u32[]{:S(2)}) copy-start(bf16[512,512]{1,0:T(8,128)(2,1)S(1)} %get-tuple-element.39.dpre_late) | copy-start | bytes 1572868
  11.2 5.9 %copy-start.16 = (bf16[512,256]{1,0:T(8,128)(2,1)}, bf16[512,256]{1,0:T(8,128)(2,1)S(1)}, u32[]{:S(2)}) copy-start(bf16[512,256]{1,0:T(8,128)(2,1)S(1)} %get-tuple-element.37.mixed_late) | copy-start | bytes 786436
  17.1 0.7 %copy-start.8 = (bf16[512,256]{1,0:T(8,128)(2,1)}, bf16[512,256]{1,0:T(8,128)(2,1)S(1)}, u32[]{:S(2)}) copy-start(bf16[512,256]{1,0:T(8,128)(2,1)S(1)} %get-tuple-element.36.mixed_early) | copy-start | bytes 786436
  17.8 2.7 %collective-permute-start.2 = (bf16[3600,128]{1,0:T(8,128)(2,1)}, bf16[3600,128]{1,0:T(8,128)(2,1)S(1)}, u32[]{:S(2)}, u32[]{:S(2)}) collective-permute-start(bf16[3600,128]{1,0:T(8,128)(2,1)} %get-tuple-element.44), channel_id=1, source_target_pairs={{0,1},{1,0},{2,3},{3,2},{4,5},{5,4},{6,7},{7,6},{8,9},{9,8},{10,11... | collective-permute-start | bytes 2764808 | tf_op jit(solution)/shard_map/ppermute | solution.py:292
  21.3 0.8 %copy-start.7 = (f32[904,128]{1,0:T(8,128)}, f32[904,128]{1,0:T(8,128)S(1)}, u32[]{:S(2)}) copy-start(f32[904,128]{1,0:T(8,128)S(1)} %get-tuple-element.45) | copy-start | bytes 1388548
  22.1 24.5 %copy-start.1 = (bf16[768,512]{1,0:T(8,128)(2,1)S(1)}, bf16[768,512]{1,0:T(8,128)(2,1)}, u32[]{:S(2)}) copy-start(bf16[768,512]{1,0:T(8,128)(2,1)} %weight.7) | copy-start | bytes 2359300
  22.1 3.9 %collective-permute-start.3 = (bf16[912,128]{1,0:T(8,128)(2,1)}, bf16[912,128]{1,0:T(8,128)(2,1)S(1)}, u32[]{:S(2)}, u32[]{:S(2)}) collective-permute-start(bf16[912,128]{1,0:T(8,128)(2,1)} %get-tuple-element.46), channel_id=1, source_target_pairs={{0,3},{2,1},{4,7},{6,5},{8,11},{10,9},{12,15},{14,13},{16,19},{18,... | collective-permute-start | bytes 700424 | tf_op jit(solution)/shard_map/ppermute | solution.py:299
  22.1 3.9 %collective-permute-start.4 = (bf16[912,128]{1,0:T(8,128)(2,1)}, bf16[912,128]{1,0:T(8,128)(2,1)S(1)}, u32[]{:S(2)}, u32[]{:S(2)}) collective-permute-start(bf16[912,128]{1,0:T(8,128)(2,1)} %get-tuple-element.47), channel_id=1, source_target_pairs={{0,5},{2,7},{4,1},{6,3},{8,13},{10,15},{12,9},{14,11},{16,21},{18,... | collective-permute-start | bytes 700424 | tf_op jit(solution)/shard_map/ppermute | solution.py:299
  22.1 6.3 %collective-permute-start.5 = (bf16[912,128]{1,0:T(8,128)(2,1)S(1)}, bf16[912,128]{1,0:T(8,128)(2,1)S(1)}, u32[]{:S(2)}, u32[]{:S(2)}) collective-permute-start(bf16[912,128]{1,0:T(8,128)(2,1)S(1)} %get-tuple-element.48), channel_id=1, source_target_pairs={{0,7},{2,5},{4,3},{6,1},{8,15},{10,13},{12,11},{14,9},{16,23},{18,... | collective-permute-start | bytes 700424 | tf_op jit(solution)/shard_map/ppermute | solution.py:299
  28.5 28.3 %copy-start.3 = (bf16[1,1024,256]{2,1,0:T(8,128)(2,1)S(1)}, bf16[1,1024,256]{2,1,0:T(8,128)(2,1)}, u32[]{:S(2)}) copy-start(bf16[1,1024,256]{2,1,0:T(8,128)(2,1)} %param.6) | copy-start | bytes 1572868
  28.5 28.3 %copy-start.6 = (bf16[1,1024,256]{2,1,0:T(8,128)(2,1)S(1)}, bf16[1,1024,256]{2,1,0:T(8,128)(2,1)}, u32[]{:S(2)}) copy-start(bf16[1,1024,256]{2,1,0:T(8,128)(2,1)} %param.11) | copy-start | bytes 1572868
  28.5 28.3 %copy-start.11 = (bf16[256,256]{1,0:T(8,128)(2,1)S(1)}, bf16[256,256]{1,0:T(8,128)(2,1)}, u32[]{:S(2)}) copy-start(bf16[256,256]{1,0:T(8,128)(2,1)} %out_weight.3) | copy-start | bytes 393220
  28.5 28.3 %copy-start.13 = (f32[256]{0:T(256)S(1)}, f32[256]{0:T(256)}, u32[]{:S(2)}) copy-start(f32[256]{0:T(256)} %param.10) | copy-start | bytes 3076
  29.1 8.3 %collective-permute-start.6 = (f32[232,128]{1,0:T(8,128)S(1)}, f32[232,128]{1,0:T(8,128)S(1)}, u32[]{:S(2)}, u32[]{:S(2)}) collective-permute-start(f32[232,128]{1,0:T(8,128)S(1)} %get-tuple-element.49), channel_id=1, source_target_pairs={{0,1},{1,0},{2,3},{3,2},{4,5},{5,4},{6,7},{7,6},{8,9},{9,8},{10,11... | collective-permute-start | bytes 356360 | tf_op jit(solution)/shard_map/ppermute | solution.py:292
  31.5 3.9 %collective-permute-start.7 = (bf16[240,128]{1,0:T(8,128)(2,1)}, bf16[240,128]{1,0:T(8,128)(2,1)S(1)}, u32[]{:S(2)}, u32[]{:S(2)}) collective-permute-start(bf16[240,128]{1,0:T(8,128)(2,1)} %get-tuple-element.50), channel_id=1, source_target_pairs={{1,8},{3,10},{5,12},{7,14},{9,0},{11,2},{13,4},{15,6},{17,24},{19,... | collective-permute-start | bytes 184328 | tf_op jit(solution)/shard_map/ppermute | solution.py:299
  31.5 5.9 %collective-permute-start.8 = (bf16[240,128]{1,0:T(8,128)(2,1)S(1)}, bf16[240,128]{1,0:T(8,128)(2,1)S(1)}, u32[]{:S(2)}, u32[]{:S(2)}) collective-permute-start(bf16[240,128]{1,0:T(8,128)(2,1)S(1)} %get-tuple-element.51), channel_id=1, source_target_pairs={{1,16},{3,18},{5,20},{7,22},{9,24},{11,26},{13,28},{15,30},{17,0},... | collective-permute-start | bytes 184328 | tf_op jit(solution)/shard_map/ppermute | solution.py:299
  31.5 5.9 %collective-permute-start.9 = (bf16[240,128]{1,0:T(8,128)(2,1)S(1)}, bf16[240,128]{1,0:T(8,128)(2,1)S(1)}, u32[]{:S(2)}, u32[]{:S(2)}) collective-permute-start(bf16[240,128]{1,0:T(8,128)(2,1)S(1)} %get-tuple-element.52), channel_id=1, source_target_pairs={{1,24},{3,26},{5,28},{7,30},{9,16},{11,18},{13,20},{15,22},{17,8},... | collective-permute-start | bytes 184328 | tf_op jit(solution)/shard_map/ppermute | solution.py:299
  37.5 3.2 %collective-permute-start.10 = (bf16[240,128]{1,0:T(8,128)(2,1)S(1)}, bf16[240,128]{1,0:T(8,128)(2,1)S(1)}, u32[]{:S(2)}, u32[]{:S(2)}) collective-permute-start(bf16[240,128]{1,0:T(8,128)(2,1)S(1)} %shard_map.116.refs_0_), channel_id=1, source_target_pairs={{0,1},{1,0},{2,3},{3,2},{4,5},{5,4},{6,7},{7,6},{8,9},{9,8},{10,11... | collective-permute-start | bytes 184328 | tf_op jit(solution)/shard_map/ppermute | solution.py:292
  37.5 3.2 %collective-permute-start.11 = (bf16[240,128]{1,0:T(8,128)(2,1)S(1)}, bf16[240,128]{1,0:T(8,128)(2,1)S(1)}, u32[]{:S(2)}, u32[]{:S(2)}) collective-permute-start(bf16[240,128]{1,0:T(8,128)(2,1)S(1)} %shard_map.116.refs_0_), channel_id=1, source_target_pairs={{0,9},{2,11},{4,13},{6,15},{8,1},{10,3},{12,5},{14,7},{16,25},{18,... | collective-permute-start | bytes 184328 | tf_op jit(solution)/shard_map/ppermute | solution.py:299
  38.9 2.4 %collective-permute-start.12 = (bf16[240,128]{1,0:T(8,128)(2,1)S(1)}, bf16[240,128]{1,0:T(8,128)(2,1)S(1)}, u32[]{:S(2)}, u32[]{:S(2)}) collective-permute-start(bf16[240,128]{1,0:T(8,128)(2,1)S(1)} %shard_map.116.refs_0_), channel_id=1, source_target_pairs={{0,17},{2,19},{4,21},{6,23},{8,25},{10,27},{12,29},{14,31},{16,1},... | collective-permute-start | bytes 184328 | tf_op jit(solution)/shard_map/ppermute | solution.py:299
  39.1 3.4 %collective-permute-start.13 = (bf16[240,128]{1,0:T(8,128)(2,1)S(1)}, bf16[240,128]{1,0:T(8,128)(2,1)S(1)}, u32[]{:S(2)}, u32[]{:S(2)}) collective-permute-start(bf16[240,128]{1,0:T(8,128)(2,1)S(1)} %shard_map.116.refs_0_), channel_id=1, source_target_pairs={{0,25},{2,27},{4,29},{6,31},{8,17},{10,19},{12,21},{14,23},{16,9},... | collective-permute-start | bytes 184328 | tf_op jit(solution)/shard_map/ppermute | solution.py:299
  43.1 6.8 %collective-permute-start.15 = (bf16[912,128]{1,0:T(8,128)(2,1)S(1)}, bf16[912,128]{1,0:T(8,128)(2,1)S(1)}, u32[]{:S(2)}, u32[]{:S(2)}) collective-permute-start(bf16[912,128]{1,0:T(8,128)(2,1)S(1)} %shard_map.117.refs_0_), channel_id=1, source_target_pairs={{1,2},{3,0},{5,6},{7,4},{9,10},{11,8},{13,14},{15,12},{17,18},{19,... | collective-permute-start | bytes 700424 | tf_op jit(solution)/shard_map/ppermute | solution.py:299
  45.5 7.8 %collective-permute-start.16 = (bf16[912,128]{1,0:T(8,128)(2,1)S(1)}, bf16[912,128]{1,0:T(8,128)(2,1)}, u32[]{:S(2)}, u32[]{:S(2)}) collective-permute-start(bf16[912,128]{1,0:T(8,128)(2,1)S(1)} %shard_map.117.refs_0_), channel_id=1, source_target_pairs={{1,4},{3,6},{5,0},{7,2},{9,12},{11,14},{13,8},{15,10},{17,20},{19,... | collective-permute-start | bytes 700424 | tf_op jit(solution)/shard_map/ppermute | solution.py:299
  45.5 8.3 %collective-permute-start.17 = (bf16[912,128]{1,0:T(8,128)(2,1)S(1)}, bf16[912,128]{1,0:T(8,128)(2,1)}, u32[]{:S(2)}, u32[]{:S(2)}) collective-permute-start(bf16[912,128]{1,0:T(8,128)(2,1)S(1)} %shard_map.117.refs_0_), channel_id=1, source_target_pairs={{1,6},{3,4},{5,2},{7,0},{9,14},{11,12},{13,10},{15,8},{17,22},{19,... | collective-permute-start | bytes 700424 | tf_op jit(solution)/shard_map/ppermute | solution.py:299
  47.1 14.2 %collective-permute-start.1 = (bf16[512,256]{1,0:T(8,128)(2,1)S(1)}, bf16[512,256]{1,0:T(8,128)(2,1)S(1)}, u32[]{:S(2)}, u32[]{:S(2)}) collective-permute-start(bf16[512,256]{1,0:T(8,128)(2,1)S(1)} %shard_map.112), channel_id=1, source_target_pairs={{2,0},{4,2},{6,4},{8,6},{10,8},{12,10},{14,12},{16,14},{18,16},{20... | collective-permute-start | bytes 786440 | tf_op jit(solution)/shard_map/ppermute | solution.py:401
  48.9 13.3 %collective-permute-start.14 = (bf16[912,128]{1,0:T(8,128)(2,1)S(1)}, bf16[912,128]{1,0:T(8,128)(2,1)}, u32[]{:S(2)}, u32[]{:S(2)}) collective-permute-start(bf16[912,128]{1,0:T(8,128)(2,1)S(1)} %shard_map.117.refs_0_), channel_id=1, source_target_pairs={{0,1},{1,0},{2,3},{3,2},{4,5},{5,4},{6,7},{7,6},{8,9},{9,8},{10,11... | collective-permute-start | bytes 700424 | tf_op jit(solution)/shard_map/ppermute | solution.py:292
  49.9 12.3 %collective-permute-start.18 = (bf16[912,128]{1,0:T(8,128)(2,1)S(1)}, bf16[912,128]{1,0:T(8,128)(2,1)}, u32[]{:S(2)}, u32[]{:S(2)}) collective-permute-start(bf16[912,128]{1,0:T(8,128)(2,1)S(1)} %collective-permute-done.15.refs_1_), channel_id=1, source_target_pairs={{0,1},{1,0},{2,3},{3,2},{4,5},{5,4},{6,7},{7,6},{8,9},{9,8},{10,11... | collective-permute-start | bytes 700424 | tf_op jit(solution)/shard_map/ppermute | solution.py:292
  53.2 8.9 %collective-permute-start.19 = (bf16[912,128]{1,0:T(8,128)(2,1)}, bf16[912,128]{1,0:T(8,128)(2,1)}, u32[]{:S(2)}, u32[]{:S(2)}) collective-permute-start(bf16[912,128]{1,0:T(8,128)(2,1)} %collective-permute-done.16.refs_2_), channel_id=1, source_target_pairs={{0,1},{1,0},{2,3},{3,2},{4,5},{5,4},{6,7},{7,6},{8,9},{9,8},{10,11... | collective-permute-start | bytes 700424 | tf_op jit(solution)/shard_map/ppermute | solution.py:292
  53.9 8.3 %collective-permute-start.20 = (bf16[912,128]{1,0:T(8,128)(2,1)}, bf16[912,128]{1,0:T(8,128)(2,1)}, u32[]{:S(2)}, u32[]{:S(2)}) collective-permute-start(bf16[912,128]{1,0:T(8,128)(2,1)} %collective-permute-done.17.refs_3_), channel_id=1, source_target_pairs={{0,1},{1,0},{2,3},{3,2},{4,5},{5,4},{6,7},{7,6},{8,9},{9,8},{10,11... | collective-permute-start | bytes 700424 | tf_op jit(solution)/shard_map/ppermute | solution.py:292
  56.7 1.0 %copy-start.9 = (bf16[512,256]{1,0:T(8,128)(2,1)S(1)}, bf16[512,256]{1,0:T(8,128)(2,1)}, u32[]{:S(2)}) copy-start(bf16[512,256]{1,0:T(8,128)(2,1)} %copy-done.8) | copy-start | bytes 786436
  57.7 1.0 %copy-start.15 = (bf16[512,512]{1,0:T(8,128)(2,1)S(1)}, bf16[512,512]{1,0:T(8,128)(2,1)}, u32[]{:S(2)}) copy-start(bf16[512,512]{1,0:T(8,128)(2,1)} %copy-done.14) | copy-start | bytes 1572868
  58.7 0.9 %copy-start.17 = (bf16[512,256]{1,0:T(8,128)(2,1)S(1)}, bf16[512,256]{1,0:T(8,128)(2,1)}, u32[]{:S(2)}) copy-start(bf16[512,256]{1,0:T(8,128)(2,1)} %copy-done.16) | copy-start | bytes 786436

commit v2 on v1

v2 whole, which is shorter than its diff:
```python
import functools

import jax
import jax.numpy as jnp
from jax import lax
from jax.experimental import pallas as pl
from jax.experimental.pallas import tpu as pltpu
from jax.sharding import PartitionSpec as P

STEP = 256
TAPS = 3
SPAN = (TAPS - 1) * STEP
BOTH = ("tm", "run")
LANES = 128
SUBLANES = 8
BIAS_ROWS = 2 * SUBLANES
F32 = jnp.float32
BF16 = jnp.bfloat16
VMEM = pl.BlockSpec(memory_space=pltpu.VMEM)
ANY = pl.BlockSpec(memory_space=pl.ANY)
HBM = pl.BlockSpec(memory_space=pltpu.HBM)
MIB = 1024 * 1024


def call(kernel, out_shape, args, flops=0, scratch=(), after=(), far=(), alias=None):
    moved = sum(a.size * a.dtype.itemsize for a in args)
    inner = kernel
    if after:
        count = len(args)
        inner = lambda *refs: kernel(*refs[:count], *refs[count + len(after) :])
    ins = [HBM if i in far else VMEM for i in range(len(args))]
    outs = [HBM if -1 - i in far else VMEM for i in range(len(out_shape))]
    placed = [
        pltpu.with_memory_space_constraint(a, pltpu.HBM if i in far else pltpu.VMEM)
        for i, a in enumerate(args)
    ]
    return pl.pallas_call(
        inner,
        out_shape=out_shape,
        in_specs=ins + [ANY] * len(after),
        out_specs=outs,
        scratch_shapes=list(scratch),
        input_output_aliases=alias or {},
        cost_estimate=pl.CostEstimate(flops=0, bytes_accessed=8, transcendentals=0),
        compiler_params=pltpu.CompilerParams(vmem_limit_bytes=(8 if count_of_chips() <= 16 else 40) * MIB),
    )(*placed, *after)


def held(dtype, *dims):
    return pltpu.VMEM(dims, dtype)


def shape(dtype, *dims):
    return jax.ShapeDtypeStruct(dims, dtype)


def count_of_chips():
    return lax.axis_size("tm") * lax.axis_size("run") // 2


def place_of():
    flat = lax.axis_index("tm") * lax.axis_size("run") + lax.axis_index("run")
    return flat // 2, lax.rem(flat, 2)


def digit_of(level):
    chip = place_of()[0]
    return sum(lax.rem(chip // (1 << bit), 2) * (1 << i) for i, bit in enumerate(level))


def steps_of(level):
    last = (1 << len(level)) - 1
    return [last, *range(1, last)]


def step_between(level, k):
    return sum(1 << bit for i, bit in enumerate(level) if k >> i & 1)


TOKEN = held(F32, SUBLANES, LANES)


def dot(a, b):
    return jnp.dot(a, b, preferred_element_type=F32)


def dot_rows(a, b):
    return lax.dot_general(a, b, (((0,), (0,)), ((), ())), preferred_element_type=F32)


def dot_columns(a, b):
    return lax.dot_general(a, b, (((1,), (1,)), ((), ())), preferred_element_type=F32)


def gates(preact, dmixed):
    channels = dmixed.shape[1]
    filtered = jnp.tanh(preact[:, :channels])
    gated = jax.nn.sigmoid(preact[:, channels:])
    mixed = filtered * gated
    dfiltered = dmixed * gated * (1.0 - filtered * filtered)
    dgated = dmixed * mixed * (1.0 - gated)
    return mixed.astype(BF16), dfiltered.astype(BF16), dgated.astype(BF16)


def late_kernel(
    signal_in, weight_in, bias, out_weight_in, cot_in,
    signal, weight, out_weight, cot,
    preact_out, dmixed_out, mixed_out, dpre_out, grad_conv, grad_proj, grad_bias, sems,
):
    rows, channels = signal.shape
    pairs = ((signal_in, signal), (weight_in, weight), (cot_in, cot), (out_weight_in, out_weight))
    copies = [pltpu.make_async_copy(a, b, sems.at[i]) for i, (a, b) in enumerate(pairs)]
    for copy in copies:
        copy.start()
    tap = lambda k: weight[k * channels : (k + 1) * channels, :]
    copies[0].wait()
    copies[1].wait()
    preact_out[...] = dot(signal[:SPAN, :], tap(0)) + bias[...]
    for k in range(1, TAPS - 1):
        preact_out[k * STEP :, :] += dot(signal[: SPAN - k * STEP, :], tap(k))
    copies[2].wait()
    copies[3].wait()
    dmixed_out[...] = dot_columns(cot[:SPAN, :], out_weight[...])
    for begin in range(SPAN, rows, STEP):
        here = slice(begin, begin + STEP)
        at = slice(begin - SPAN, begin - SPAN + STEP)
        preact = bias[...]
        for k in range(TAPS):
            preact = preact + dot(signal[begin - k * STEP : begin - k * STEP + STEP, :], tap(k))
        mixed, dfiltered, dgated = gates(preact, dot_columns(cot[here, :], out_weight[...]))
        mixed_out[at, :] = mixed
        dpre_out[at, :channels] = dfiltered
        dpre_out[at, channels:] = dgated
    dpre = dpre_out[...]
    for k in range(TAPS):
        grad_conv[k * channels : (k + 1) * channels, :] = dot_rows(
            signal[SPAN - k * STEP : rows - k * STEP, :], dpre
        )
    grad_proj[...] = dot_rows(mixed_out[...], cot[SPAN:, :])
    ones = jnp.ones((BIAS_ROWS, rows), BF16)
    grad_bias[:, : 2 * channels] = dot(ones[:, : rows - SPAN], dpre)[:SUBLANES]
    grad_bias[:, 2 * channels :] = dot(ones, cot[...])[:SUBLANES]


def early_kernel(
    level, pieces, history, signal, weight, cot, preact_in, dmixed_in, conv_in, proj_in, bias_in,
    mixed_out, dpre_out, *refs,
):
    radix, digit, core = 1 << len(level), digit_of(level), place_of()[1]
    turn = steps_of(level)
    first = lax.axis_index("tm") == 0
    own, offered = refs[:radix], refs[radix : 2 * radix - 1]
    past, grad_conv, grad_proj = refs[2 * radix - 1 :]
    rows, channels = signal.shape
    tap = lambda k: weight[k * channels : (k + 1) * channels, :]
    past[...] = jnp.where(first, jnp.zeros_like(history), history[...])
    for begin in range(0, SPAN, STEP):
        here = slice(begin, begin + STEP)
        preact = preact_in[here, :]
        for k in range(begin // STEP + 1, TAPS):
            source = SPAN + begin - k * STEP
            preact = preact + dot(past[source : source + STEP, :], tap(k))
        mixed, dfiltered, dgated = gates(preact, dmixed_in[here, :])
        mixed_out[here, :] = mixed
        dpre_out[here, :channels] = dfiltered
        dpre_out[here, channels:] = dgated
    dpre = dpre_out[...]
    for k in range(TAPS):
        at = slice(k * channels, (k + 1) * channels)
        total = conv_in[at, :]
        if k:
            total = total + dot_rows(past[SPAN - k * STEP :, :], dpre[: k * STEP, :])
        if k < TAPS - 1:
            total = total + dot_rows(signal[: SPAN - k * STEP, :], dpre[k * STEP :, :])
        grad_conv[at, :] = total
    grad_proj[: proj_in.shape[0], :] = proj_in[...] + dot_rows(mixed_out[...], cot[:SPAN, :])
    for grad, filled in ((grad_conv, conv_in.shape[0]), (grad_proj, proj_in.shape[0])):
        if filled < grad.shape[0]:
            grad[filled:, :] = jnp.zeros((grad.shape[0] - filled, grad.shape[1]), F32)
    ones = jnp.ones((BIAS_ROWS, SPAN), BF16)
    columns = dot(ones, dpre)[:SUBLANES]
    bias = bias_in[...]
    bias = jnp.concatenate([bias[:, : 2 * channels] + columns, bias[:, 2 * channels :]], 1)
    lines = [bias[:1, c : c + LANES] for c in range(0, bias.shape[1], LANES)]
    lines += [jnp.zeros((1, LANES), F32)] * (SUBLANES - len(lines))
    bias = jnp.concatenate(lines, 0)
    for k in range(radix):
        at = 0
        for piece in range(pieces // radix):
            index = (digit ^ k) * (pieces // radix) + piece
            for grad in (grad_conv, grad_proj):
                height = grad.shape[0] // pieces
                begin = pl.multiple_of(index * height, 16)
                for column in range(0, grad.shape[1], LANES):
                    block = grad[pl.ds(begin, height), column : column + LANES]
                    own[k][at : at + height, :] = block
                    if k in turn[1:]:
                        offered[turn.index(k)][at : at + height, :] = block.astype(BF16)
                    at += height
        own[k][at:, :] = bias
        if k in turn[1:]:
            offered[turn.index(k)][at:, :] = narrowed(bias)
    offered[0][at:, :] = narrowed(bias)
    for mine, k in ((0, 0), (1, turn[0])):

        @pl.when(core == mine)
        def _():
            offered[0][:at, :] = own[k][:at, :].astype(BF16)


def back_kernel(dpre, weight, out):
    channels = out.shape[1]
    tap = lambda k: weight[k * channels : (k + 1) * channels, :]
    for begin in range(0, SPAN, STEP):
        total = dot_columns(dpre[begin : begin + STEP, :], tap(TAPS - 1))
        for k in range(1, TAPS - 1):
            source = begin - SPAN + k * STEP
            if source >= 0:
                total = total + dot_columns(dpre[source : source + STEP, :], tap(k))
        out[begin : begin + STEP, :] = total.astype(BF16)


def own_kernel(signal, weight, out_weight, out_bias, cot, mixed_early, mixed_late, dpre_early, dpre_late, output, partial, token):
    rows, channels = signal.shape
    tap = lambda k: weight[k * channels : (k + 1) * channels, :]
    token[...] = jnp.zeros_like(token)

    def part(early, late, begin):
        ref, at = (early, begin) if begin < SPAN else (late, begin - SPAN)
        return ref[at : at + STEP, :]

    for begin in range(0, rows, STEP):
        here = slice(begin, begin + STEP)
        hidden = dot(part(mixed_early, mixed_late, begin), out_weight[...]) + out_bias[...]
        output[here, :] = (signal[here, :].astype(F32) + hidden).astype(BF16)
        total = cot[here, :].astype(F32)
        for k in range(TAPS):
            if begin + k * STEP < rows:
                total = total + dot_columns(part(dpre_early, dpre_late, begin + k * STEP), tap(k))
        partial[here, :] = total


PLANE = 4


def relay_pairs():
    runs, size = lax.axis_size("run"), lax.axis_size("tm")
    pairs = []
    for t in range(size):
        for r in range(runs):
            to = ((t - PLANE) % size) * runs + r if t % PLANE == 0 else t * runs + (r ^ 1)
            pairs.append((t * runs + r, to))
    return pairs


def plane_pairs():
    size = lax.axis_size("tm")
    return [(t, t - 1 if t % PLANE else t + PLANE - 1) for t in range(size)]


def relay_kernel(back, relayed, onward):
    first = lax.rem(lax.axis_index("tm"), PLANE) == 0
    onward[...] = jnp.where(first, relayed[...], back[...])


def join_kernel(partial, incoming, out, token):
    token[...] = jnp.zeros_like(token)
    rows = partial.shape[0]
    last = lax.axis_index("tm") == lax.axis_size("tm") - 1
    out[: rows - SPAN, :] = partial[: rows - SPAN, :].astype(BF16)
    more = jnp.where(last, jnp.zeros(incoming.shape, F32), incoming[...].astype(F32))
    out[rows - SPAN :, :] = (partial[rows - SPAN :, :] + more).astype(BF16)


def piece_height(rows, pieces):
    return -(-rows // (pieces * 16)) * 16


def widened(block):
    wide = block.astype(F32)
    return wide[:SUBLANES] + wide[SUBLANES:]


def narrowed(total):
    high = total.astype(BF16).astype(F32)
    return jnp.concatenate([high, total - high], 0).astype(BF16)


def first_kernel(keep_own, send_own, received, keep, send):
    end = send.shape[0] - BIAS_ROWS
    more, bias = received[:end, :].astype(F32), widened(received[end:, :])
    keep[:end, :] = keep_own[:end, :] + more
    keep[end:, :] = keep_own[end:, :] + bias
    send[:end, :] = (send_own[:end, :] + more).astype(BF16)
    send[end:, :] = narrowed(send_own[end:, :] + bias)


def next_kernel(send_own, received, send):
    end = send.shape[0] - BIAS_ROWS
    send[:end, :] = (send_own[:end, :] + received[:end, :].astype(F32)).astype(BF16)
    send[end:, :] = narrowed(send_own[end:, :] + widened(received[end:, :]))


def split_kernel(level, more, *refs):
    radix, digit = 1 << len(level), digit_of(level)
    main, received = refs[0], refs[1 : 1 + more]
    sends, keep = refs[1 + more : -1], refs[-1]
    rows, end = sends[0].shape[0] - BIAS_ROWS, main.shape[0] - SUBLANES
    total = main[end:, :]
    for ref in received:
        total = total + widened(ref[end:, :])
    for k in range(radix):
        start = pl.multiple_of((digit ^ k) * rows, 16)
        block = main[pl.ds(start, rows), :]
        for ref in received:
            block = block + ref[pl.ds(start, rows), :].astype(F32)
        if k:
            sends[k - 1][:rows, :] = block.astype(BF16)
            sends[k - 1][rows:, :] = narrowed(total)
        else:
            keep[:rows, :] = block
            keep[rows:, :] = total


def finish_kernel(scale, *refs):
    keep, received, out = refs[0], refs[1:-1], refs[-1]
    rows = out.shape[0] - BIAS_ROWS
    block, total = keep[:rows, :], keep[rows:, :]
    for ref in received:
        block = block + ref[:rows, :].astype(F32)
        total = total + widened(ref[rows:, :])
    out[:rows, :] = (block * scale).astype(BF16)
    out[rows:, :] = narrowed(total * scale)


def place_kernel(level, taker, given, *refs):
    radix, digit, core = 1 << len(level), digit_of(level), place_of()[1]
    parts, out = refs[:radix], refs[radix]
    rows = parts[0].shape[0] - BIAS_ROWS
    own = jnp.where(core == taker, given[...], parts[0][...])
    for k in range(radix):
        block = parts[k][...] if k else own
        index = digit ^ k
        out[pl.ds(pl.multiple_of(index * rows, 16), rows), :] = block[:rows]

        @pl.when(index == 0)
        def _():
            out[radix * rows :, :] = block[rows:]


def spread_kernel(steps, level, taker, pieces, *refs):
    count = len(steps)
    ends = steps[-1] != 0 and count == 1
    digit, core = digit_of(level), place_of()[1]
    direct, passed, refs = refs[:count], refs[count : 2 * count], refs[2 * count :]
    before, refs = (refs[0], refs[3:]) if ends else (None, refs)
    (conv, proj), refs = refs[:2], refs[2:]
    bias_out, (wide_conv, wide_proj, wide_bias, sems) = refs[:-4], refs[-4:]
    bias = before[...] if ends else jnp.zeros((SUBLANES, LANES), F32)
    copies = []

    def send(source, target, *at):
        copies.append(pltpu.make_async_copy(source, target, sems.at[at]))
        copies[-1].start()

    for k, here, there in zip(steps, direct, passed):
        end = here.shape[0] - BIAS_ROWS
        block = jnp.where((core == taker) == (k > 0), here[end:, :], there[end:, :])
        bias = jnp.where((digit ^ k) == 0, widened(block), bias)
    if ends:
        wide_bias[...] = jnp.concatenate([bias[i : i + 1, :] for i in range(SUBLANES)], 1)
        column = 0
        for n, out in enumerate(bias_out):
            send(wide_bias.at[:, column : column + out.shape[1]], out, count, n)
            column += out.shape[1]
    else:
        bias_out[0][...] = bias
    for n, (k, here, there) in enumerate(zip(steps, direct, passed)):
        block = jnp.where((core == taker) == (k > 0), here[...], there[...])
        at = 0
        for piece in range(pieces):
            for wide in (wide_conv, wide_proj):
                height = wide.shape[1] // pieces
                for column in range(0, wide.shape[2], LANES):
                    wide[n, piece * height : (piece + 1) * height, column : column + LANES] = (
                        block[at : at + height].astype(F32)
                    )
                    at += height
        for m, (wide, out) in enumerate(((wide_conv, conv), (wide_proj, proj))):
            height = wide.shape[1]
            start = pl.multiple_of((digit ^ k) * height, 16)
            send(wide.at[n], out.at[pl.ds(start, height), :], n, m)
    for copy in copies:
        copy.wait()


def levels_of(chips):
    count = chips.bit_length() - 1
    bits = list(range(count))
    return [tuple(bits[i : i + 2]) for i in range(0, count, 2)]


def swapped(array):
    chips = count_of_chips()
    return lax.ppermute(array, BOTH, [(i, i ^ 1) for i in range(2 * chips)])


def crossed(array, source, step):
    chips = count_of_chips()
    pairs = [(2 * c + source, 2 * (c ^ step) + 1 - source) for c in range(chips)]
    pairs += [(2 * c + 1 - source, 2 * c + source) for c in range(chips)]
    return lax.ppermute(array, BOTH, pairs)


def summed_everywhere(own, offered, scale, heights, widths, fill):
    chips = count_of_chips()
    levels = levels_of(chips)
    radix, turn = 1 << len(levels[0]), steps_of(levels[0])
    rows = own[0].shape[0] - SUBLANES
    exchanged = [swapped(message) for message in offered]
    keep, send = call(
        first_kernel,
        [held(F32, rows + SUBLANES, LANES), held(BF16, rows + BIAS_ROWS, LANES)],
        (own[0], own[turn[0]], exchanged[0]),
        after=fill(0, ()),
    )
    received = [crossed(send, 0, step_between(levels[0], turn[0]))]
    for k, message in zip(turn[1:], exchanged[1:]):
        (send,) = call(next_kernel, [held(BF16, rows + BIAS_ROWS, LANES)], (own[k], message))
        received.append(crossed(send, 0, step_between(levels[0], k)))
    ready = fill(1, (send,))
    source = 1
    for level in range(1, len(levels)):
        radix = 1 << len(levels[level])
        rows //= radix
        *sends, keep = call(
            functools.partial(split_kernel, levels[level], len(received)),
            [held(BF16, rows + BIAS_ROWS, LANES)] * (radix - 1) + [held(F32, rows + SUBLANES, LANES)],
            (keep, *received),
            after=ready if level == 1 else (),
        )
        if level == 1:
            fill(2, (sends[0],))
        keep = swapped(keep)
        received = [
            crossed(sends[k - 1], source, step_between(levels[level], k))
            for k in steps_of(levels[level])
        ]
        source = 1 - source
    (part,) = call(
        functools.partial(finish_kernel, scale),
        [held(BF16, rows + BIAS_ROWS, LANES)],
        (keep, *received),
        after=ready if len(levels) == 1 else (),
    )
    if len(levels) == 1:
        fill(2, (part,))
    for level in reversed(range(len(levels))):
        radix = 1 << len(levels[level])
        crossing = {
            k: crossed(part, source, step_between(levels[level], k)) for k in steps_of(levels[level])
        }
        given = swapped(part)
        parts = [part] + [crossing[k] for k in range(1, radix)]
        if level:
            rows = part.shape[0] - BIAS_ROWS
            (part,) = call(
                functools.partial(place_kernel, levels[level], 1 - source),
                [held(BF16, radix * rows + BIAS_ROWS, LANES)],
                (given, *parts),
                after=fill(3, ()) if level == 1 else (),
            )
            source = 1 - source
    taker, pieces = 1 - source, chips // radix
    whole = [shape(F32, chips * h, w) for h, w in zip(heights, widths)]

    def room(count):
        return [
            *[pltpu.VMEM((count, pieces * h, w), F32) for h, w in zip(heights, widths)],
            pltpu.VMEM((1, SUBLANES * LANES), F32),
            pltpu.SemaphoreType.DMA((count + 1, 2)),
        ]

    early, last = [0, *turn[:-1]], turn[-1]
    forwarded = [given] + [swapped(parts[k]) for k in early[1:]]
    conv, proj, bias = call(
        functools.partial(spread_kernel, early, levels[0], taker, pieces),
        whole + [held(F32, SUBLANES, LANES)],
        (*[parts[k] for k in early], *forwarded),
        scratch=room(len(early)),
        far=(-1, -2),
    )
    return call(
        functools.partial(spread_kernel, [last], levels[0], taker, pieces),
        whole + [shape(F32, 1, w) for w in widths],
        (parts[last], swapped(parts[last]), bias, conv, proj),
        scratch=room(1),
        far=(-1, -2, -3, -4, 3, 4),
        alias={3: 0, 4: 1},
    )


def local(signal, conv_weight, conv_bias, out_weight, out_bias, cotangent):
    rows, channels = signal.shape[1:]
    wide = 2 * channels
    late = rows - SPAN
    size = lax.axis_size("tm")
    chips = count_of_chips()
    level = levels_of(chips)[0]
    radix = 1 << len(level)
    widths = (wide, channels)
    heights = [piece_height(n, chips) for n in (TAPS * channels, channels)]
    piece = chips // radix * sum(h * w // LANES for h, w in zip(heights, widths))

    history = lax.ppermute(signal[0, late:], "tm", [(i, (i + 1) % size) for i in range(size)])
    x, weight, proj_weight, cot, preact, dmixed, mixed_late, dpre_late, conv, proj, bias = call(
        late_kernel,
        [
            held(BF16, rows, channels), held(BF16, TAPS * channels, wide), held(BF16, channels, channels),
            held(BF16, rows, channels),
            held(F32, SPAN, wide), held(F32, SPAN, channels), held(BF16, late, channels),
            held(BF16, late, wide), held(F32, TAPS * channels, wide), held(F32, channels, channels),
            held(F32, SUBLANES, wide + channels),
        ],
        (signal[0], conv_weight, conv_bias.reshape(1, -1), out_weight, cotangent[0]),
        flops=3 * rows * channels * channels * 8,
        scratch=[pltpu.SemaphoreType.DMA((4,))],
        far=(0, 1, 3, 4),
    )
    mixed_early, dpre_early, *pieces = call(
        functools.partial(early_kernel, level, chips),
        [held(BF16, SPAN, channels), held(BF16, SPAN, wide)]
        + [held(F32, piece + SUBLANES, LANES)] * radix
        + [held(BF16, piece + BIAS_ROWS, LANES)] * (radix - 1),
        (
            history, x, weight, cot, preact, dmixed, conv, proj, bias,
        ),
        flops=2 * rows * channels * channels * 8,
        scratch=[pltpu.VMEM((SPAN, channels), BF16)]
        + [pltpu.VMEM((chips * h, w), F32) for h, w in zip(heights, widths)],
    )
    results = {}

    def fill(stage, after):
        if stage == 0:
            (results["back"],) = call(
                back_kernel, [held(BF16, SPAN, channels)], (dpre_early, weight), after=after
            )
            results["relayed"] = lax.ppermute(results["back"], BOTH, relay_pairs())
            return (results["back"],)
        if stage == 1:
            results["output"], results["partial"], token = call(
                own_kernel,
                [shape(BF16, rows, channels), held(F32, rows, channels), TOKEN],
                (
                    x, weight, proj_weight, out_bias.reshape(1, -1), cot,
                    mixed_early, mixed_late, dpre_early, dpre_late,
                ),
                after=after,
            )
            return (token,)
        if stage == 2:
            (onward,) = call(
                relay_kernel,
                [held(BF16, SPAN, channels)],
                (results["back"], results["relayed"]),
                after=after,
            )
            results["incoming"] = lax.ppermute(onward, "tm", plane_pairs())
            return ()
        results["grad_signal"], token = call(
            join_kernel,
            [shape(BF16, rows, channels), TOKEN],
            (
                results["partial"],
                results["incoming"],
            ),
            after=after,
        )
        return (token,)

    scale = float(signal.shape[0] * lax.axis_size("run") * rows * size) ** -0.5
    grad_conv, grad_proj, grad_cbias, grad_pbias = summed_everywhere(
        pieces[:radix], pieces[radix:], scale, heights, widths, fill
    )
    return (
        results["output"][None],
        results["grad_signal"][None],
        grad_conv[: TAPS * channels],
        grad_cbias[0],
        grad_proj[:channels],
        grad_pbias[0],
    )


def solution(mesh):
    placed = (P("run", "tm", None), P(), P(), P(), P(), P("run", "tm", None))
    return jax.shard_map(
        local,
        mesh=mesh,
        in_specs=placed,
        out_specs=(P("run", "tm", None), P("run", "tm", None), P(), P(), P(), P()),
        check_vma=False,
    )
```

time: 67.3 us -> 52 us (0.77); the launches traced: 66.4 us -> 51.8 us
  local copies, waits for them, and re-layouts: 13.2 us -> 1.92 us
  starting transfers between devices: 18.5 us -> 14.8 us
  waiting for transfers between devices: 21.7 us -> 24.2 us
  Pallas kernels: 12 us -> 10.1 us
    unnamed x36 -> x4, local copies, waits for them, and re-layouts: 9.24 us -> 0.95 us
    ppermute x7 -> x9, starting transfers between devices: 6.24 us -> 1.33 us  [swapped(): return lax.ppermute(array, BOTH, [(i, i ^ 1) for i in range(2 * chips)])]
    slice x5 -> x0, local copies, waits for them, and re-layouts: 3.92 us -> none  [the longest x2 1.8 us: summed_everywhere(): main, bias = (keep[:rows], keep[rows:])]
    ppermute x2 -> x3, waiting for transfers between devices: 3.73 us -> 6.78 us  [the longest x1 6.28 us: local(): lax.ppermute(signal[0, late:], 'tm', [(i, (i + 1) % size) for i in range(...]
    ppermute x2 -> x3, starting transfers between devices: 4.81 us -> 7.32 us  [the longest x1 2.99 us: local(): lax.ppermute(signal[0, late:], 'tm', [(i, (i + 1) % size) for i in range(...]
    pallas_call x10 -> x14, Pallas kernels: 12 us -> 10.1 us  [call(): pl.pallas_call(inner, out_shape=out_shape, in_specs=ins + [ANY] * len(aft...]
    ppermute x7 -> x9, waiting for transfers between devices: 2.7 us -> 0.78 us  [swapped(): return lax.ppermute(array, BOTH, [(i, i ^ 1) for i in range(2 * chips)])]
    ppermute x12, waiting for transfers between devices: 15.3 us -> 16.6 us  [crossed(): return lax.ppermute(array, BOTH, pairs)]
  transfers between devices with their start and end apart: 21 -> 24, of which waited for: 10 -> 12; matrix products, arithmetic and copies ran while one was open for 3% -> 0% of each run, Pallas kernels for 7% -> 15%
where the time goes in v2:
time: 52 us; the launch traced here: 51.8 us
  waiting for transfers between devices  24.2 us (47%)
  starting transfers between devices  14.8 us (28%)
  Pallas kernels  10.1 us (19%)
  local copies, waits for them, and re-layouts  1.92 us (4%)
  between operations  0.78 us (2%)
    ppermute x12, waiting for transfers between devices, crossed(): return lax.ppermute(array, BOTH, pairs)  16.6 us
    pallas_call x14, Pallas kernels, call(): pl.pallas_call(inner, out_shape=out_shape, in_specs=ins + [ANY] * len(aft...  10.1 us
    ppermute x1, waiting for transfers between devices, local(): lax.ppermute(signal[0, late:], 'tm', [(i, (i + 1) % size) for i in range(...  6.28 us
    ppermute x12, starting transfers between devices, crossed(): return lax.ppermute(array, BOTH, pairs)  6.18 us
    ppermute x1, starting transfers between devices, local(): lax.ppermute(signal[0, late:], 'tm', [(i, (i + 1) % size) for i in range(...  2.99 us
    ppermute x1, starting transfers between devices, fill(): results['incoming'] = lax.ppermute(onward, 'tm', plane_pairs())  2.63 us
    ppermute x1, starting transfers between devices, fill(): results['relayed'] = lax.ppermute(results['back'], BOTH, relay_pairs())  1.7 us
    ppermute x9, starting transfers between devices, swapped(): return lax.ppermute(array, BOTH, [(i, i ^ 1) for i in range(2 * chips)])  1.33 us
  transfers between devices with their start and end apart: 24, of which 12 were waited for; matrix products, arithmetic and copies ran while one was open for 0% of the time, Pallas kernels for 15%

profile of v2, /device:TPU:0, one launch (start us, length us, event | category | flops | bytes accessed | tf_op | source)
XLA Modules:
  0.0 51.8 jit_solution(1990360449189701928)
XLA Ops:
  0.6 1.0 %slice_bitcast_fusion = bf16[512,256]{1,0:T(8,128)(2,1)S(1)} fusion(bf16[1,1024,256]{2,1,0:T(8,128)(2,1)} %param.6), kind=kLoop, calls=%fused_computation | loop fusion | bytes 524288 | tf_op jit(solution)/shard_map/squeeze | solution.py:515
  1.6 3.0 %collective-permute-start = (bf16[512,256]{1,0:T(8,128)(2,1)S(1)}, bf16[512,256]{1,0:T(8,128)(2,1)S(1)}, u32[]{:S(2)}, u32[]{:S(2)}) collective-permute-start(bf16[512,256]{1,0:T(8,128)(2,1)S(1)} %slice_bitcast_fusion), channel_id=1, source_target_pairs={{0,2},{2,4},{4,6},{6,8},{8,10},{10,12},{12,14},{14,16},{16,18},{18... | collective-permute-start | bytes 786440 | tf_op jit(solution)/shard_map/ppermute | solution.py:515
  4.6 0.7 %copy-done = f32[512]{0:T(512)S(1)} copy-done((f32[512]{0:T(512)S(1)}, f32[512]{0:T(512)}, u32[]{:S(2)}) %copy-start) | copy-done | bytes 2072
  5.3 3.3 %shard_map.109 = (bf16[1024,256]{1,0:T(8,128)(2,1)S(1)}, bf16[768,512]{1,0:T(8,128)(2,1)S(1)}, bf16[256,256]{1,0:T(8,128)(2,1)S(1)}, bf16[1024,256]{1,0:T(8,128)...) custom-call(bf16[1024,256]{1,0:T(8,128)(2,1)} %bitcast.12, ...), custom_call_target="tpu_custom_call" | custom-call | bytes 8 | tf_op jit(solution)/shard_map/pallas_call | solution.py:37
  8.6 6.3 %collective-permute-done.history = bf16[512,256]{1,0:T(8,128)(2,1)S(1)} collective-permute-done((bf16[512,256]{1,0:T(8,128)(2,1)S(1)}, bf16[512,256]{1,0:T(8,128)(2,1)S(1)}, u32[]{:S(2)}, u32[]{:S(2)}) %collective-permute-start) | collective-permute-done | bytes 262176 | tf_op jit(solution)/shard_map/ppermute | solution.py:515
  14.9 1.4 %shard_map.110 = (bf16[512,256]{1,0:T(8,128)(2,1)S(1)}, bf16[512,512]{1,0:T(8,128)(2,1)S(1)}, f32[904,128]{1,0:T(8,128)S(1)}, f32[904,128]{1,0:T(8,128)S(1)}, f3...) custom-call(bf16[512,256]{1,0:T(8,128)(2,1)S(1)} %collective-permute, ...), custom_call_target="tpu_custom_call" | custom-call | bytes 8 | tf_op jit(solution)/shard_map/pallas_call | solution.py:37
  16.3 0.1 collective-permute-start.1
  16.4 0.5 collective-permute-start.3
  16.9 0.1 collective-permute-start.5
  16.9 0.4 shard_map.113.refs_3_.refs_0_
  17.3 1.7 %collective-permute-start.2 = (bf16[512,256]{1,0:T(8,128)(2,1)S(1)}, bf16[512,256]{1,0:T(8,128)(2,1)S(1)}, u32[]{:S(2)}, u32[]{:S(2)}) collective-permute-start(bf16[512,256]{1,0:T(8,128)(2,1)S(1)} %shard_map.113.refs_3_.refs_0_), channel_id=1, source_target_pairs={{0,24},{1,25},{2,3},{3,2},{4,5},{5,4},{6,7},{7,6},{8,0},{9,1},{10,... | collective-permute-start | bytes 786440 | tf_op jit(solution)/shard_map/ppermute | solution.py:549
  19.0 0.0 collective-permute-done.1.received
  19.1 0.1 collective-permute-start.7
  19.2 0.1 shard_map.114
  19.3 0.1 collective-permute-start.4
  19.3 0.0 collective-permute-done.5.received
  19.4 0.1 collective-permute-start.6
  19.5 0.3 copy-done.1
  19.7 1.6 %shard_map.112 = (bf16[1024,256]{1,0:T(8,128)(2,1)}, f32[1024,256]{1,0:T(8,128)S(1)}, f32[8,128]{1,0:T(8,128)S(1)}) custom-call(bf16[1024,256]{1,0:T(8,128)(2,1)S(1)} %get-tuple-element.44.signal.refs_0_, bf16[768,512]{1,0:T(8,128)(2,1)S(1)} %get-tuple-element.45.weight.refs_1_, bf16[256,256]{1,0:T(8,128)(2,1)S(1)} %get-tuple-element.46.refs_2_, ...), custom_call_target="tpu_custom_call" | custom-call | bytes 8 | tf_op jit(solution)/shard_map/pallas_call | solution.py:37
  21.3 2.5 %collective-permute-done.7.refs_3_ = bf16[912,128]{1,0:T(8,128)(2,1)S(1)} collective-permute-done((bf16[912,128]{1,0:T(8,128)(2,1)S(1)}, bf16[912,128]{1,0:T(8,128)(2,1)S(1)}, u32[]{:S(2)}, u32[]{:S(2)}) %collective-permute-start.7) | collective-permute-done | bytes 233504 | tf_op jit(solution)/shard_map/ppermute | solution.py:412
  23.9 0.0 collective-permute-done.4.refs_1_
  23.9 1.5 %collective-permute-done.6.refs_2_ = bf16[912,128]{1,0:T(8,128)(2,1)S(1)} collective-permute-done((bf16[912,128]{1,0:T(8,128)(2,1)S(1)}, bf16[912,128]{1,0:T(8,128)(2,1)S(1)}, u32[]{:S(2)}, u32[]{:S(2)}) %collective-permute-start.6) | collective-permute-done | bytes 233504 | tf_op jit(solution)/shard_map/ppermute | solution.py:412
  25.4 0.1 shard_map.116
  25.5 0.5 collective-permute-done.2.refs_1_
  26.1 2.6 %collective-permute-start.8 = (bf16[512,256]{1,0:T(8,128)(2,1)S(1)}, bf16[512,256]{1,0:T(8,128)(2,1)S(1)}, u32[]{:S(2)}, u32[]{:S(2)}) collective-permute-start(bf16[512,256]{1,0:T(8,128)(2,1)S(1)} %shard_map.117), channel_id=1, source_target_pairs={{0,6},{2,0},{4,2},{6,4},{8,14},{10,8},{12,10},{14,12},{16,22},{18,... | collective-permute-start | bytes 786440 | tf_op jit(solution)/shard_map/ppermute | solution.py:569
  28.7 0.2 collective-permute-start.9
  28.9 0.3 collective-permute-start.10
  29.2 0.6 %collective-permute-start.12 = (bf16[240,128]{1,0:T(8,128)(2,1)S(1)}, bf16[240,128]{1,0:T(8,128)(2,1)S(1)}, u32[]{:S(2)}, u32[]{:S(2)}) collective-permute-start(bf16[240,128]{1,0:T(8,128)(2,1)S(1)} %get-tuple-element.73), channel_id=1, source_target_pairs={{1,16},{3,18},{5,20},{7,22},{9,24},{11,26},{13,28},{15,30},{17,0},... | collective-permute-start | bytes 184328 | tf_op jit(solution)/shard_map/ppermute | solution.py:412
  29.8 4.7 %collective-permute-done.10.refs_1_ = bf16[240,128]{1,0:T(8,128)(2,1)S(1)} collective-permute-done((bf16[240,128]{1,0:T(8,128)(2,1)S(1)}, bf16[240,128]{1,0:T(8,128)(2,1)S(1)}, u32[]{:S(2)}, u32[]{:S(2)}) %collective-permute-start.10) | collective-permute-done | bytes 61472 | tf_op jit(solution)/shard_map/ppermute | solution.py:412
  34.5 0.0 collective-permute-done.12.refs_3_
  34.5 0.3 collective-permute-done.11.refs_2_
  34.8 0.0 collective-permute-done.9.refs_0_
  34.8 0.2 collective-permute-start.16
  35.1 1.4 %collective-permute-start.15 = (bf16[240,128]{1,0:T(8,128)(2,1)S(1)}, bf16[240,128]{1,0:T(8,128)(2,1)S(1)}, u32[]{:S(2)}, u32[]{:S(2)}) collective-permute-start(bf16[240,128]{1,0:T(8,128)(2,1)S(1)} %shard_map.119.refs_1_), channel_id=1, source_target_pairs={{0,17},{2,19},{4,21},{6,23},{8,25},{10,27},{12,29},{14,31},{16,1},... | collective-permute-start | bytes 184328 | tf_op jit(solution)/shard_map/ppermute | solution.py:412
  36.5 0.5 collective-permute-start.13
  37.0 0.9 %shard_map.118 = (bf16[1024,256]{1,0:T(8,128)(2,1)}, f32[8,128]{1,0:T(8,128)S(1)}) custom-call(f32[1024,256]{1,0:T(8,128)S(1)} %get-tuple-element.60.partial, bf16[512,256]{1,0:T(8,128)(2,1)S(1)} %collective-permute-done.8.incoming), custom_call_target="tpu_custom_call" | custom-call | bytes 8 | tf_op jit(solution)/shard_map/pallas_call | solution.py:37
  37.9 0.5 collective-permute-done.15.refs_3_
  38.4 0.6 %collective-permute-done.14.refs_2_ = bf16[240,128]{1,0:T(8,128)(2,1)S(1)} collective-permute-done((bf16[240,128]{1,0:T(8,128)(2,1)S(1)}, bf16[240,128]{1,0:T(8,128)(2,1)S(1)}, u32[]{:S(2)}, u32[]{:S(2)}) %collective-permute-start.14) | collective-permute-done | bytes 61472 | tf_op jit(solution)/shard_map/ppermute | solution.py:412
  39.0 0.1 shard_map.120.refs_0_
  39.0 1.7 %collective-permute-start.20 = (bf16[912,128]{1,0:T(8,128)(2,1)S(1)}, bf16[912,128]{1,0:T(8,128)(2,1)S(1)}, u32[]{:S(2)}, u32[]{:S(2)}) collective-permute-start(bf16[912,128]{1,0:T(8,128)(2,1)S(1)} %shard_map.120.refs_0_), channel_id=1, source_target_pairs={{1,2},{3,0},{5,6},{7,4},{9,10},{11,8},{13,14},{15,12},{17,18},{19,... | collective-permute-start | bytes 700424 | tf_op jit(solution)/shard_map/ppermute | solution.py:412
  40.7 0.1 collective-permute-start.19
  40.8 1.6 %collective-permute-start.17 = (bf16[912,128]{1,0:T(8,128)(2,1)S(1)}, bf16[912,128]{1,0:T(8,128)(2,1)S(1)}, u32[]{:S(2)}, u32[]{:S(2)}) collective-permute-start(bf16[912,128]{1,0:T(8,128)(2,1)S(1)} %shard_map.120.refs_0_), channel_id=1, source_target_pairs={{1,4},{3,6},{5,0},{7,2},{9,12},{11,14},{13,8},{15,10},{17,20},{19,... | collective-permute-start | bytes 700424 | tf_op jit(solution)/shard_map/ppermute | solution.py:412
  42.4 2.5 %collective-permute-done.20.refs_2_ = bf16[912,128]{1,0:T(8,128)(2,1)S(1)} collective-permute-done((bf16[912,128]{1,0:T(8,128)(2,1)S(1)}, bf16[912,128]{1,0:T(8,128)(2,1)S(1)}, u32[]{:S(2)}, u32[]{:S(2)}) %collective-permute-start.20) | collective-permute-done | bytes 233504 | tf_op jit(solution)/shard_map/ppermute | solution.py:412
  44.9 3.4 %collective-permute-done.19.refs_1_ = bf16[912,128]{1,0:T(8,128)(2,1)S(1)} collective-permute-done((bf16[912,128]{1,0:T(8,128)(2,1)S(1)}, bf16[912,128]{1,0:T(8,128)(2,1)S(1)}, u32[]{:S(2)}, u32[]{:S(2)}) %collective-permute-start.19) | collective-permute-done | bytes 233504 | tf_op jit(solution)/shard_map/ppermute | solution.py:412
  48.3 0.7 %collective-permute-done.17.refs_0_ = bf16[912,128]{1,0:T(8,128)(2,1)S(1)} collective-permute-done((bf16[912,128]{1,0:T(8,128)(2,1)S(1)}, bf16[912,128]{1,0:T(8,128)(2,1)S(1)}, u32[]{:S(2)}, u32[]{:S(2)}) %collective-permute-start.17) | collective-permute-done | bytes 233504 | tf_op jit(solution)/shard_map/ppermute | solution.py:412
  49.0 0.8 %collective-permute-done.22.refs_4_ = bf16[912,128]{1,0:T(8,128)(2,1)S(1)} collective-permute-done((bf16[912,128]{1,0:T(8,128)(2,1)S(1)}, bf16[912,128]{1,0:T(8,128)(2,1)S(1)}, u32[]{:S(2)}, u32[]{:S(2)}) %collective-permute-start.22) | collective-permute-done | bytes 233504 | tf_op jit(solution)/shard_map/ppermute | solution.py:405
  49.7 1.2 %shard_map.121 = (f32[768,512]{1,0:T(8,128)}, f32[256,256]{1,0:T(8,128)}, f32[8,128]{1,0:T(8,128)S(1)}) custom-call(bf16[912,128]{1,0:T(8,128)(2,1)S(1)} %shard_map.120.refs_0_, bf16[912,128]{1,0:T(8,128)(2,1)S(1)} %collective-permute-done.19.refs_1_, bf16[912,128]{1,0:T(8,128)(2,1)S(1)} %collective-permute-done.20.refs_2_, ...), custom_call_target="tpu_custom_call" | custom-call | bytes 8 | tf_op jit(solution)/shard_map/pallas_call | solution.py:37
  51.0 0.9 %shard_map.122 = (f32[768,512]{1,0:T(8,128)}, f32[256,256]{1,0:T(8,128)}, f32[1,512]{1,0:T(1,128)}, f32[1,256]{1,0:T(1,128)}) custom-call(bf16[912,128]{1,0:T(8,128)(2,1)S(1)} %collective-permute-done.17.refs_0_, bf16[912,128]{1,0:T(8,128)(2,1)S(1)} %collective-permute-done.18.refs_1_, ...), custom_call_target="tpu_custom_call", output_to_operand_aliasing={{0}: (3, {}), {1}: (4, {})} | custom-call | bytes 8 | tf_op jit(solution)/shard_map/pallas_call | solution.py:37
  (19 shorter events, 0.2 us)
Async XLA Ops:
  1.6 13.3 %collective-permute-start = (bf16[512,256]{1,0:T(8,128)(2,1)S(1)}, bf16[512,256]{1,0:T(8,128)(2,1)S(1)}, u32[]{:S(2)}, u32[]{:S(2)}) collective-permute-start(bf16[512,256]{1,0:T(8,128)(2,1)S(1)} %slice_bitcast_fusion), channel_id=1, source_target_pairs={{0,2},{2,4},{4,6},{6,8},{8,10},{10,12},{12,14},{14,16},{16,18},{18... | collective-permute-start | bytes 786440 | tf_op jit(solution)/shard_map/ppermute | solution.py:515
  4.6 0.7 %copy-start = (f32[512]{0:T(512)S(1)}, f32[512]{0:T(512)}, u32[]{:S(2)}) copy-start(f32[512]{0:T(512)} %param.8) | copy-start | bytes 6148
  16.3 2.8 %collective-permute-start.1 = (bf16[912,128]{1,0:T(8,128)(2,1)S(1)}, bf16[912,128]{1,0:T(8,128)(2,1)S(1)}, u32[]{:S(2)}, u32[]{:S(2)}) collective-permute-start(bf16[912,128]{1,0:T(8,128)(2,1)S(1)} %get-tuple-element.58), channel_id=1, source_target_pairs={{0,1},{1,0},{2,3},{3,2},{4,5},{5,4},{6,7},{7,6},{8,9},{9,8},{10,11... | collective-permute-start | bytes 700424 | tf_op jit(solution)/shard_map/ppermute | solution.py:405
  16.4 2.8 %collective-permute-start.3 = (bf16[912,128]{1,0:T(8,128)(2,1)S(1)}, bf16[912,128]{1,0:T(8,128)(2,1)S(1)}, u32[]{:S(2)}, u32[]{:S(2)}) collective-permute-start(bf16[912,128]{1,0:T(8,128)(2,1)S(1)} %get-tuple-element.63), channel_id=1, source_target_pairs={{0,1},{1,0},{2,3},{3,2},{4,5},{5,4},{6,7},{7,6},{8,9},{9,8},{10,11... | collective-permute-start | bytes 700424 | tf_op jit(solution)/shard_map/ppermute | solution.py:405
  16.9 2.5 %collective-permute-start.5 = (bf16[912,128]{1,0:T(8,128)(2,1)S(1)}, bf16[912,128]{1,0:T(8,128)(2,1)S(1)}, u32[]{:S(2)}, u32[]{:S(2)}) collective-permute-start(bf16[912,128]{1,0:T(8,128)(2,1)S(1)} %get-tuple-element.67), channel_id=1, source_target_pairs={{0,1},{1,0},{2,3},{3,2},{4,5},{5,4},{6,7},{7,6},{8,9},{9,8},{10,11... | collective-permute-start | bytes 700424 | tf_op jit(solution)/shard_map/ppermute | solution.py:405
  17.3 8.7 %collective-permute-start.2 = (bf16[512,256]{1,0:T(8,128)(2,1)S(1)}, bf16[512,256]{1,0:T(8,128)(2,1)S(1)}, u32[]{:S(2)}, u32[]{:S(2)}) collective-permute-start(bf16[512,256]{1,0:T(8,128)(2,1)S(1)} %shard_map.113.refs_3_.refs_0_), channel_id=1, source_target_pairs={{0,24},{1,25},{2,3},{3,2},{4,5},{5,4},{6,7},{7,6},{8,0},{9,1},{10,... | collective-permute-start | bytes 786440 | tf_op jit(solution)/shard_map/ppermute | solution.py:549
  19.0 0.7 %copy-start.1 = (f32[256]{0:T(256)S(1)}, f32[256]{0:T(256)}, u32[]{:S(2)}) copy-start(f32[256]{0:T(256)} %param.10) | copy-start | bytes 3076
  19.1 4.8 %collective-permute-start.7 = (bf16[912,128]{1,0:T(8,128)(2,1)S(1)}, bf16[912,128]{1,0:T(8,128)(2,1)S(1)}, u32[]{:S(2)}, u32[]{:S(2)}) collective-permute-start(bf16[912,128]{1,0:T(8,128)(2,1)S(1)} %shard_map.111.refs_9_), channel_id=1, source_target_pairs={{0,5},{2,7},{4,1},{6,3},{8,13},{10,15},{12,9},{14,11},{16,21},{18,... | collective-permute-start | bytes 700424 | tf_op jit(solution)/shard_map/ppermute | solution.py:412
  19.3 4.6 %collective-permute-start.4 = (bf16[912,128]{1,0:T(8,128)(2,1)S(1)}, bf16[912,128]{1,0:T(8,128)(2,1)S(1)}, u32[]{:S(2)}, u32[]{:S(2)}) collective-permute-start(bf16[912,128]{1,0:T(8,128)(2,1)S(1)} %get-tuple-element.65), channel_id=1, source_target_pairs={{0,7},{2,5},{4,3},{6,1},{8,15},{10,13},{12,11},{14,9},{16,23},{18,... | collective-permute-start | bytes 700424 | tf_op jit(solution)/shard_map/ppermute | solution.py:412
  19.4 6.0 %collective-permute-start.6 = (bf16[912,128]{1,0:T(8,128)(2,1)S(1)}, bf16[912,128]{1,0:T(8,128)(2,1)S(1)}, u32[]{:S(2)}, u32[]{:S(2)}) collective-permute-start(bf16[912,128]{1,0:T(8,128)(2,1)S(1)} %shard_map.115), channel_id=1, source_target_pairs={{0,3},{2,1},{4,7},{6,5},{8,11},{10,9},{12,15},{14,13},{16,19},{18,... | collective-permute-start | bytes 700424 | tf_op jit(solution)/shard_map/ppermute | solution.py:412
  26.1 10.9 %collective-permute-start.8 = (bf16[512,256]{1,0:T(8,128)(2,1)S(1)}, bf16[512,256]{1,0:T(8,128)(2,1)S(1)}, u32[]{:S(2)}, u32[]{:S(2)}) collective-permute-start(bf16[512,256]{1,0:T(8,128)(2,1)S(1)} %shard_map.117), channel_id=1, source_target_pairs={{0,6},{2,0},{4,2},{6,4},{8,14},{10,8},{12,10},{14,12},{16,22},{18,... | collective-permute-start | bytes 786440 | tf_op jit(solution)/shard_map/ppermute | solution.py:569
  28.7 6.1 %collective-permute-start.9 = (f32[232,128]{1,0:T(8,128)S(1)}, f32[232,128]{1,0:T(8,128)S(1)}, u32[]{:S(2)}, u32[]{:S(2)}) collective-permute-start(f32[232,128]{1,0:T(8,128)S(1)} %get-tuple-element.71), channel_id=1, source_target_pairs={{0,1},{1,0},{2,3},{3,2},{4,5},{5,4},{6,7},{7,6},{8,9},{9,8},{10,11... | collective-permute-start | bytes 356360 | tf_op jit(solution)/shard_map/ppermute | solution.py:405
  28.9 5.7 %collective-permute-start.10 = (bf16[240,128]{1,0:T(8,128)(2,1)S(1)}, bf16[240,128]{1,0:T(8,128)(2,1)S(1)}, u32[]{:S(2)}, u32[]{:S(2)}) collective-permute-start(bf16[240,128]{1,0:T(8,128)(2,1)S(1)} %get-tuple-element.72), channel_id=1, source_target_pairs={{1,24},{3,26},{5,28},{7,30},{9,16},{11,18},{13,20},{15,22},{17,8},... | collective-permute-start | bytes 184328 | tf_op jit(solution)/shard_map/ppermute | solution.py:412
  29.2 5.3 %collective-permute-start.12 = (bf16[240,128]{1,0:T(8,128)(2,1)S(1)}, bf16[240,128]{1,0:T(8,128)(2,1)S(1)}, u32[]{:S(2)}, u32[]{:S(2)}) collective-permute-start(bf16[240,128]{1,0:T(8,128)(2,1)S(1)} %get-tuple-element.73), channel_id=1, source_target_pairs={{1,16},{3,18},{5,20},{7,22},{9,24},{11,26},{13,28},{15,30},{17,0},... | collective-permute-start | bytes 184328 | tf_op jit(solution)/shard_map/ppermute | solution.py:412
  29.8 5.0 %collective-permute-start.11 = (bf16[240,128]{1,0:T(8,128)(2,1)S(1)}, bf16[240,128]{1,0:T(8,128)(2,1)S(1)}, u32[]{:S(2)}, u32[]{:S(2)}) collective-permute-start(bf16[240,128]{1,0:T(8,128)(2,1)S(1)} %get-tuple-element.69.refs_2_), channel_id=1, source_target_pairs={{1,8},{3,10},{5,12},{7,14},{9,0},{11,2},{13,4},{15,6},{17,24},{19,... | collective-permute-start | bytes 184328 | tf_op jit(solution)/shard_map/ppermute | solution.py:412
  34.8 3.1 %collective-permute-start.16 = (bf16[240,128]{1,0:T(8,128)(2,1)S(1)}, bf16[240,128]{1,0:T(8,128)(2,1)S(1)}, u32[]{:S(2)}, u32[]{:S(2)}) collective-permute-start(bf16[240,128]{1,0:T(8,128)(2,1)S(1)} %shard_map.119.refs_1_), channel_id=1, source_target_pairs={{0,25},{2,27},{4,29},{6,31},{8,17},{10,19},{12,21},{14,23},{16,9},... | collective-permute-start | bytes 184328 | tf_op jit(solution)/shard_map/ppermute | solution.py:412
  35.1 3.3 %collective-permute-start.15 = (bf16[240,128]{1,0:T(8,128)(2,1)S(1)}, bf16[240,128]{1,0:T(8,128)(2,1)S(1)}, u32[]{:S(2)}, u32[]{:S(2)}) collective-permute-start(bf16[240,128]{1,0:T(8,128)(2,1)S(1)} %shard_map.119.refs_1_), channel_id=1, source_target_pairs={{0,17},{2,19},{4,21},{6,23},{8,25},{10,27},{12,29},{14,31},{16,1},... | collective-permute-start | bytes 184328 | tf_op jit(solution)/shard_map/ppermute | solution.py:412
  36.5 2.4 %collective-permute-start.14 = (bf16[240,128]{1,0:T(8,128)(2,1)S(1)}, bf16[240,128]{1,0:T(8,128)(2,1)S(1)}, u32[]{:S(2)}, u32[]{:S(2)}) collective-permute-start(bf16[240,128]{1,0:T(8,128)(2,1)S(1)} %shard_map.119.refs_1_), channel_id=1, source_target_pairs={{0,9},{2,11},{4,13},{6,15},{8,1},{10,3},{12,5},{14,7},{16,25},{18,... | collective-permute-start | bytes 184328 | tf_op jit(solution)/shard_map/ppermute | solution.py:412
  36.5 2.4 %collective-permute-start.13 = (bf16[240,128]{1,0:T(8,128)(2,1)S(1)}, bf16[240,128]{1,0:T(8,128)(2,1)S(1)}, u32[]{:S(2)}, u32[]{:S(2)}) collective-permute-start(bf16[240,128]{1,0:T(8,128)(2,1)S(1)} %shard_map.119.refs_1_), channel_id=1, source_target_pairs={{0,1},{1,0},{2,3},{3,2},{4,5},{5,4},{6,7},{7,6},{8,9},{9,8},{10,11... | collective-permute-start | bytes 184328 | tf_op jit(solution)/shard_map/ppermute | solution.py:405
  39.0 5.9 %collective-permute-start.20 = (bf16[912,128]{1,0:T(8,128)(2,1)S(1)}, bf16[912,128]{1,0:T(8,128)(2,1)S(1)}, u32[]{:S(2)}, u32[]{:S(2)}) collective-permute-start(bf16[912,128]{1,0:T(8,128)(2,1)S(1)} %shard_map.120.refs_0_), channel_id=1, source_target_pairs={{1,2},{3,0},{5,6},{7,4},{9,10},{11,8},{13,14},{15,12},{17,18},{19,... | collective-permute-start | bytes 700424 | tf_op jit(solution)/shard_map/ppermute | solution.py:412
  40.7 7.5 %collective-permute-start.19 = (bf16[912,128]{1,0:T(8,128)(2,1)S(1)}, bf16[912,128]{1,0:T(8,128)(2,1)S(1)}, u32[]{:S(2)}, u32[]{:S(2)}) collective-permute-start(bf16[912,128]{1,0:T(8,128)(2,1)S(1)} %shard_map.120.refs_0_), channel_id=1, source_target_pairs={{1,6},{3,4},{5,2},{7,0},{9,14},{11,12},{13,10},{15,8},{17,22},{19,... | collective-permute-start | bytes 700424 | tf_op jit(solution)/shard_map/ppermute | solution.py:412
  40.8 8.2 %collective-permute-start.17 = (bf16[912,128]{1,0:T(8,128)(2,1)S(1)}, bf16[912,128]{1,0:T(8,128)(2,1)S(1)}, u32[]{:S(2)}, u32[]{:S(2)}) collective-permute-start(bf16[912,128]{1,0:T(8,128)(2,1)S(1)} %shard_map.120.refs_0_), channel_id=1, source_target_pairs={{1,4},{3,6},{5,0},{7,2},{9,12},{11,14},{13,8},{15,10},{17,20},{19,... | collective-permute-start | bytes 700424 | tf_op jit(solution)/shard_map/ppermute | solution.py:412
  42.4 6.6 %collective-permute-start.21 = (bf16[912,128]{1,0:T(8,128)(2,1)S(1)}, bf16[912,128]{1,0:T(8,128)(2,1)S(1)}, u32[]{:S(2)}, u32[]{:S(2)}) collective-permute-start(bf16[912,128]{1,0:T(8,128)(2,1)S(1)} %shard_map.120.refs_0_), channel_id=1, source_target_pairs={{0,1},{1,0},{2,3},{3,2},{4,5},{5,4},{6,7},{7,6},{8,9},{9,8},{10,11... | collective-permute-start | bytes 700424 | tf_op jit(solution)/shard_map/ppermute | solution.py:405
  44.9 4.1 %collective-permute-start.23 = (bf16[912,128]{1,0:T(8,128)(2,1)S(1)}, bf16[912,128]{1,0:T(8,128)(2,1)S(1)}, u32[]{:S(2)}, u32[]{:S(2)}) collective-permute-start(bf16[912,128]{1,0:T(8,128)(2,1)S(1)} %collective-permute-done.20.refs_2_), channel_id=1, source_target_pairs={{0,1},{1,0},{2,3},{3,2},{4,5},{5,4},{6,7},{7,6},{8,9},{9,8},{10,11... | collective-permute-start | bytes 700424 | tf_op jit(solution)/shard_map/ppermute | solution.py:405
  48.3 1.5 %collective-permute-start.22 = (bf16[912,128]{1,0:T(8,128)(2,1)S(1)}, bf16[912,128]{1,0:T(8,128)(2,1)S(1)}, u32[]{:S(2)}, u32[]{:S(2)}) collective-permute-start(bf16[912,128]{1,0:T(8,128)(2,1)S(1)} %collective-permute-done.19.refs_1_), channel_id=1, source_target_pairs={{0,1},{1,0},{2,3},{3,2},{4,5},{5,4},{6,7},{7,6},{8,9},{9,8},{10,11... | collective-permute-start | bytes 700424 | tf_op jit(solution)/shard_map/ppermute | solution.py:405
  49.0 2.0 %collective-permute-start.18 = (bf16[912,128]{1,0:T(8,128)(2,1)S(1)}, bf16[912,128]{1,0:T(8,128)(2,1)S(1)}, u32[]{:S(2)}, u32[]{:S(2)}) collective-permute-start(bf16[912,128]{1,0:T(8,128)(2,1)S(1)} %collective-permute-done.17.refs_0_), channel_id=1, source_target_pairs={{0,1},{1,0},{2,3},{3,2},{4,5},{5,4},{6,7},{7,6},{8,9},{9,8},{10,11... | collective-permute-start | bytes 700424 | tf_op jit(solution)/shard_map/ppermute | solution.py:405

commit v3 on v2

--- a/solution.py
+++ b/solution.py
@@ -41,7 +41,7 @@
         out_specs=outs,
         scratch_shapes=list(scratch),
         input_output_aliases=alias or {},
-        cost_estimate=pl.CostEstimate(flops=0, bytes_accessed=8, transcendentals=0),
+        cost_estimate=pl.CostEstimate(flops=flops, bytes_accessed=8, transcendentals=0),
         compiler_params=pltpu.CompilerParams(vmem_limit_bytes=(8 if count_of_chips() <= 16 else 40) * MIB),
     )(*placed, *after)
 
@@ -348,6 +348,10 @@
             out[radix * rows :, :] = block[rows:]
 
 
+def copy_kernel(source, out):
+    out[...] = source[...]
+
+
 def spread_kernel(steps, level, taker, pieces, *refs):
     count = len(steps)
     ends = steps[-1] != 0 and count == 1
@@ -451,6 +455,7 @@
         functools.partial(finish_kernel, scale),
         [held(BF16, rows + BIAS_ROWS, LANES)],
         (keep, *received),
+        flops=3000000000,
         after=ready if len(levels) == 1 else (),
     )
     if len(levels) == 1:
@@ -482,7 +487,12 @@
         ]
 
     early, last = [0, *turn[:-1]], turn[-1]
-    forwarded = [given] + [swapped(parts[k]) for k in early[1:]]
+    forwarded = [given]
+    for k in early[1:]:
+        message = parts[k]
+        if k == turn[0]:
+            (message,) = call(copy_kernel, [held(BF16, *message.shape)], (message,), after=fill(4, ()))
+        forwarded.append(swapped(message))
     conv, proj, bias = call(
         functools.partial(spread_kernel, early, levels[0], taker, pieces),
         whole + [held(F32, SUBLANES, LANES)],
@@ -523,7 +533,6 @@
             held(F32, SUBLANES, wide + channels),
         ],
         (signal[0], conv_weight, conv_bias.reshape(1, -1), out_weight, cotangent[0]),
-        flops=3 * rows * channels * channels * 8,
         scratch=[pltpu.SemaphoreType.DMA((4,))],
         far=(0, 1, 3, 4),
     )
@@ -535,7 +544,6 @@
         (
             history, x, weight, cot, preact, dmixed, conv, proj, bias,
         ),
-        flops=2 * rows * channels * channels * 8,
         scratch=[pltpu.VMEM((SPAN, channels), BF16)]
         + [pltpu.VMEM((chips * h, w), F32) for h, w in zip(heights, widths)],
     )
@@ -568,14 +576,12 @@
             )
             results["incoming"] = lax.ppermute(onward, "tm", plane_pairs())
             return ()
+        if stage == 3:
+            return (results["incoming"],)
         results["grad_signal"], token = call(
             join_kernel,
             [shape(BF16, rows, channels), TOKEN],
-            (
-                results["partial"],
-                results["incoming"],
-            ),
-            after=after,
+            (results["partial"], results["incoming"]),
         )
         return (token,)
 

time: 52 us -> 49.9 us (0.960)
  waiting for transfers between devices: 24.2 us -> 20.5 us
  starting transfers between devices: 14.8 us -> 16.7 us
    ppermute x12, waiting for transfers between devices: 16.6 us -> 11.8 us  [crossed(): return lax.ppermute(array, BOTH, pairs)]
    ppermute x9, starting transfers between devices: 1.33 us -> 3.74 us  [swapped(): return lax.ppermute(array, BOTH, [(i, i ^ 1) for i in range(2 * chips)])]
    ppermute x1, starting transfers between devices: 2.63 us -> 0.79 us  [fill(): results['incoming'] = lax.ppermute(onward, 'tm', plane_pairs())]
    ppermute x9, waiting for transfers between devices: 0.78 us -> 1.78 us  [swapped(): return lax.ppermute(array, BOTH, [(i, i ^ 1) for i in range(2 * chips)])]
    ppermute x12, starting transfers between devices: 6.18 us -> 6.81 us  [crossed(): return lax.ppermute(array, BOTH, pairs)]
    ppermute x1, starting transfers between devices: 1.7 us -> 2.33 us  [fill(): results['relayed'] = lax.ppermute(results['back'], BOTH, relay_pairs())]
    ppermute x1, waiting for transfers between devices: 0.01 us -> 0.57 us  [fill(): results['incoming'] = lax.ppermute(onward, 'tm', plane_pairs())]
    pallas_call x14 -> x15, Pallas kernels: 10.1 us -> 10.1 us  [call(): pl.pallas_call(inner, out_shape=out_shape, in_specs=ins + [ANY] * len(aft...]
  transfers between devices with their start and end apart: 24 -> 24, of which waited for: 12 -> 15; matrix products, arithmetic and copies ran while one was open for 0% -> 0% of each run, Pallas kernels for 15% -> 16%
where the time goes in v3:
time: 49.9 us; the launch traced here: 49.7 us
  waiting for transfers between devices  20.5 us (41%)
  starting transfers between devices  16.7 us (33%)
  Pallas kernels  10.1 us (20%)
  local copies, waits for them, and re-layouts  1.66 us (3%)
  between operations  0.78 us (2%)
    ppermute x12, waiting for transfers between devices, crossed(): return lax.ppermute(array, BOTH, pairs)  11.8 us
    pallas_call x15, Pallas kernels, call(): pl.pallas_call(inner, out_shape=out_shape, in_specs=ins + [ANY] * len(aft...  10.1 us
    ppermute x12, starting transfers between devices, crossed(): return lax.ppermute(array, BOTH, pairs)  6.81 us
    ppermute x1, waiting for transfers between devices, local(): lax.ppermute(signal[0, late:], 'tm', [(i, (i + 1) % size) for i in range(...  6.28 us
    ppermute x9, starting transfers between devices, swapped(): return lax.ppermute(array, BOTH, [(i, i ^ 1) for i in range(2 * chips)])  3.74 us
    ppermute x1, starting transfers between devices, local(): lax.ppermute(signal[0, late:], 'tm', [(i, (i + 1) % size) for i in range(...  2.99 us
    ppermute x1, starting transfers between devices, fill(): results['relayed'] = lax.ppermute(results['back'], BOTH, relay_pairs())  2.33 us
    ppermute x9, waiting for transfers between devices, swapped(): return lax.ppermute(array, BOTH, [(i, i ^ 1) for i in range(2 * chips)])  1.78 us
  transfers between devices with their start and end apart: 24, of which 15 were waited for; matrix products, arithmetic and copies ran while one was open for 0% of the time, Pallas kernels for 16%

profile of v3, /device:TPU:0, one launch (start us, length us, event | category | flops | bytes accessed | tf_op | source)
XLA Modules:
  0.0 49.7 jit_solution(7827301627720669614)
XLA Ops:
  0.6 1.0 %slice_bitcast_fusion = bf16[512,256]{1,0:T(8,128)(2,1)S(1)} fusion(bf16[1,1024,256]{2,1,0:T(8,128)(2,1)} %param.6), kind=kLoop, calls=%fused_computation | loop fusion | bytes 524288 | tf_op jit(solution)/shard_map/squeeze | solution.py:525
  1.6 3.0 %collective-permute-start = (bf16[512,256]{1,0:T(8,128)(2,1)S(1)}, bf16[512,256]{1,0:T(8,128)(2,1)S(1)}, u32[]{:S(2)}, u32[]{:S(2)}) collective-permute-start(bf16[512,256]{1,0:T(8,128)(2,1)S(1)} %slice_bitcast_fusion), channel_id=1, source_target_pairs={{0,2},{2,4},{4,6},{6,8},{8,10},{10,12},{12,14},{14,16},{16,18},{18... | collective-permute-start | bytes 786440 | tf_op jit(solution)/shard_map/ppermute | solution.py:525
  4.6 0.7 %copy-done = f32[512]{0:T(512)S(1)} copy-done((f32[512]{0:T(512)S(1)}, f32[512]{0:T(512)}, u32[]{:S(2)}) %copy-start) | copy-done | bytes 2072
  5.3 3.3 %shard_map.109 = (bf16[1024,256]{1,0:T(8,128)(2,1)S(1)}, bf16[768,512]{1,0:T(8,128)(2,1)S(1)}, bf16[256,256]{1,0:T(8,128)(2,1)S(1)}, bf16[1024,256]{1,0:T(8,128)...) custom-call(bf16[1024,256]{1,0:T(8,128)(2,1)} %bitcast.12, ...), custom_call_target="tpu_custom_call" | custom-call | bytes 8 | tf_op jit(solution)/shard_map/pallas_call | solution.py:37
  8.6 6.3 %collective-permute-done.history = bf16[512,256]{1,0:T(8,128)(2,1)S(1)} collective-permute-done((bf16[512,256]{1,0:T(8,128)(2,1)S(1)}, bf16[512,256]{1,0:T(8,128)(2,1)S(1)}, u32[]{:S(2)}, u32[]{:S(2)}) %collective-permute-start) | collective-permute-done | bytes 262176 | tf_op jit(solution)/shard_map/ppermute | solution.py:525
  14.9 1.4 %shard_map.110 = (bf16[512,256]{1,0:T(8,128)(2,1)S(1)}, bf16[512,512]{1,0:T(8,128)(2,1)S(1)}, f32[904,128]{1,0:T(8,128)S(1)}, f32[904,128]{1,0:T(8,128)S(1)}, f3...) custom-call(bf16[512,256]{1,0:T(8,128)(2,1)S(1)} %collective-permute, ...), custom_call_target="tpu_custom_call" | custom-call | bytes 8 | tf_op jit(solution)/shard_map/pallas_call | solution.py:37
  16.3 0.1 collective-permute-start.1
  16.3 0.5 collective-permute-start.3
  16.8 0.1 collective-permute-start.5
  16.9 0.4 shard_map.113.refs_3_.refs_0_
  17.3 0.5 %collective-permute-done.1.received = bf16[912,128]{1,0:T(8,128)(2,1)S(1)} collective-permute-done((bf16[912,128]{1,0:T(8,128)(2,1)S(1)}, bf16[912,128]{1,0:T(8,128)(2,1)S(1)}, u32[]{:S(2)}, u32[]{:S(2)}) %collective-permute-start.1) | collective-permute-done | bytes 233504 | tf_op jit(solution)/shard_map/ppermute | solution.py:409
  17.8 0.1 shard_map.111.refs_9_
  17.9 0.1 collective-permute-start.7
  18.0 0.2 collective-permute-done.3.refs_2_
  18.2 0.1 shard_map.114
  18.3 0.1 collective-permute-start.4
  18.3 0.2 collective-permute-done.5.received
  18.5 0.1 shard_map.115
  18.6 0.1 collective-permute-start.6
  18.6 2.3 %collective-permute-start.2 = (bf16[512,256]{1,0:T(8,128)(2,1)S(1)}, bf16[512,256]{1,0:T(8,128)(2,1)S(1)}, u32[]{:S(2)}, u32[]{:S(2)}) collective-permute-start(bf16[512,256]{1,0:T(8,128)(2,1)S(1)} %shard_map.113.refs_3_.refs_0_), channel_id=1, source_target_pairs={{0,24},{1,25},{2,3},{3,2},{4,5},{5,4},{6,7},{7,6},{8,0},{9,1},{10,... | collective-permute-start | bytes 786440 | tf_op jit(solution)/shard_map/ppermute | solution.py:557
  21.0 1.6 %shard_map.112 = (bf16[1024,256]{1,0:T(8,128)(2,1)}, f32[1024,256]{1,0:T(8,128)S(1)}, f32[8,128]{1,0:T(8,128)S(1)}) custom-call(bf16[1024,256]{1,0:T(8,128)(2,1)S(1)} %get-tuple-element.44.signal.refs_0_, bf16[768,512]{1,0:T(8,128)(2,1)S(1)} %get-tuple-element.45.weight.refs_1_, bf16[256,256]{1,0:T(8,128)(2,1)S(1)} %get-tuple-element.46.refs_2_, ...), custom_call_target="tpu_custom_call" | custom-call | bytes 8 | tf_op jit(solution)/shard_map/pallas_call | solution.py:37
  22.6 1.3 %collective-permute-done.7.refs_3_ = bf16[912,128]{1,0:T(8,128)(2,1)S(1)} collective-permute-done((bf16[912,128]{1,0:T(8,128)(2,1)S(1)}, bf16[912,128]{1,0:T(8,128)(2,1)S(1)}, u32[]{:S(2)}, u32[]{:S(2)}) %collective-permute-start.7) | collective-permute-done | bytes 233504 | tf_op jit(solution)/shard_map/ppermute | solution.py:416
  23.9 0.5 %collective-permute-done.6.refs_2_ = bf16[912,128]{1,0:T(8,128)(2,1)S(1)} collective-permute-done((bf16[912,128]{1,0:T(8,128)(2,1)S(1)}, bf16[912,128]{1,0:T(8,128)(2,1)S(1)}, u32[]{:S(2)}, u32[]{:S(2)}) %collective-permute-start.6) | collective-permute-done | bytes 233504 | tf_op jit(solution)/shard_map/ppermute | solution.py:416
  24.4 0.1 shard_map.116
  24.5 2.1 %collective-permute-start.9 = (f32[232,128]{1,0:T(8,128)S(1)}, f32[232,128]{1,0:T(8,128)S(1)}, u32[]{:S(2)}, u32[]{:S(2)}) collective-permute-start(f32[232,128]{1,0:T(8,128)S(1)} %get-tuple-element.71), channel_id=1, source_target_pairs={{0,1},{1,0},{2,3},{3,2},{4,5},{5,4},{6,7},{7,6},{8,9},{9,8},{10,11... | collective-permute-start | bytes 356360 | tf_op jit(solution)/shard_map/ppermute | solution.py:409
  26.6 0.1 collective-permute-start.10
  26.6 2.3 %collective-permute-start.12 = (bf16[240,128]{1,0:T(8,128)(2,1)S(1)}, bf16[240,128]{1,0:T(8,128)(2,1)S(1)}, u32[]{:S(2)}, u32[]{:S(2)}) collective-permute-start(bf16[240,128]{1,0:T(8,128)(2,1)S(1)} %get-tuple-element.73), channel_id=1, source_target_pairs={{1,16},{3,18},{5,20},{7,22},{9,24},{11,26},{13,28},{15,30},{17,0},... | collective-permute-start | bytes 184328 | tf_op jit(solution)/shard_map/ppermute | solution.py:416
  29.0 0.8 %collective-permute-start.8 = (bf16[512,256]{1,0:T(8,128)(2,1)S(1)}, bf16[512,256]{1,0:T(8,128)(2,1)S(1)}, u32[]{:S(2)}, u32[]{:S(2)}) collective-permute-start(bf16[512,256]{1,0:T(8,128)(2,1)S(1)} %shard_map.117), channel_id=1, source_target_pairs={{0,6},{2,0},{4,2},{6,4},{8,14},{10,8},{12,10},{14,12},{16,22},{18,... | collective-permute-start | bytes 786440 | tf_op jit(solution)/shard_map/ppermute | solution.py:577
  29.8 2.2 %collective-permute-done.10.refs_1_ = bf16[240,128]{1,0:T(8,128)(2,1)S(1)} collective-permute-done((bf16[240,128]{1,0:T(8,128)(2,1)S(1)}, bf16[240,128]{1,0:T(8,128)(2,1)S(1)}, u32[]{:S(2)}, u32[]{:S(2)}) %collective-permute-start.10) | collective-permute-done | bytes 61472 | tf_op jit(solution)/shard_map/ppermute | solution.py:416
  32.0 0.6 %collective-permute-done.11.refs_2_ = bf16[240,128]{1,0:T(8,128)(2,1)S(1)} collective-permute-done((bf16[240,128]{1,0:T(8,128)(2,1)S(1)}, bf16[240,128]{1,0:T(8,128)(2,1)S(1)}, u32[]{:S(2)}, u32[]{:S(2)}) %collective-permute-start.11) | collective-permute-done | bytes 61472 | tf_op jit(solution)/shard_map/ppermute | solution.py:416
  32.7 0.1 collective-permute-start.16
  32.8 1.5 %collective-permute-start.15 = (bf16[240,128]{1,0:T(8,128)(2,1)S(1)}, bf16[240,128]{1,0:T(8,128)(2,1)S(1)}, u32[]{:S(2)}, u32[]{:S(2)}) collective-permute-start(bf16[240,128]{1,0:T(8,128)(2,1)S(1)} %shard_map.119.refs_1_), channel_id=1, source_target_pairs={{0,17},{2,19},{4,21},{6,23},{8,25},{10,27},{12,29},{14,31},{16,1},... | collective-permute-start | bytes 184328 | tf_op jit(solution)/shard_map/ppermute | solution.py:416
  34.3 0.5 %collective-permute-start.13 = (bf16[240,128]{1,0:T(8,128)(2,1)S(1)}, bf16[240,128]{1,0:T(8,128)(2,1)S(1)}, u32[]{:S(2)}, u32[]{:S(2)}) collective-permute-start(bf16[240,128]{1,0:T(8,128)(2,1)S(1)} %shard_map.119.refs_1_), channel_id=1, source_target_pairs={{0,1},{1,0},{2,3},{3,2},{4,5},{5,4},{6,7},{7,6},{8,9},{9,8},{10,11... | collective-permute-start | bytes 184328 | tf_op jit(solution)/shard_map/ppermute | solution.py:409
  34.8 1.4 %collective-permute-done.15.refs_3_ = bf16[240,128]{1,0:T(8,128)(2,1)S(1)} collective-permute-done((bf16[240,128]{1,0:T(8,128)(2,1)S(1)}, bf16[240,128]{1,0:T(8,128)(2,1)S(1)}, u32[]{:S(2)}, u32[]{:S(2)}) %collective-permute-start.15) | collective-permute-done | bytes 61472 | tf_op jit(solution)/shard_map/ppermute | solution.py:416
  36.1 0.6 %collective-permute-done.14.refs_2_ = bf16[240,128]{1,0:T(8,128)(2,1)S(1)} collective-permute-done((bf16[240,128]{1,0:T(8,128)(2,1)S(1)}, bf16[240,128]{1,0:T(8,128)(2,1)S(1)}, u32[]{:S(2)}, u32[]{:S(2)}) %collective-permute-start.14) | collective-permute-done | bytes 61472 | tf_op jit(solution)/shard_map/ppermute | solution.py:416
  36.7 0.6 %collective-permute-done.8.incoming.refs_5_ = bf16[512,256]{1,0:T(8,128)(2,1)S(1)} collective-permute-done((bf16[512,256]{1,0:T(8,128)(2,1)S(1)}, bf16[512,256]{1,0:T(8,128)(2,1)S(1)}, u32[]{:S(2)}, u32[]{:S(2)}) %collective-permute-start.8) | collective-permute-done | bytes 262176 | tf_op jit(solution)/shard_map/ppermute | solution.py:577
  37.3 1.1 %collective-permute-start.20 = (bf16[912,128]{1,0:T(8,128)(2,1)S(1)}, bf16[912,128]{1,0:T(8,128)(2,1)S(1)}, u32[]{:S(2)}, u32[]{:S(2)}) collective-permute-start(bf16[912,128]{1,0:T(8,128)(2,1)S(1)} %shard_map.120.refs_0_), channel_id=1, source_target_pairs={{1,2},{3,0},{5,6},{7,4},{9,10},{11,8},{13,14},{15,12},{17,18},{19,... | collective-permute-start | bytes 700424 | tf_op jit(solution)/shard_map/ppermute | solution.py:416
  38.4 0.3 collective-permute-start.19
  38.7 1.3 %collective-permute-start.17 = (bf16[912,128]{1,0:T(8,128)(2,1)S(1)}, bf16[912,128]{1,0:T(8,128)(2,1)S(1)}, u32[]{:S(2)}, u32[]{:S(2)}) collective-permute-start(bf16[912,128]{1,0:T(8,128)(2,1)S(1)} %shard_map.120.refs_0_), channel_id=1, source_target_pairs={{1,4},{3,6},{5,0},{7,2},{9,12},{11,14},{13,8},{15,10},{17,20},{19,... | collective-permute-start | bytes 700424 | tf_op jit(solution)/shard_map/ppermute | solution.py:416
  40.1 0.5 collective-permute-start.21
  40.5 0.9 %shard_map.118 = (bf16[1024,256]{1,0:T(8,128)(2,1)}, f32[8,128]{1,0:T(8,128)S(1)}) custom-call(f32[1024,256]{1,0:T(8,128)S(1)} %get-tuple-element.60.partial, bf16[512,256]{1,0:T(8,128)(2,1)S(1)} %collective-permute-done.8.incoming.refs_5_), custom_call_target="tpu_custom_call" | custom-call | bytes 8 | tf_op jit(solution)/shard_map/pallas_call | solution.py:37
  41.4 1.5 %collective-permute-done.20.refs_2_ = bf16[912,128]{1,0:T(8,128)(2,1)S(1)} collective-permute-done((bf16[912,128]{1,0:T(8,128)(2,1)S(1)}, bf16[912,128]{1,0:T(8,128)(2,1)S(1)}, u32[]{:S(2)}, u32[]{:S(2)}) %collective-permute-start.20) | collective-permute-done | bytes 233504 | tf_op jit(solution)/shard_map/ppermute | solution.py:416
  42.9 3.1 %collective-permute-done.19.refs_0_.refs_1_ = bf16[912,128]{1,0:T(8,128)(2,1)S(1)} collective-permute-done((bf16[912,128]{1,0:T(8,128)(2,1)S(1)}, bf16[912,128]{1,0:T(8,128)(2,1)S(1)}, u32[]{:S(2)}, u32[]{:S(2)}) %collective-permute-start.19) | collective-permute-done | bytes 233504 | tf_op jit(solution)/shard_map/ppermute | solution.py:416
  46.1 0.1 collective-permute-start.22
  46.1 0.6 %collective-permute-done.17.refs_0_ = bf16[912,128]{1,0:T(8,128)(2,1)S(1)} collective-permute-done((bf16[912,128]{1,0:T(8,128)(2,1)S(1)}, bf16[912,128]{1,0:T(8,128)(2,1)S(1)}, u32[]{:S(2)}, u32[]{:S(2)}) %collective-permute-start.17) | collective-permute-done | bytes 233504 | tf_op jit(solution)/shard_map/ppermute | solution.py:416
  46.7 0.9 %collective-permute-done.22.refs_4_ = bf16[912,128]{1,0:T(8,128)(2,1)S(1)} collective-permute-done((bf16[912,128]{1,0:T(8,128)(2,1)S(1)}, bf16[912,128]{1,0:T(8,128)(2,1)S(1)}, u32[]{:S(2)}, u32[]{:S(2)}) %collective-permute-start.22) | collective-permute-done | bytes 233504 | tf_op jit(solution)/shard_map/ppermute | solution.py:409
  47.6 1.2 %shard_map.122 = (f32[768,512]{1,0:T(8,128)}, f32[256,256]{1,0:T(8,128)}, f32[8,128]{1,0:T(8,128)S(1)}) custom-call(bf16[912,128]{1,0:T(8,128)(2,1)S(1)} %shard_map.120.refs_0_, bf16[912,128]{1,0:T(8,128)(2,1)S(1)} %collective-permute-done.19.refs_0_.refs_1_, bf16[912,128]{1,0:T(8,128)(2,1)S(1)} %collective-permute-done.20.refs_2_, ...), custom_call_target="tpu_custom_call" | custom-call | bytes 8 | tf_op jit(solution)/shard_map/pallas_call | solution.py:37
  48.8 0.9 %shard_map.123 = (f32[768,512]{1,0:T(8,128)}, f32[256,256]{1,0:T(8,128)}, f32[1,512]{1,0:T(1,128)}, f32[1,256]{1,0:T(1,128)}) custom-call(bf16[912,128]{1,0:T(8,128)(2,1)S(1)} %collective-permute-done.17.refs_0_, bf16[912,128]{1,0:T(8,128)(2,1)S(1)} %collective-permute-done.18.refs_1_, ...), custom_call_target="tpu_custom_call", output_to_operand_aliasing={{0}: (3, {}), {1}: (4, {})} | custom-call | bytes 8 | tf_op jit(solution)/shard_map/pallas_call | solution.py:37
  (20 shorter events, 0.2 us)
Async XLA Ops:
  1.6 13.3 %collective-permute-start = (bf16[512,256]{1,0:T(8,128)(2,1)S(1)}, bf16[512,256]{1,0:T(8,128)(2,1)S(1)}, u32[]{:S(2)}, u32[]{:S(2)}) collective-permute-start(bf16[512,256]{1,0:T(8,128)(2,1)S(1)} %slice_bitcast_fusion), channel_id=1, source_target_pairs={{0,2},{2,4},{4,6},{6,8},{8,10},{10,12},{12,14},{14,16},{16,18},{18... | collective-permute-start | bytes 786440 | tf_op jit(solution)/shard_map/ppermute | solution.py:525
  4.6 0.7 %copy-start = (f32[512]{0:T(512)S(1)}, f32[512]{0:T(512)}, u32[]{:S(2)}) copy-start(f32[512]{0:T(512)} %param.8) | copy-start | bytes 6148
  16.3 1.6 %collective-permute-start.1 = (bf16[912,128]{1,0:T(8,128)(2,1)S(1)}, bf16[912,128]{1,0:T(8,128)(2,1)S(1)}, u32[]{:S(2)}, u32[]{:S(2)}) collective-permute-start(bf16[912,128]{1,0:T(8,128)(2,1)S(1)} %get-tuple-element.58), channel_id=1, source_target_pairs={{0,1},{1,0},{2,3},{3,2},{4,5},{5,4},{6,7},{7,6},{8,9},{9,8},{10,11... | collective-permute-start | bytes 700424 | tf_op jit(solution)/shard_map/ppermute | solution.py:409
  16.3 1.8 %collective-permute-start.3 = (bf16[912,128]{1,0:T(8,128)(2,1)S(1)}, bf16[912,128]{1,0:T(8,128)(2,1)S(1)}, u32[]{:S(2)}, u32[]{:S(2)}) collective-permute-start(bf16[912,128]{1,0:T(8,128)(2,1)S(1)} %get-tuple-element.63), channel_id=1, source_target_pairs={{0,1},{1,0},{2,3},{3,2},{4,5},{5,4},{6,7},{7,6},{8,9},{9,8},{10,11... | collective-permute-start | bytes 700424 | tf_op jit(solution)/shard_map/ppermute | solution.py:409
  16.8 1.7 %collective-permute-start.5 = (bf16[912,128]{1,0:T(8,128)(2,1)S(1)}, bf16[912,128]{1,0:T(8,128)(2,1)S(1)}, u32[]{:S(2)}, u32[]{:S(2)}) collective-permute-start(bf16[912,128]{1,0:T(8,128)(2,1)S(1)} %get-tuple-element.67), channel_id=1, source_target_pairs={{0,1},{1,0},{2,3},{3,2},{4,5},{5,4},{6,7},{7,6},{8,9},{9,8},{10,11... | collective-permute-start | bytes 700424 | tf_op jit(solution)/shard_map/ppermute | solution.py:409
  17.8 3.1 %copy-start.1 = (f32[256]{0:T(256)S(1)}, f32[256]{0:T(256)}, u32[]{:S(2)}) copy-start(f32[256]{0:T(256)} %param.10) | copy-start | bytes 3076
  17.9 6.0 %collective-permute-start.7 = (bf16[912,128]{1,0:T(8,128)(2,1)S(1)}, bf16[912,128]{1,0:T(8,128)(2,1)S(1)}, u32[]{:S(2)}, u32[]{:S(2)}) collective-permute-start(bf16[912,128]{1,0:T(8,128)(2,1)S(1)} %shard_map.111.refs_9_), channel_id=1, source_target_pairs={{0,5},{2,7},{4,1},{6,3},{8,13},{10,15},{12,9},{14,11},{16,21},{18,... | collective-permute-start | bytes 700424 | tf_op jit(solution)/shard_map/ppermute | solution.py:416
  18.3 5.6 %collective-permute-start.4 = (bf16[912,128]{1,0:T(8,128)(2,1)S(1)}, bf16[912,128]{1,0:T(8,128)(2,1)S(1)}, u32[]{:S(2)}, u32[]{:S(2)}) collective-permute-start(bf16[912,128]{1,0:T(8,128)(2,1)S(1)} %get-tuple-element.65), channel_id=1, source_target_pairs={{0,7},{2,5},{4,3},{6,1},{8,15},{10,13},{12,11},{14,9},{16,23},{18,... | collective-permute-start | bytes 700424 | tf_op jit(solution)/shard_map/ppermute | solution.py:416
  18.6 5.8 %collective-permute-start.6 = (bf16[912,128]{1,0:T(8,128)(2,1)S(1)}, bf16[912,128]{1,0:T(8,128)(2,1)S(1)}, u32[]{:S(2)}, u32[]{:S(2)}) collective-permute-start(bf16[912,128]{1,0:T(8,128)(2,1)S(1)} %shard_map.115), channel_id=1, source_target_pairs={{0,3},{2,1},{4,7},{6,5},{8,11},{10,9},{12,15},{14,13},{16,19},{18,... | collective-permute-start | bytes 700424 | tf_op jit(solution)/shard_map/ppermute | solution.py:416
  18.6 10.3 %collective-permute-start.2 = (bf16[512,256]{1,0:T(8,128)(2,1)S(1)}, bf16[512,256]{1,0:T(8,128)(2,1)S(1)}, u32[]{:S(2)}, u32[]{:S(2)}) collective-permute-start(bf16[512,256]{1,0:T(8,128)(2,1)S(1)} %shard_map.113.refs_3_.refs_0_), channel_id=1, source_target_pairs={{0,24},{1,25},{2,3},{3,2},{4,5},{5,4},{6,7},{7,6},{8,0},{9,1},{10,... | collective-permute-start | bytes 786440 | tf_op jit(solution)/shard_map/ppermute | solution.py:557
  24.5 8.2 %collective-permute-start.9 = (f32[232,128]{1,0:T(8,128)S(1)}, f32[232,128]{1,0:T(8,128)S(1)}, u32[]{:S(2)}, u32[]{:S(2)}) collective-permute-start(f32[232,128]{1,0:T(8,128)S(1)} %get-tuple-element.71), channel_id=1, source_target_pairs={{0,1},{1,0},{2,3},{3,2},{4,5},{5,4},{6,7},{7,6},{8,9},{9,8},{10,11... | collective-permute-start | bytes 356360 | tf_op jit(solution)/shard_map/ppermute | solution.py:409
  26.6 5.5 %collective-permute-start.10 = (bf16[240,128]{1,0:T(8,128)(2,1)S(1)}, bf16[240,128]{1,0:T(8,128)(2,1)S(1)}, u32[]{:S(2)}, u32[]{:S(2)}) collective-permute-start(bf16[240,128]{1,0:T(8,128)(2,1)S(1)} %get-tuple-element.72), channel_id=1, source_target_pairs={{1,24},{3,26},{5,28},{7,30},{9,16},{11,18},{13,20},{15,22},{17,8},... | collective-permute-start | bytes 184328 | tf_op jit(solution)/shard_map/ppermute | solution.py:416
  26.6 5.4 %collective-permute-start.12 = (bf16[240,128]{1,0:T(8,128)(2,1)S(1)}, bf16[240,128]{1,0:T(8,128)(2,1)S(1)}, u32[]{:S(2)}, u32[]{:S(2)}) collective-permute-start(bf16[240,128]{1,0:T(8,128)(2,1)S(1)} %get-tuple-element.73), channel_id=1, source_target_pairs={{1,16},{3,18},{5,20},{7,22},{9,24},{11,26},{13,28},{15,30},{17,0},... | collective-permute-start | bytes 184328 | tf_op jit(solution)/shard_map/ppermute | solution.py:416
  29.0 3.7 %collective-permute-start.11 = (bf16[240,128]{1,0:T(8,128)(2,1)S(1)}, bf16[240,128]{1,0:T(8,128)(2,1)S(1)}, u32[]{:S(2)}, u32[]{:S(2)}) collective-permute-start(bf16[240,128]{1,0:T(8,128)(2,1)S(1)} %get-tuple-element.69.refs_2_), channel_id=1, source_target_pairs={{1,8},{3,10},{5,12},{7,14},{9,0},{11,2},{13,4},{15,6},{17,24},{19,... | collective-permute-start | bytes 184328 | tf_op jit(solution)/shard_map/ppermute | solution.py:416
  29.0 8.3 %collective-permute-start.8 = (bf16[512,256]{1,0:T(8,128)(2,1)S(1)}, bf16[512,256]{1,0:T(8,128)(2,1)S(1)}, u32[]{:S(2)}, u32[]{:S(2)}) collective-permute-start(bf16[512,256]{1,0:T(8,128)(2,1)S(1)} %shard_map.117), channel_id=1, source_target_pairs={{0,6},{2,0},{4,2},{6,4},{8,14},{10,8},{12,10},{14,12},{16,22},{18,... | collective-permute-start | bytes 786440 | tf_op jit(solution)/shard_map/ppermute | solution.py:577
  32.7 2.1 %collective-permute-start.16 = (bf16[240,128]{1,0:T(8,128)(2,1)S(1)}, bf16[240,128]{1,0:T(8,128)(2,1)S(1)}, u32[]{:S(2)}, u32[]{:S(2)}) collective-permute-start(bf16[240,128]{1,0:T(8,128)(2,1)S(1)} %shard_map.119.refs_1_), channel_id=1, source_target_pairs={{0,25},{2,27},{4,29},{6,31},{8,17},{10,19},{12,21},{14,23},{16,9},... | collective-permute-start | bytes 184328 | tf_op jit(solution)/shard_map/ppermute | solution.py:416
  32.8 3.3 %collective-permute-start.15 = (bf16[240,128]{1,0:T(8,128)(2,1)S(1)}, bf16[240,128]{1,0:T(8,128)(2,1)S(1)}, u32[]{:S(2)}, u32[]{:S(2)}) collective-permute-start(bf16[240,128]{1,0:T(8,128)(2,1)S(1)} %shard_map.119.refs_1_), channel_id=1, source_target_pairs={{0,17},{2,19},{4,21},{6,23},{8,25},{10,27},{12,29},{14,31},{16,1},... | collective-permute-start | bytes 184328 | tf_op jit(solution)/shard_map/ppermute | solution.py:416
  34.3 2.4 %collective-permute-start.14 = (bf16[240,128]{1,0:T(8,128)(2,1)S(1)}, bf16[240,128]{1,0:T(8,128)(2,1)S(1)}, u32[]{:S(2)}, u32[]{:S(2)}) collective-permute-start(bf16[240,128]{1,0:T(8,128)(2,1)S(1)} %shard_map.119.refs_1_), channel_id=1, source_target_pairs={{0,9},{2,11},{4,13},{6,15},{8,1},{10,3},{12,5},{14,7},{16,25},{18,... | collective-permute-start | bytes 184328 | tf_op jit(solution)/shard_map/ppermute | solution.py:416
  34.3 2.4 %collective-permute-start.13 = (bf16[240,128]{1,0:T(8,128)(2,1)S(1)}, bf16[240,128]{1,0:T(8,128)(2,1)S(1)}, u32[]{:S(2)}, u32[]{:S(2)}) collective-permute-start(bf16[240,128]{1,0:T(8,128)(2,1)S(1)} %shard_map.119.refs_1_), channel_id=1, source_target_pairs={{0,1},{1,0},{2,3},{3,2},{4,5},{5,4},{6,7},{7,6},{8,9},{9,8},{10,11... | collective-permute-start | bytes 184328 | tf_op jit(solution)/shard_map/ppermute | solution.py:409
  37.3 5.5 %collective-permute-start.20 = (bf16[912,128]{1,0:T(8,128)(2,1)S(1)}, bf16[912,128]{1,0:T(8,128)(2,1)S(1)}, u32[]{:S(2)}, u32[]{:S(2)}) collective-permute-start(bf16[912,128]{1,0:T(8,128)(2,1)S(1)} %shard_map.120.refs_0_), channel_id=1, source_target_pairs={{1,2},{3,0},{5,6},{7,4},{9,10},{11,8},{13,14},{15,12},{17,18},{19,... | collective-permute-start | bytes 700424 | tf_op jit(solution)/shard_map/ppermute | solution.py:416
  38.4 7.6 %collective-permute-start.19 = (bf16[912,128]{1,0:T(8,128)(2,1)S(1)}, bf16[912,128]{1,0:T(8,128)(2,1)S(1)}, u32[]{:S(2)}, u32[]{:S(2)}) collective-permute-start(bf16[912,128]{1,0:T(8,128)(2,1)S(1)} %shard_map.120.refs_0_), channel_id=1, source_target_pairs={{1,6},{3,4},{5,2},{7,0},{9,14},{11,12},{13,10},{15,8},{17,22},{19,... | collective-permute-start | bytes 700424 | tf_op jit(solution)/shard_map/ppermute | solution.py:416
  38.7 8.0 %collective-permute-start.17 = (bf16[912,128]{1,0:T(8,128)(2,1)S(1)}, bf16[912,128]{1,0:T(8,128)(2,1)S(1)}, u32[]{:S(2)}, u32[]{:S(2)}) collective-permute-start(bf16[912,128]{1,0:T(8,128)(2,1)S(1)} %shard_map.120.refs_0_), channel_id=1, source_target_pairs={{1,4},{3,6},{5,0},{7,2},{9,12},{11,14},{13,8},{15,10},{17,20},{19,... | collective-permute-start | bytes 700424 | tf_op jit(solution)/shard_map/ppermute | solution.py:416
  40.1 6.7 %collective-permute-start.21 = (bf16[912,128]{1,0:T(8,128)(2,1)S(1)}, bf16[912,128]{1,0:T(8,128)(2,1)S(1)}, u32[]{:S(2)}, u32[]{:S(2)}) collective-permute-start(bf16[912,128]{1,0:T(8,128)(2,1)S(1)} %shard_map.120.refs_0_), channel_id=1, source_target_pairs={{0,1},{1,0},{2,3},{3,2},{4,5},{5,4},{6,7},{7,6},{8,9},{9,8},{10,11... | collective-permute-start | bytes 700424 | tf_op jit(solution)/shard_map/ppermute | solution.py:409
  42.9 3.8 %collective-permute-start.23 = (bf16[912,128]{1,0:T(8,128)(2,1)S(1)}, bf16[912,128]{1,0:T(8,128)(2,1)S(1)}, u32[]{:S(2)}, u32[]{:S(2)}) collective-permute-start(bf16[912,128]{1,0:T(8,128)(2,1)S(1)} %collective-permute-done.20.refs_2_), channel_id=1, source_target_pairs={{0,1},{1,0},{2,3},{3,2},{4,5},{5,4},{6,7},{7,6},{8,9},{9,8},{10,11... | collective-permute-start | bytes 700424 | tf_op jit(solution)/shard_map/ppermute | solution.py:409
  46.1 1.6 %collective-permute-start.22 = (bf16[912,128]{1,0:T(8,128)(2,1)S(1)}, bf16[912,128]{1,0:T(8,128)(2,1)S(1)}, u32[]{:S(2)}, u32[]{:S(2)}) collective-permute-start(bf16[912,128]{1,0:T(8,128)(2,1)S(1)} %shard_map.121), channel_id=1, source_target_pairs={{0,1},{1,0},{2,3},{3,2},{4,5},{5,4},{6,7},{7,6},{8,9},{9,8},{10,11... | collective-permute-start | bytes 700424 | tf_op jit(solution)/shard_map/ppermute | solution.py:409
  46.7 2.1 %collective-permute-start.18 = (bf16[912,128]{1,0:T(8,128)(2,1)S(1)}, bf16[912,128]{1,0:T(8,128)(2,1)S(1)}, u32[]{:S(2)}, u32[]{:S(2)}) collective-permute-start(bf16[912,128]{1,0:T(8,128)(2,1)S(1)} %collective-permute-done.17.refs_0_), channel_id=1, source_target_pairs={{0,1},{1,0},{2,3},{3,2},{4,5},{5,4},{6,7},{7,6},{8,9},{9,8},{10,11... | collective-permute-start | bytes 700424 | tf_op jit(solution)/shard_map/ppermute | solution.py:409

commit v4 on v3

--- a/solution.py
+++ b/solution.py
@@ -142,45 +142,46 @@
     grad_bias[:, 2 * channels :] = dot(ones, cot[...])[:SUBLANES]
 
 
-def early_kernel(
-    level, pieces, history, signal, weight, cot, preact_in, dmixed_in, conv_in, proj_in, bias_in,
-    mixed_out, dpre_out, *refs,
-):
-    radix, digit, core = 1 << len(level), digit_of(level), place_of()[1]
-    turn = steps_of(level)
-    first = lax.axis_index("tm") == 0
-    own, offered = refs[:radix], refs[radix : 2 * radix - 1]
-    past, grad_conv, grad_proj = refs[2 * radix - 1 :]
-    rows, channels = signal.shape
-    tap = lambda k: weight[k * channels : (k + 1) * channels, :]
-    past[...] = jnp.where(first, jnp.zeros_like(history), history[...])
-    for begin in range(0, SPAN, STEP):
-        here = slice(begin, begin + STEP)
-        preact = preact_in[here, :]
-        for k in range(begin // STEP + 1, TAPS):
-            source = SPAN + begin - k * STEP
-            preact = preact + dot(past[source : source + STEP, :], tap(k))
-        mixed, dfiltered, dgated = gates(preact, dmixed_in[here, :])
-        mixed_out[here, :] = mixed
-        dpre_out[here, :channels] = dfiltered
-        dpre_out[here, channels:] = dgated
+def chunk(begin, past, signal, weight, cot, preact_in, dmixed_in, conv_in, proj_in, bias_in, mixed_out, dpre_out, conv, proj):
+    channels = signal.shape[1]
+    here = slice(begin, begin + STEP)
+    own = begin // STEP + 1
+    past = [
+        jnp.where(lax.axis_index("tm") == 0, jnp.zeros_like(block), block[...]) for block in past
+    ]
+    preact = preact_in[here, :]
+    for k in range(own, TAPS):
+        preact = preact + dot(past[k - own], weight[k * channels : (k + 1) * channels, :])
+    mixed, dfiltered, dgated = gates(preact, dmixed_in[here, :])
+    mixed_out[...] = mixed
+    dpre_out[:, :channels] = dfiltered
+    dpre_out[:, channels:] = dgated
     dpre = dpre_out[...]
     for k in range(TAPS):
         at = slice(k * channels, (k + 1) * channels)
-        total = conv_in[at, :]
-        if k:
-            total = total + dot_rows(past[SPAN - k * STEP :, :], dpre[: k * STEP, :])
-        if k < TAPS - 1:
-            total = total + dot_rows(signal[: SPAN - k * STEP, :], dpre[k * STEP :, :])
-        grad_conv[at, :] = total
-    grad_proj[: proj_in.shape[0], :] = proj_in[...] + dot_rows(mixed_out[...], cot[:SPAN, :])
+        seen = past[k - own] if k >= own else signal[begin - k * STEP : begin - k * STEP + STEP, :]
+        conv[at, :] = conv_in[at, :] + dot_rows(seen, dpre)
+    proj[: channels, :] = proj_in[...] + dot_rows(mixed, cot[here, :])
+    columns = dot(jnp.ones((BIAS_ROWS, STEP), BF16), dpre)[:SUBLANES]
+    return jnp.concatenate([bias_in[:, : 2 * channels] + columns, bias_in[:, 2 * channels :]], 1)
+
+
+def middle_kernel(begin, *refs):
+    *ins, grad_bias = refs
+    grad_bias[...] = chunk(begin, ins[:1], *ins[1:])
+
+
+def early_kernel(level, pieces, *refs):
+    radix, digit, core = 1 << len(level), digit_of(level), place_of()[1]
+    turn = steps_of(level)
+    ins, (mixed_out, dpre_out), refs = refs[: TAPS + 7], refs[TAPS + 7 : TAPS + 9], refs[TAPS + 9 :]
+    own, offered = refs[:radix], refs[radix : 2 * radix - 1]
+    grad_conv, grad_proj = refs[2 * radix - 1 :]
+    bias = chunk(0, ins[: TAPS - 1], *ins[TAPS - 1 :], mixed_out, dpre_out, grad_conv, grad_proj)
+    conv_in, proj_in = ins[-3], ins[-2]
     for grad, filled in ((grad_conv, conv_in.shape[0]), (grad_proj, proj_in.shape[0])):
         if filled < grad.shape[0]:
             grad[filled:, :] = jnp.zeros((grad.shape[0] - filled, grad.shape[1]), F32)
-    ones = jnp.ones((BIAS_ROWS, SPAN), BF16)
-    columns = dot(ones, dpre)[:SUBLANES]
-    bias = bias_in[...]
-    bias = jnp.concatenate([bias[:, : 2 * channels] + columns, bias[:, 2 * channels :]], 1)
     lines = [bias[:1, c : c + LANES] for c in range(0, bias.shape[1], LANES)]
     lines += [jnp.zeros((1, LANES), F32)] * (SUBLANES - len(lines))
     bias = jnp.concatenate(lines, 0)
@@ -208,35 +209,35 @@
             offered[0][:at, :] = own[k][:at, :].astype(BF16)
 
 
-def back_kernel(dpre, weight, out):
+def back_kernel(*refs):
+    *blocks, weight, out = refs
     channels = out.shape[1]
     tap = lambda k: weight[k * channels : (k + 1) * channels, :]
-    for begin in range(0, SPAN, STEP):
-        total = dot_columns(dpre[begin : begin + STEP, :], tap(TAPS - 1))
-        for k in range(1, TAPS - 1):
-            source = begin - SPAN + k * STEP
-            if source >= 0:
-                total = total + dot_columns(dpre[source : source + STEP, :], tap(k))
-        out[begin : begin + STEP, :] = total.astype(BF16)
-
-
-def own_kernel(signal, weight, out_weight, out_bias, cot, mixed_early, mixed_late, dpre_early, dpre_late, output, partial, token):
+    for n in range(TAPS - 1):
+        total = dot_columns(blocks[n][...], tap(TAPS - 1))
+        for k in range(TAPS - 1 - n, TAPS - 1):
+            total = total + dot_columns(blocks[n - TAPS + 1 + k][...], tap(k))
+        out[n * STEP : (n + 1) * STEP, :] = total.astype(BF16)
+
+
+def own_kernel(signal, weight, out_weight, out_bias, cot, *refs):
     rows, channels = signal.shape
     tap = lambda k: weight[k * channels : (k + 1) * channels, :]
+    mixed, dpre, (output, partial, token) = refs[:TAPS], refs[TAPS : 2 * TAPS], refs[2 * TAPS :]
     token[...] = jnp.zeros_like(token)
 
-    def part(early, late, begin):
-        ref, at = (early, begin) if begin < SPAN else (late, begin - SPAN)
-        return ref[at : at + STEP, :]
+    def part(refs, begin):
+        block = min(begin // STEP, TAPS - 1)
+        return refs[block][begin - block * STEP : begin - block * STEP + STEP, :]
 
     for begin in range(0, rows, STEP):
         here = slice(begin, begin + STEP)
-        hidden = dot(part(mixed_early, mixed_late, begin), out_weight[...]) + out_bias[...]
+        hidden = dot(part(mixed, begin), out_weight[...]) + out_bias[...]
         output[here, :] = (signal[here, :].astype(F32) + hidden).astype(BF16)
         total = cot[here, :].astype(F32)
         for k in range(TAPS):
             if begin + k * STEP < rows:
-                total = total + dot_columns(part(dpre_early, dpre_late, begin + k * STEP), tap(k))
+                total = total + dot_columns(part(dpre, begin + k * STEP), tap(k))
         partial[here, :] = total
 
 
@@ -522,7 +523,14 @@
     heights = [piece_height(n, chips) for n in (TAPS * channels, channels)]
     piece = chips // radix * sum(h * w // LANES for h, w in zip(heights, widths))
 
-    history = lax.ppermute(signal[0, late:], "tm", [(i, (i + 1) % size) for i in range(size)])
+    history = [
+        lax.ppermute(
+            signal[0, rows - n * STEP : rows - n * STEP + STEP],
+            "tm",
+            [(i, (i + 1) % size) for i in range(size)],
+        )
+        for n in range(1, TAPS)
+    ]
     x, weight, proj_weight, cot, preact, dmixed, mixed_late, dpre_late, conv, proj, bias = call(
         late_kernel,
         [
@@ -536,23 +544,26 @@
         scratch=[pltpu.SemaphoreType.DMA((4,))],
         far=(0, 1, 3, 4),
     )
+    grads = [held(F32, TAPS * channels, wide), held(F32, channels, channels)]
+    mixed_middle, dpre_middle, conv, proj, bias = call(
+        functools.partial(middle_kernel, STEP),
+        [held(BF16, STEP, channels), held(BF16, STEP, wide), *grads, held(F32, SUBLANES, wide + channels)],
+        (history[0], x, weight, cot, preact, dmixed, conv, proj, bias),
+    )
     mixed_early, dpre_early, *pieces = call(
         functools.partial(early_kernel, level, chips),
-        [held(BF16, SPAN, channels), held(BF16, SPAN, wide)]
+        [held(BF16, STEP, channels), held(BF16, STEP, wide)]
         + [held(F32, piece + SUBLANES, LANES)] * radix
         + [held(BF16, piece + BIAS_ROWS, LANES)] * (radix - 1),
-        (
-            history, x, weight, cot, preact, dmixed, conv, proj, bias,
-        ),
-        scratch=[pltpu.VMEM((SPAN, channels), BF16)]
-        + [pltpu.VMEM((chips * h, w), F32) for h, w in zip(heights, widths)],
+        (*history, x, weight, cot, preact, dmixed, conv, proj, bias),
+        scratch=[pltpu.VMEM((chips * h, w), F32) for h, w in zip(heights, widths)],
     )
     results = {}
 
     def fill(stage, after):
         if stage == 0:
             (results["back"],) = call(
-                back_kernel, [held(BF16, SPAN, channels)], (dpre_early, weight), after=after
+                back_kernel, [held(BF16, SPAN, channels)], (dpre_early, dpre_middle, weight), after=after
             )
             results["relayed"] = lax.ppermute(results["back"], BOTH, relay_pairs())
             return (results["back"],)
@@ -562,7 +573,7 @@
                 [shape(BF16, rows, channels), held(F32, rows, channels), TOKEN],
                 (
                     x, weight, proj_weight, out_bias.reshape(1, -1), cot,
-                    mixed_early, mixed_late, dpre_early, dpre_late,
+                    mixed_early, mixed_middle, mixed_late, dpre_early, dpre_middle, dpre_late,
                 ),
                 after=after,
             )

time: 49.9 us -> 49.6 us (level)
  waiting for transfers between devices: 20.5 us -> 18.3 us
  starting transfers between devices: 16.7 us -> 18.1 us
    ppermute x1 -> x2, waiting for transfers between devices: 6.28 us -> 4.05 us  [local(): lax.ppermute(signal[0, rows - n * STEP:rows - n * STEP + STEP], 'tm', [(i...]
    ppermute x1 -> x2, starting transfers between devices: 2.99 us -> 4.48 us  [local(): lax.ppermute(signal[0, rows - n * STEP:rows - n * STEP + STEP], 'tm', [(i...]
    pallas_call x15 -> x16, Pallas kernels: 10.1 us -> 10.5 us  [call(): pl.pallas_call(inner, out_shape=out_shape, in_specs=ins + [ANY] * len(aft...]
  transfers between devices with their start and end apart: 24 -> 25, of which waited for: 15 -> 16; matrix products, arithmetic and copies ran while one was open for 0% -> 0% of each run, Pallas kernels for 16% -> 17%
where the time goes in v4:
time: 49.6 us; the launch traced here: 49.4 us
  waiting for transfers between devices  18.3 us (37%)
  starting transfers between devices  18.1 us (36%)
  Pallas kernels  10.5 us (21%)
  local copies, waits for them, and re-layouts  1.67 us (3%)
  between operations  0.78 us (2%)
    ppermute x12, waiting for transfers between devices, crossed(): return lax.ppermute(array, BOTH, pairs)  11.9 us
    pallas_call x16, Pallas kernels, call(): pl.pallas_call(inner, out_shape=out_shape, in_specs=ins + [ANY] * len(aft...  10.5 us
    ppermute x12, starting transfers between devices, crossed(): return lax.ppermute(array, BOTH, pairs)  6.83 us
    ppermute x2, starting transfers between devices, local(): lax.ppermute(signal[0, rows - n * STEP:rows - n * STEP + STEP], 'tm', [(i...  4.48 us
    ppermute x2, waiting for transfers between devices, local(): lax.ppermute(signal[0, rows - n * STEP:rows - n * STEP + STEP], 'tm', [(i...  4.05 us
    ppermute x9, starting transfers between devices, swapped(): return lax.ppermute(array, BOTH, [(i, i ^ 1) for i in range(2 * chips)])  3.71 us
    ppermute x1, starting transfers between devices, fill(): results['relayed'] = lax.ppermute(results['back'], BOTH, relay_pairs())  2.33 us
    ppermute x9, waiting for transfers between devices, swapped(): return lax.ppermute(array, BOTH, [(i, i ^ 1) for i in range(2 * chips)])  1.77 us
  transfers between devices with their start and end apart: 25, of which 16 were waited for; matrix products, arithmetic and copies ran while one was open for 0% of the time, Pallas kernels for 17%

profile of v4, /device:TPU:0, one launch (start us, length us, event | category | flops | bytes accessed | tf_op | source)
XLA Modules:
  0.0 49.4 jit_solution(779570006467081520)
XLA Ops:
  0.6 1.0 %slice_bitcast_fusion = (bf16[256,256]{1,0:T(8,128)(2,1)S(1)}, bf16[256,256]{1,0:T(8,128)(2,1)S(1)}) fusion(bf16[1,1024,256]{2,1,0:T(8,128)(2,1)} %param.6), kind=kLoop, calls=%fused_computation | loop fusion | bytes 524288 | tf_op jit(solution)/shard_map/squeeze | solution.py:528
  1.6 3.0 %collective-permute-start = (bf16[256,256]{1,0:T(8,128)(2,1)S(1)}, bf16[256,256]{1,0:T(8,128)(2,1)S(1)}, u32[]{:S(2)}, u32[]{:S(2)}) collective-permute-start(bf16[256,256]{1,0:T(8,128)(2,1)S(1)} %get-tuple-element.93), channel_id=1, source_target_pairs={{0,2},{2,4},{4,6},{6,8},{8,10},{10,12},{12,14},{14,16},{16,18},{18... | collective-permute-start | bytes 393224 | tf_op jit(solution)/shard_map/ppermute | solution.py:527
  4.6 1.5 %collective-permute-start.1 = (bf16[256,256]{1,0:T(8,128)(2,1)S(1)}, bf16[256,256]{1,0:T(8,128)(2,1)S(1)}, u32[]{:S(2)}, u32[]{:S(2)}) collective-permute-start(bf16[256,256]{1,0:T(8,128)(2,1)S(1)} %get-tuple-element.92), channel_id=1, source_target_pairs={{0,2},{2,4},{4,6},{6,8},{8,10},{10,12},{12,14},{14,16},{16,18},{18... | collective-permute-start | bytes 393224 | tf_op jit(solution)/shard_map/ppermute | solution.py:527
  6.1 0.7 %copy-done = f32[512]{0:T(512)S(1)} copy-done((f32[512]{0:T(512)S(1)}, f32[512]{0:T(512)}, u32[]{:S(2)}) %copy-start) | copy-done | bytes 2072
  6.8 3.3 %shard_map.109 = (bf16[1024,256]{1,0:T(8,128)(2,1)S(1)}, bf16[768,512]{1,0:T(8,128)(2,1)S(1)}, bf16[256,256]{1,0:T(8,128)(2,1)S(1)}, bf16[1024,256]{1,0:T(8,128)...) custom-call(bf16[1024,256]{1,0:T(8,128)(2,1)} %bitcast.14, ...), custom_call_target="tpu_custom_call" | custom-call | bytes 8 | tf_op jit(solution)/shard_map/pallas_call | solution.py:37
  10.1 2.8 %collective-permute-done.refs_0_ = bf16[256,256]{1,0:T(8,128)(2,1)S(1)} collective-permute-done((bf16[256,256]{1,0:T(8,128)(2,1)S(1)}, bf16[256,256]{1,0:T(8,128)(2,1)S(1)}, u32[]{:S(2)}, u32[]{:S(2)}) %collective-permute-start) | collective-permute-done | bytes 131104 | tf_op jit(solution)/shard_map/ppermute | solution.py:527
  12.9 0.7 %shard_map.110 = (bf16[256,256]{1,0:T(8,128)(2,1)S(1)}, bf16[256,512]{1,0:T(8,128)(2,1)S(1)}, f32[768,512]{1,0:T(8,128)S(1)}, f32[256,256]{1,0:T(8,128)S(1)}, f32[8,768]{1,0:T(8,128)S(1)}) custom-call(bf16[256,256]{1,0:T(8,128)(2,1)S(1)} %collective-permute-done.refs_0_, bf16[1024,256]{1,0:T(8,128)(2,1)S(1)} %get-tuple-element.49.refs_1_.refs_2_.refs_0_, ...), custom_call_target="tpu_custom_call" | custom-call | bytes 8 | tf_op jit(solution)/shard_map/pallas_call | solution.py:37
  13.7 1.2 %collective-permute-done.1.refs_1_ = bf16[256,256]{1,0:T(8,128)(2,1)S(1)} collective-permute-done((bf16[256,256]{1,0:T(8,128)(2,1)S(1)}, bf16[256,256]{1,0:T(8,128)(2,1)S(1)}, u32[]{:S(2)}, u32[]{:S(2)}) %collective-permute-start.1) | collective-permute-done | bytes 131104 | tf_op jit(solution)/shard_map/ppermute | solution.py:527
  14.9 1.0 %shard_map.111 = (bf16[256,256]{1,0:T(8,128)(2,1)S(1)}, bf16[256,512]{1,0:T(8,128)(2,1)S(1)}, f32[904,128]{1,0:T(8,128)S(1)}, f32[904,128]{1,0:T(8,128)S(1)}, f3...) custom-call(bf16[256,256]{1,0:T(8,128)(2,1)S(1)} %collective-permute, ...), custom_call_target="tpu_custom_call" | custom-call | bytes 8 | tf_op jit(solution)/shard_map/pallas_call | solution.py:37
  15.9 0.1 collective-permute-start.2
  16.0 0.5 %collective-permute-start.4 = (bf16[912,128]{1,0:T(8,128)(2,1)S(1)}, bf16[912,128]{1,0:T(8,128)(2,1)S(1)}, u32[]{:S(2)}, u32[]{:S(2)}) collective-permute-start(bf16[912,128]{1,0:T(8,128)(2,1)S(1)} %get-tuple-element.73), channel_id=1, source_target_pairs={{0,1},{1,0},{2,3},{3,2},{4,5},{5,4},{6,7},{7,6},{8,9},{9,8},{10,11... | collective-permute-start | bytes 700424 | tf_op jit(solution)/shard_map/ppermute | solution.py:410
  16.5 0.1 collective-permute-start.6
  16.6 0.4 shard_map.114.refs_3_.refs_0_
  17.0 0.5 %collective-permute-done.2.received = bf16[912,128]{1,0:T(8,128)(2,1)S(1)} collective-permute-done((bf16[912,128]{1,0:T(8,128)(2,1)S(1)}, bf16[912,128]{1,0:T(8,128)(2,1)S(1)}, u32[]{:S(2)}, u32[]{:S(2)}) %collective-permute-start.2) | collective-permute-done | bytes 233504 | tf_op jit(solution)/shard_map/ppermute | solution.py:410
  17.5 0.1 shard_map.112.refs_11_
  17.6 0.2 collective-permute-done.4.refs_2_
  17.8 0.1 shard_map.115
  18.0 0.2 collective-permute-done.6.received
  18.1 0.1 shard_map.116
  18.3 2.3 %collective-permute-start.3 = (bf16[512,256]{1,0:T(8,128)(2,1)S(1)}, bf16[512,256]{1,0:T(8,128)(2,1)S(1)}, u32[]{:S(2)}, u32[]{:S(2)}) collective-permute-start(bf16[512,256]{1,0:T(8,128)(2,1)S(1)} %shard_map.114.refs_3_.refs_0_), channel_id=1, source_target_pairs={{0,24},{1,25},{2,3},{3,2},{4,5},{5,4},{6,7},{7,6},{8,0},{9,1},{10,... | collective-permute-start | bytes 786440 | tf_op jit(solution)/shard_map/ppermute | solution.py:568
  20.6 1.6 %shard_map.113 = (bf16[1024,256]{1,0:T(8,128)(2,1)}, f32[1024,256]{1,0:T(8,128)S(1)}, f32[8,128]{1,0:T(8,128)S(1)}) custom-call(bf16[1024,256]{1,0:T(8,128)(2,1)S(1)} %get-tuple-element.49.refs_1_.refs_2_.refs_0_, bf16[768,512]{1,0:T(8,128)(2,1)S(1)} %get-tuple-element.50.refs_2_.refs_3_.refs_1_, bf16[256,256]{1,0:T(8,128)(2,1)S(1)} %get-tuple-element.51.refs_2_, ...), custom_call_target="tpu_custom_call" | custom-call | bytes 8 | tf_op jit(solution)/shard_map/pallas_call | solution.py:37
  22.2 1.3 %collective-permute-done.8.refs_3_ = bf16[912,128]{1,0:T(8,128)(2,1)S(1)} collective-permute-done((bf16[912,128]{1,0:T(8,128)(2,1)S(1)}, bf16[912,128]{1,0:T(8,128)(2,1)S(1)}, u32[]{:S(2)}, u32[]{:S(2)}) %collective-permute-start.8) | collective-permute-done | bytes 233504 | tf_op jit(solution)/shard_map/ppermute | solution.py:417
  23.5 0.5 %collective-permute-done.7.refs_2_ = bf16[912,128]{1,0:T(8,128)(2,1)S(1)} collective-permute-done((bf16[912,128]{1,0:T(8,128)(2,1)S(1)}, bf16[912,128]{1,0:T(8,128)(2,1)S(1)}, u32[]{:S(2)}, u32[]{:S(2)}) %collective-permute-start.7) | collective-permute-done | bytes 233504 | tf_op jit(solution)/shard_map/ppermute | solution.py:417
  24.1 0.1 shard_map.117
  24.2 2.0 %collective-permute-start.10 = (f32[232,128]{1,0:T(8,128)S(1)}, f32[232,128]{1,0:T(8,128)S(1)}, u32[]{:S(2)}, u32[]{:S(2)}) collective-permute-start(f32[232,128]{1,0:T(8,128)S(1)} %get-tuple-element.81), channel_id=1, source_target_pairs={{0,1},{1,0},{2,3},{3,2},{4,5},{5,4},{6,7},{7,6},{8,9},{9,8},{10,11... | collective-permute-start | bytes 356360 | tf_op jit(solution)/shard_map/ppermute | solution.py:410
  26.2 0.1 collective-permute-start.11
  26.3 2.3 %collective-permute-start.13 = (bf16[240,128]{1,0:T(8,128)(2,1)S(1)}, bf16[240,128]{1,0:T(8,128)(2,1)S(1)}, u32[]{:S(2)}, u32[]{:S(2)}) collective-permute-start(bf16[240,128]{1,0:T(8,128)(2,1)S(1)} %get-tuple-element.83), channel_id=1, source_target_pairs={{1,16},{3,18},{5,20},{7,22},{9,24},{11,26},{13,28},{15,30},{17,0},... | collective-permute-start | bytes 184328 | tf_op jit(solution)/shard_map/ppermute | solution.py:417
  28.7 0.8 %collective-permute-start.9 = (bf16[512,256]{1,0:T(8,128)(2,1)S(1)}, bf16[512,256]{1,0:T(8,128)(2,1)S(1)}, u32[]{:S(2)}, u32[]{:S(2)}) collective-permute-start(bf16[512,256]{1,0:T(8,128)(2,1)S(1)} %shard_map.118), channel_id=1, source_target_pairs={{0,6},{2,0},{4,2},{6,4},{8,14},{10,8},{12,10},{14,12},{16,22},{18,... | collective-permute-start | bytes 786440 | tf_op jit(solution)/shard_map/ppermute | solution.py:588
  29.5 2.2 %collective-permute-done.11.refs_1_ = bf16[240,128]{1,0:T(8,128)(2,1)S(1)} collective-permute-done((bf16[240,128]{1,0:T(8,128)(2,1)S(1)}, bf16[240,128]{1,0:T(8,128)(2,1)S(1)}, u32[]{:S(2)}, u32[]{:S(2)}) %collective-permute-start.11) | collective-permute-done | bytes 61472 | tf_op jit(solution)/shard_map/ppermute | solution.py:417
  31.7 0.6 %collective-permute-done.12.refs_2_ = bf16[240,128]{1,0:T(8,128)(2,1)S(1)} collective-permute-done((bf16[240,128]{1,0:T(8,128)(2,1)S(1)}, bf16[240,128]{1,0:T(8,128)(2,1)S(1)}, u32[]{:S(2)}, u32[]{:S(2)}) %collective-permute-start.12) | collective-permute-done | bytes 61472 | tf_op jit(solution)/shard_map/ppermute | solution.py:417
  32.4 0.1 collective-permute-start.17
  32.5 1.5 %collective-permute-start.16 = (bf16[240,128]{1,0:T(8,128)(2,1)S(1)}, bf16[240,128]{1,0:T(8,128)(2,1)S(1)}, u32[]{:S(2)}, u32[]{:S(2)}) collective-permute-start(bf16[240,128]{1,0:T(8,128)(2,1)S(1)} %shard_map.120.refs_1_), channel_id=1, source_target_pairs={{0,17},{2,19},{4,21},{6,23},{8,25},{10,27},{12,29},{14,31},{16,1},... | collective-permute-start | bytes 184328 | tf_op jit(solution)/shard_map/ppermute | solution.py:417
  33.9 0.5 %collective-permute-start.14 = (bf16[240,128]{1,0:T(8,128)(2,1)S(1)}, bf16[240,128]{1,0:T(8,128)(2,1)S(1)}, u32[]{:S(2)}, u32[]{:S(2)}) collective-permute-start(bf16[240,128]{1,0:T(8,128)(2,1)S(1)} %shard_map.120.refs_1_), channel_id=1, source_target_pairs={{0,1},{1,0},{2,3},{3,2},{4,5},{5,4},{6,7},{7,6},{8,9},{9,8},{10,11... | collective-permute-start | bytes 184328 | tf_op jit(solution)/shard_map/ppermute | solution.py:410
  34.5 1.4 %collective-permute-done.16.refs_3_ = bf16[240,128]{1,0:T(8,128)(2,1)S(1)} collective-permute-done((bf16[240,128]{1,0:T(8,128)(2,1)S(1)}, bf16[240,128]{1,0:T(8,128)(2,1)S(1)}, u32[]{:S(2)}, u32[]{:S(2)}) %collective-permute-start.16) | collective-permute-done | bytes 61472 | tf_op jit(solution)/shard_map/ppermute | solution.py:417
  35.8 0.6 %collective-permute-done.15.refs_2_ = bf16[240,128]{1,0:T(8,128)(2,1)S(1)} collective-permute-done((bf16[240,128]{1,0:T(8,128)(2,1)S(1)}, bf16[240,128]{1,0:T(8,128)(2,1)S(1)}, u32[]{:S(2)}, u32[]{:S(2)}) %collective-permute-start.15) | collective-permute-done | bytes 61472 | tf_op jit(solution)/shard_map/ppermute | solution.py:417
  36.4 0.6 %collective-permute-done.9.incoming.refs_5_ = bf16[512,256]{1,0:T(8,128)(2,1)S(1)} collective-permute-done((bf16[512,256]{1,0:T(8,128)(2,1)S(1)}, bf16[512,256]{1,0:T(8,128)(2,1)S(1)}, u32[]{:S(2)}, u32[]{:S(2)}) %collective-permute-start.9) | collective-permute-done | bytes 262176 | tf_op jit(solution)/shard_map/ppermute | solution.py:588
  37.0 1.1 %collective-permute-start.21 = (bf16[912,128]{1,0:T(8,128)(2,1)S(1)}, bf16[912,128]{1,0:T(8,128)(2,1)S(1)}, u32[]{:S(2)}, u32[]{:S(2)}) collective-permute-start(bf16[912,128]{1,0:T(8,128)(2,1)S(1)} %shard_map.121.refs_0_), channel_id=1, source_target_pairs={{1,2},{3,0},{5,6},{7,4},{9,10},{11,8},{13,14},{15,12},{17,18},{19,... | collective-permute-start | bytes 700424 | tf_op jit(solution)/shard_map/ppermute | solution.py:417
  38.1 0.3 collective-permute-start.20
  38.4 1.3 %collective-permute-start.18 = (bf16[912,128]{1,0:T(8,128)(2,1)S(1)}, bf16[912,128]{1,0:T(8,128)(2,1)S(1)}, u32[]{:S(2)}, u32[]{:S(2)}) collective-permute-start(bf16[912,128]{1,0:T(8,128)(2,1)S(1)} %shard_map.121.refs_0_), channel_id=1, source_target_pairs={{1,4},{3,6},{5,0},{7,2},{9,12},{11,14},{13,8},{15,10},{17,20},{19,... | collective-permute-start | bytes 700424 | tf_op jit(solution)/shard_map/ppermute | solution.py:417
  39.7 0.4 collective-permute-start.22
  40.2 0.9 %shard_map.119 = (bf16[1024,256]{1,0:T(8,128)(2,1)}, f32[8,128]{1,0:T(8,128)S(1)}) custom-call(f32[1024,256]{1,0:T(8,128)S(1)} %get-tuple-element.70.partial, bf16[512,256]{1,0:T(8,128)(2,1)S(1)} %collective-permute-done.9.incoming.refs_5_), custom_call_target="tpu_custom_call" | custom-call | bytes 8 | tf_op jit(solution)/shard_map/pallas_call | solution.py:37
  41.1 1.5 %collective-permute-done.21.refs_2_ = bf16[912,128]{1,0:T(8,128)(2,1)S(1)} collective-permute-done((bf16[912,128]{1,0:T(8,128)(2,1)S(1)}, bf16[912,128]{1,0:T(8,128)(2,1)S(1)}, u32[]{:S(2)}, u32[]{:S(2)}) %collective-permute-start.21) | collective-permute-done | bytes 233504 | tf_op jit(solution)/shard_map/ppermute | solution.py:417
  42.6 3.1 %collective-permute-done.20.refs_0_.refs_1_ = bf16[912,128]{1,0:T(8,128)(2,1)S(1)} collective-permute-done((bf16[912,128]{1,0:T(8,128)(2,1)S(1)}, bf16[912,128]{1,0:T(8,128)(2,1)S(1)}, u32[]{:S(2)}, u32[]{:S(2)}) %collective-permute-start.20) | collective-permute-done | bytes 233504 | tf_op jit(solution)/shard_map/ppermute | solution.py:417
  45.7 0.1 collective-permute-start.23
  45.8 0.6 %collective-permute-done.18.refs_0_ = bf16[912,128]{1,0:T(8,128)(2,1)S(1)} collective-permute-done((bf16[912,128]{1,0:T(8,128)(2,1)S(1)}, bf16[912,128]{1,0:T(8,128)(2,1)S(1)}, u32[]{:S(2)}, u32[]{:S(2)}) %collective-permute-start.18) | collective-permute-done | bytes 233504 | tf_op jit(solution)/shard_map/ppermute | solution.py:417
  46.4 0.9 %collective-permute-done.23.refs_4_ = bf16[912,128]{1,0:T(8,128)(2,1)S(1)} collective-permute-done((bf16[912,128]{1,0:T(8,128)(2,1)S(1)}, bf16[912,128]{1,0:T(8,128)(2,1)S(1)}, u32[]{:S(2)}, u32[]{:S(2)}) %collective-permute-start.23) | collective-permute-done | bytes 233504 | tf_op jit(solution)/shard_map/ppermute | solution.py:410
  47.3 1.2 %shard_map.123 = (f32[768,512]{1,0:T(8,128)}, f32[256,256]{1,0:T(8,128)}, f32[8,128]{1,0:T(8,128)S(1)}) custom-call(bf16[912,128]{1,0:T(8,128)(2,1)S(1)} %shard_map.121.refs_0_, bf16[912,128]{1,0:T(8,128)(2,1)S(1)} %collective-permute-done.20.refs_0_.refs_1_, bf16[912,128]{1,0:T(8,128)(2,1)S(1)} %collective-permute-done.21.refs_2_, ...), custom_call_target="tpu_custom_call" | custom-call | bytes 8 | tf_op jit(solution)/shard_map/pallas_call | solution.py:37
  48.5 0.9 %shard_map.124 = (f32[768,512]{1,0:T(8,128)}, f32[256,256]{1,0:T(8,128)}, f32[1,512]{1,0:T(1,128)}, f32[1,256]{1,0:T(1,128)}) custom-call(bf16[912,128]{1,0:T(8,128)(2,1)S(1)} %collective-permute-done.18.refs_0_, bf16[912,128]{1,0:T(8,128)(2,1)S(1)} %collective-permute-done.19.refs_1_, ...), custom_call_target="tpu_custom_call", output_to_operand_aliasing={{0}: (3, {}), {1}: (4, {})} | custom-call | bytes 8 | tf_op jit(solution)/shard_map/pallas_call | solution.py:37
  (23 shorter events, 0.4 us)
Async XLA Ops:
  1.6 11.3 %collective-permute-start = (bf16[256,256]{1,0:T(8,128)(2,1)S(1)}, bf16[256,256]{1,0:T(8,128)(2,1)S(1)}, u32[]{:S(2)}, u32[]{:S(2)}) collective-permute-start(bf16[256,256]{1,0:T(8,128)(2,1)S(1)} %get-tuple-element.93), channel_id=1, source_target_pairs={{0,2},{2,4},{4,6},{6,8},{8,10},{10,12},{12,14},{14,16},{16,18},{18... | collective-permute-start | bytes 393224 | tf_op jit(solution)/shard_map/ppermute | solution.py:527
  4.6 10.3 %collective-permute-start.1 = (bf16[256,256]{1,0:T(8,128)(2,1)S(1)}, bf16[256,256]{1,0:T(8,128)(2,1)S(1)}, u32[]{:S(2)}, u32[]{:S(2)}) collective-permute-start(bf16[256,256]{1,0:T(8,128)(2,1)S(1)} %get-tuple-element.92), channel_id=1, source_target_pairs={{0,2},{2,4},{4,6},{6,8},{8,10},{10,12},{12,14},{14,16},{16,18},{18... | collective-permute-start | bytes 393224 | tf_op jit(solution)/shard_map/ppermute | solution.py:527
  6.1 0.7 %copy-start = (f32[512]{0:T(512)S(1)}, f32[512]{0:T(512)}, u32[]{:S(2)}) copy-start(f32[512]{0:T(512)} %param.8) | copy-start | bytes 6148
  15.9 1.6 %collective-permute-start.2 = (bf16[912,128]{1,0:T(8,128)(2,1)S(1)}, bf16[912,128]{1,0:T(8,128)(2,1)S(1)}, u32[]{:S(2)}, u32[]{:S(2)}) collective-permute-start(bf16[912,128]{1,0:T(8,128)(2,1)S(1)} %get-tuple-element.68), channel_id=1, source_target_pairs={{0,1},{1,0},{2,3},{3,2},{4,5},{5,4},{6,7},{7,6},{8,9},{9,8},{10,11... | collective-permute-start | bytes 700424 | tf_op jit(solution)/shard_map/ppermute | solution.py:410
  16.0 1.8 %collective-permute-start.4 = (bf16[912,128]{1,0:T(8,128)(2,1)S(1)}, bf16[912,128]{1,0:T(8,128)(2,1)S(1)}, u32[]{:S(2)}, u32[]{:S(2)}) collective-permute-start(bf16[912,128]{1,0:T(8,128)(2,1)S(1)} %get-tuple-element.73), channel_id=1, source_target_pairs={{0,1},{1,0},{2,3},{3,2},{4,5},{5,4},{6,7},{7,6},{8,9},{9,8},{10,11... | collective-permute-start | bytes 700424 | tf_op jit(solution)/shard_map/ppermute | solution.py:410
  16.5 1.7 %collective-permute-start.6 = (bf16[912,128]{1,0:T(8,128)(2,1)S(1)}, bf16[912,128]{1,0:T(8,128)(2,1)S(1)}, u32[]{:S(2)}, u32[]{:S(2)}) collective-permute-start(bf16[912,128]{1,0:T(8,128)(2,1)S(1)} %get-tuple-element.77), channel_id=1, source_target_pairs={{0,1},{1,0},{2,3},{3,2},{4,5},{5,4},{6,7},{7,6},{8,9},{9,8},{10,11... | collective-permute-start | bytes 700424 | tf_op jit(solution)/shard_map/ppermute | solution.py:410
  17.5 3.1 %copy-start.1 = (f32[256]{0:T(256)S(1)}, f32[256]{0:T(256)}, u32[]{:S(2)}) copy-start(f32[256]{0:T(256)} %param.10) | copy-start | bytes 3076
  17.5 6.0 %collective-permute-start.8 = (bf16[912,128]{1,0:T(8,128)(2,1)S(1)}, bf16[912,128]{1,0:T(8,128)(2,1)S(1)}, u32[]{:S(2)}, u32[]{:S(2)}) collective-permute-start(bf16[912,128]{1,0:T(8,128)(2,1)S(1)} %shard_map.112.refs_11_), channel_id=1, source_target_pairs={{0,5},{2,7},{4,1},{6,3},{8,13},{10,15},{12,9},{14,11},{16,21},{18,... | collective-permute-start | bytes 700424 | tf_op jit(solution)/shard_map/ppermute | solution.py:417
  17.9 5.6 %collective-permute-start.5 = (bf16[912,128]{1,0:T(8,128)(2,1)S(1)}, bf16[912,128]{1,0:T(8,128)(2,1)S(1)}, u32[]{:S(2)}, u32[]{:S(2)}) collective-permute-start(bf16[912,128]{1,0:T(8,128)(2,1)S(1)} %get-tuple-element.75), channel_id=1, source_target_pairs={{0,7},{2,5},{4,3},{6,1},{8,15},{10,13},{12,11},{14,9},{16,23},{18,... | collective-permute-start | bytes 700424 | tf_op jit(solution)/shard_map/ppermute | solution.py:417
  18.2 5.9 %collective-permute-start.7 = (bf16[912,128]{1,0:T(8,128)(2,1)S(1)}, bf16[912,128]{1,0:T(8,128)(2,1)S(1)}, u32[]{:S(2)}, u32[]{:S(2)}) collective-permute-start(bf16[912,128]{1,0:T(8,128)(2,1)S(1)} %shard_map.116), channel_id=1, source_target_pairs={{0,3},{2,1},{4,7},{6,5},{8,11},{10,9},{12,15},{14,13},{16,19},{18,... | collective-permute-start | bytes 700424 | tf_op jit(solution)/shard_map/ppermute | solution.py:417
  18.3 10.4 %collective-permute-start.3 = (bf16[512,256]{1,0:T(8,128)(2,1)S(1)}, bf16[512,256]{1,0:T(8,128)(2,1)S(1)}, u32[]{:S(2)}, u32[]{:S(2)}) collective-permute-start(bf16[512,256]{1,0:T(8,128)(2,1)S(1)} %shard_map.114.refs_3_.refs_0_), channel_id=1, source_target_pairs={{0,24},{1,25},{2,3},{3,2},{4,5},{5,4},{6,7},{7,6},{8,0},{9,1},{10,... | collective-permute-start | bytes 786440 | tf_op jit(solution)/shard_map/ppermute | solution.py:568
  24.2 8.1 %collective-permute-start.10 = (f32[232,128]{1,0:T(8,128)S(1)}, f32[232,128]{1,0:T(8,128)S(1)}, u32[]{:S(2)}, u32[]{:S(2)}) collective-permute-start(f32[232,128]{1,0:T(8,128)S(1)} %get-tuple-element.81), channel_id=1, source_target_pairs={{0,1},{1,0},{2,3},{3,2},{4,5},{5,4},{6,7},{7,6},{8,9},{9,8},{10,11... | collective-permute-start | bytes 356360 | tf_op jit(solution)/shard_map/ppermute | solution.py:410
  26.2 5.5 %collective-permute-start.11 = (bf16[240,128]{1,0:T(8,128)(2,1)S(1)}, bf16[240,128]{1,0:T(8,128)(2,1)S(1)}, u32[]{:S(2)}, u32[]{:S(2)}) collective-permute-start(bf16[240,128]{1,0:T(8,128)(2,1)S(1)} %get-tuple-element.82), channel_id=1, source_target_pairs={{1,24},{3,26},{5,28},{7,30},{9,16},{11,18},{13,20},{15,22},{17,8},... | collective-permute-start | bytes 184328 | tf_op jit(solution)/shard_map/ppermute | solution.py:417
  26.3 5.4 %collective-permute-start.13 = (bf16[240,128]{1,0:T(8,128)(2,1)S(1)}, bf16[240,128]{1,0:T(8,128)(2,1)S(1)}, u32[]{:S(2)}, u32[]{:S(2)}) collective-permute-start(bf16[240,128]{1,0:T(8,128)(2,1)S(1)} %get-tuple-element.83), channel_id=1, source_target_pairs={{1,16},{3,18},{5,20},{7,22},{9,24},{11,26},{13,28},{15,30},{17,0},... | collective-permute-start | bytes 184328 | tf_op jit(solution)/shard_map/ppermute | solution.py:417
  28.6 3.7 %collective-permute-start.12 = (bf16[240,128]{1,0:T(8,128)(2,1)S(1)}, bf16[240,128]{1,0:T(8,128)(2,1)S(1)}, u32[]{:S(2)}, u32[]{:S(2)}) collective-permute-start(bf16[240,128]{1,0:T(8,128)(2,1)S(1)} %get-tuple-element.79.refs_2_), channel_id=1, source_target_pairs={{1,8},{3,10},{5,12},{7,14},{9,0},{11,2},{13,4},{15,6},{17,24},{19,... | collective-permute-start | bytes 184328 | tf_op jit(solution)/shard_map/ppermute | solution.py:417
  28.7 8.3 %collective-permute-start.9 = (bf16[512,256]{1,0:T(8,128)(2,1)S(1)}, bf16[512,256]{1,0:T(8,128)(2,1)S(1)}, u32[]{:S(2)}, u32[]{:S(2)}) collective-permute-start(bf16[512,256]{1,0:T(8,128)(2,1)S(1)} %shard_map.118), channel_id=1, source_target_pairs={{0,6},{2,0},{4,2},{6,4},{8,14},{10,8},{12,10},{14,12},{16,22},{18,... | collective-permute-start | bytes 786440 | tf_op jit(solution)/shard_map/ppermute | solution.py:588
  32.4 2.1 %collective-permute-start.17 = (bf16[240,128]{1,0:T(8,128)(2,1)S(1)}, bf16[240,128]{1,0:T(8,128)(2,1)S(1)}, u32[]{:S(2)}, u32[]{:S(2)}) collective-permute-start(bf16[240,128]{1,0:T(8,128)(2,1)S(1)} %shard_map.120.refs_1_), channel_id=1, source_target_pairs={{0,25},{2,27},{4,29},{6,31},{8,17},{10,19},{12,21},{14,23},{16,9},... | collective-permute-start | bytes 184328 | tf_op jit(solution)/shard_map/ppermute | solution.py:417
  32.5 3.4 %collective-permute-start.16 = (bf16[240,128]{1,0:T(8,128)(2,1)S(1)}, bf16[240,128]{1,0:T(8,128)(2,1)S(1)}, u32[]{:S(2)}, u32[]{:S(2)}) collective-permute-start(bf16[240,128]{1,0:T(8,128)(2,1)S(1)} %shard_map.120.refs_1_), channel_id=1, source_target_pairs={{0,17},{2,19},{4,21},{6,23},{8,25},{10,27},{12,29},{14,31},{16,1},... | collective-permute-start | bytes 184328 | tf_op jit(solution)/shard_map/ppermute | solution.py:417
  33.9 2.4 %collective-permute-start.15 = (bf16[240,128]{1,0:T(8,128)(2,1)S(1)}, bf16[240,128]{1,0:T(8,128)(2,1)S(1)}, u32[]{:S(2)}, u32[]{:S(2)}) collective-permute-start(bf16[240,128]{1,0:T(8,128)(2,1)S(1)} %shard_map.120.refs_1_), channel_id=1, source_target_pairs={{0,9},{2,11},{4,13},{6,15},{8,1},{10,3},{12,5},{14,7},{16,25},{18,... | collective-permute-start | bytes 184328 | tf_op jit(solution)/shard_map/ppermute | solution.py:417
  33.9 2.4 %collective-permute-start.14 = (bf16[240,128]{1,0:T(8,128)(2,1)S(1)}, bf16[240,128]{1,0:T(8,128)(2,1)S(1)}, u32[]{:S(2)}, u32[]{:S(2)}) collective-permute-start(bf16[240,128]{1,0:T(8,128)(2,1)S(1)} %shard_map.120.refs_1_), channel_id=1, source_target_pairs={{0,1},{1,0},{2,3},{3,2},{4,5},{5,4},{6,7},{7,6},{8,9},{9,8},{10,11... | collective-permute-start | bytes 184328 | tf_op jit(solution)/shard_map/ppermute | solution.py:410
  37.0 5.5 %collective-permute-start.21 = (bf16[912,128]{1,0:T(8,128)(2,1)S(1)}, bf16[912,128]{1,0:T(8,128)(2,1)S(1)}, u32[]{:S(2)}, u32[]{:S(2)}) collective-permute-start(bf16[912,128]{1,0:T(8,128)(2,1)S(1)} %shard_map.121.refs_0_), channel_id=1, source_target_pairs={{1,2},{3,0},{5,6},{7,4},{9,10},{11,8},{13,14},{15,12},{17,18},{19,... | collective-permute-start | bytes 700424 | tf_op jit(solution)/shard_map/ppermute | solution.py:417
  38.1 7.6 %collective-permute-start.20 = (bf16[912,128]{1,0:T(8,128)(2,1)S(1)}, bf16[912,128]{1,0:T(8,128)(2,1)S(1)}, u32[]{:S(2)}, u32[]{:S(2)}) collective-permute-start(bf16[912,128]{1,0:T(8,128)(2,1)S(1)} %shard_map.121.refs_0_), channel_id=1, source_target_pairs={{1,6},{3,4},{5,2},{7,0},{9,14},{11,12},{13,10},{15,8},{17,22},{19,... | collective-permute-start | bytes 700424 | tf_op jit(solution)/shard_map/ppermute | solution.py:417
  38.4 8.0 %collective-permute-start.18 = (bf16[912,128]{1,0:T(8,128)(2,1)S(1)}, bf16[912,128]{1,0:T(8,128)(2,1)S(1)}, u32[]{:S(2)}, u32[]{:S(2)}) collective-permute-start(bf16[912,128]{1,0:T(8,128)(2,1)S(1)} %shard_map.121.refs_0_), channel_id=1, source_target_pairs={{1,4},{3,6},{5,0},{7,2},{9,12},{11,14},{13,8},{15,10},{17,20},{19,... | collective-permute-start | bytes 700424 | tf_op jit(solution)/shard_map/ppermute | solution.py:417
  39.7 6.7 %collective-permute-start.22 = (bf16[912,128]{1,0:T(8,128)(2,1)S(1)}, bf16[912,128]{1,0:T(8,128)(2,1)S(1)}, u32[]{:S(2)}, u32[]{:S(2)}) collective-permute-start(bf16[912,128]{1,0:T(8,128)(2,1)S(1)} %shard_map.121.refs_0_), channel_id=1, source_target_pairs={{0,1},{1,0},{2,3},{3,2},{4,5},{5,4},{6,7},{7,6},{8,9},{9,8},{10,11... | collective-permute-start | bytes 700424 | tf_op jit(solution)/shard_map/ppermute | solution.py:410
  42.6 3.8 %collective-permute-start.24 = (bf16[912,128]{1,0:T(8,128)(2,1)S(1)}, bf16[912,128]{1,0:T(8,128)(2,1)S(1)}, u32[]{:S(2)}, u32[]{:S(2)}) collective-permute-start(bf16[912,128]{1,0:T(8,128)(2,1)S(1)} %collective-permute-done.21.refs_2_), channel_id=1, source_target_pairs={{0,1},{1,0},{2,3},{3,2},{4,5},{5,4},{6,7},{7,6},{8,9},{9,8},{10,11... | collective-permute-start | bytes 700424 | tf_op jit(solution)/shard_map/ppermute | solution.py:410
  45.7 1.6 %collective-permute-start.23 = (bf16[912,128]{1,0:T(8,128)(2,1)S(1)}, bf16[912,128]{1,0:T(8,128)(2,1)S(1)}, u32[]{:S(2)}, u32[]{:S(2)}) collective-permute-start(bf16[912,128]{1,0:T(8,128)(2,1)S(1)} %shard_map.122), channel_id=1, source_target_pairs={{0,1},{1,0},{2,3},{3,2},{4,5},{5,4},{6,7},{7,6},{8,9},{9,8},{10,11... | collective-permute-start | bytes 700424 | tf_op jit(solution)/shard_map/ppermute | solution.py:410
  46.4 2.1 %collective-permute-start.19 = (bf16[912,128]{1,0:T(8,128)(2,1)S(1)}, bf16[912,128]{1,0:T(8,128)(2,1)S(1)}, u32[]{:S(2)}, u32[]{:S(2)}) collective-permute-start(bf16[912,128]{1,0:T(8,128)(2,1)S(1)} %collective-permute-done.18.refs_0_), channel_id=1, source_target_pairs={{0,1},{1,0},{2,3},{3,2},{4,5},{5,4},{6,7},{7,6},{8,9},{9,8},{10,11... | collective-permute-start | bytes 700424 | tf_op jit(solution)/shard_map/ppermute | solution.py:410

commit v5 on v4

--- a/solution.py
+++ b/solution.py
@@ -323,15 +323,18 @@
             keep[rows:, :] = total
 
 
-def finish_kernel(scale, *refs):
-    keep, received, out = refs[0], refs[1:-1], refs[-1]
+def gather_kernel(*refs):
+    *received, out = refs
+    rows = received[0].shape[0] - BIAS_ROWS
+    out[:rows, :] = sum(ref[:rows, :].astype(F32) for ref in received)
+    out[rows:, :] = sum(widened(ref[rows:, :]) for ref in received)
+
+
+def finish_kernel(scale, keep, more, out):
     rows = out.shape[0] - BIAS_ROWS
-    block, total = keep[:rows, :], keep[rows:, :]
-    for ref in received:
-        block = block + ref[:rows, :].astype(F32)
-        total = total + widened(ref[rows:, :])
-    out[:rows, :] = (block * scale).astype(BF16)
-    out[rows:, :] = narrowed(total * scale)
+    total = (keep[...] + more[...]) * scale
+    out[:rows, :] = total[:rows].astype(BF16)
+    out[rows:, :] = narrowed(total[rows:])
 
 
 def place_kernel(level, taker, given, *refs):
@@ -354,14 +357,14 @@
 
 
 def spread_kernel(steps, level, taker, pieces, *refs):
-    count = len(steps)
-    ends = steps[-1] != 0 and count == 1
+    count, starts = len(steps), steps[0] == 0
+    ends = steps[-1] == steps_of(level)[-1]
     digit, core = digit_of(level), place_of()[1]
     direct, passed, refs = refs[:count], refs[count : 2 * count], refs[2 * count :]
-    before, refs = (refs[0], refs[3:]) if ends else (None, refs)
+    before, refs = (None, refs) if starts else (refs[0], refs[3:])
     (conv, proj), refs = refs[:2], refs[2:]
     bias_out, (wide_conv, wide_proj, wide_bias, sems) = refs[:-4], refs[-4:]
-    bias = before[...] if ends else jnp.zeros((SUBLANES, LANES), F32)
+    bias = jnp.zeros((SUBLANES, LANES), F32) if starts else before[...]
     copies = []
 
     def send(source, target, *at):
@@ -452,10 +455,11 @@
             for k in steps_of(levels[level])
         ]
         source = 1 - source
+    (more,) = call(gather_kernel, [held(F32, rows + SUBLANES, LANES)], received, flops=1000000000)
     (part,) = call(
         functools.partial(finish_kernel, scale),
         [held(BF16, rows + BIAS_ROWS, LANES)],
-        (keep, *received),
+        (keep, more),
         flops=3000000000,
         after=ready if len(levels) == 1 else (),
     )
@@ -487,28 +491,36 @@
             pltpu.SemaphoreType.DMA((count + 1, 2)),
         ]
 
-    early, last = [0, *turn[:-1]], turn[-1]
-    forwarded = [given]
-    for k in early[1:]:
+    def spread(steps, forwarded, state):
+        ends = steps[-1] == turn[-1]
+        biases = [shape(F32, 1, w) for w in widths] if ends else [held(F32, SUBLANES, LANES)]
+        at = 2 * len(steps) + 1
+        conv, proj, *bias = call(
+            functools.partial(spread_kernel, steps, levels[0], taker, pieces),
+            whole + biases,
+            (*[parts[k] for k in steps], *forwarded, *state),
+            scratch=room(len(steps)),
+            far=(-1, -2, -3, -4, at, at + 1) if ends else (-1, -2, at, at + 1),
+            alias={at: 0, at + 1: 1} if state else None,
+        )
+        return (*bias, conv, proj)
+
+    state = spread([0], [given], ())
+    forwarded = []
+    for k in turn:
         message = parts[k]
+        after = ()
         if k == turn[0]:
-            (message,) = call(copy_kernel, [held(BF16, *message.shape)], (message,), after=fill(4, ()))
+            after = fill(4, ())
+        if k == turn[-2:][0]:
+            after = (*after, state[0])
+        if after:
+            (message,) = call(copy_kernel, [held(BF16, *message.shape)], (message,), after=after)
         forwarded.append(swapped(message))
-    conv, proj, bias = call(
-        functools.partial(spread_kernel, early, levels[0], taker, pieces),
-        whole + [held(F32, SUBLANES, LANES)],
-        (*[parts[k] for k in early], *forwarded),
-        scratch=room(len(early)),
-        far=(-1, -2),
-    )
-    return call(
-        functools.partial(spread_kernel, [last], levels[0], taker, pieces),
-        whole + [shape(F32, 1, w) for w in widths],
-        (parts[last], swapped(parts[last]), bias, conv, proj),
-        scratch=room(1),
-        far=(-1, -2, -3, -4, 3, 4),
-        alias={3: 0, 4: 1},
-    )
+    if len(turn) > 1:
+        state = spread(turn[:-1], forwarded[:-1], state)
+    conv_bias, proj_bias, conv, proj = spread(turn[-1:], forwarded[-1:], state)
+    return conv, proj, conv_bias, proj_bias
 
 
 def local(signal, conv_weight, conv_bias, out_weight, out_bias, cotangent):

time: 49.6 us -> 48.8 us (0.984)
  starting transfers between devices: 18.1 us -> 17 us
  Pallas kernels: 10.5 us -> 11.2 us
    ppermute x12, waiting for transfers between devices: 11.9 us -> 10.3 us  [crossed(): return lax.ppermute(array, BOTH, pairs)]
    ppermute x12, starting transfers between devices: 6.83 us -> 5.67 us  [crossed(): return lax.ppermute(array, BOTH, pairs)]
    ppermute x1, waiting for transfers between devices: 0.56 us -> 1.7 us  [fill(): results['incoming'] = lax.ppermute(onward, 'tm', plane_pairs())]
    pallas_call x16 -> x19, Pallas kernels: 10.5 us -> 11.2 us  [call(): pl.pallas_call(inner, out_shape=out_shape, in_specs=ins + [ANY] * len(aft...]
    ppermute x9, starting transfers between devices: 3.71 us -> 3.16 us  [swapped(): return lax.ppermute(array, BOTH, [(i, i ^ 1) for i in range(2 * chips)])]
    ppermute x1, starting transfers between devices: 0.79 us -> 1.33 us  [fill(): results['incoming'] = lax.ppermute(onward, 'tm', plane_pairs())]
  transfers between devices with their start and end apart: 25 -> 25, of which waited for: 16 -> 17; matrix products, arithmetic and copies ran while one was open for 0% -> 0% of each run, Pallas kernels for 17% -> 19%
where the time goes in v5:
time: 48.8 us; the launch traced here: 48.6 us
  waiting for transfers between devices  17.9 us (37%)
  starting transfers between devices  17 us (35%)
  Pallas kernels  11.2 us (23%)
  local copies, waits for them, and re-layouts  1.67 us (3%)
  between operations  0.82 us (2%)
    pallas_call x19, Pallas kernels, call(): pl.pallas_call(inner, out_shape=out_shape, in_specs=ins + [ANY] * len(aft...  11.2 us
    ppermute x12, waiting for transfers between devices, crossed(): return lax.ppermute(array, BOTH, pairs)  10.3 us
    ppermute x12, starting transfers between devices, crossed(): return lax.ppermute(array, BOTH, pairs)  5.67 us
    ppermute x2, starting transfers between devices, local(): lax.ppermute(signal[0, rows - n * STEP:rows - n * STEP + STEP], 'tm', [(i...  4.48 us
    ppermute x2, waiting for transfers between devices, local(): lax.ppermute(signal[0, rows - n * STEP:rows - n * STEP + STEP], 'tm', [(i...  4.05 us
    ppermute x9, starting transfers between devices, swapped(): return lax.ppermute(array, BOTH, [(i, i ^ 1) for i in range(2 * chips)])  3.16 us
    ppermute x1, starting transfers between devices, fill(): results['relayed'] = lax.ppermute(results['back'], BOTH, relay_pairs())  2.33 us
    ppermute x9, waiting for transfers between devices, swapped(): return lax.ppermute(array, BOTH, [(i, i ^ 1) for i in range(2 * chips)])  1.85 us
  transfers between devices with their start and end apart: 25, of which 17 were waited for; matrix products, arithmetic and copies ran while one was open for 0% of the time, Pallas kernels for 19%

profile of v5, /device:TPU:0, one launch (start us, length us, event | category | flops | bytes accessed | tf_op | source)
XLA Modules:
  0.0 48.6 jit_solution(760860186832007972)
XLA Ops:
  0.6 1.0 %slice_bitcast_fusion = (bf16[256,256]{1,0:T(8,128)(2,1)S(1)}, bf16[256,256]{1,0:T(8,128)(2,1)S(1)}) fusion(bf16[1,1024,256]{2,1,0:T(8,128)(2,1)} %param.6), kind=kLoop, calls=%fused_computation | loop fusion | bytes 524288 | tf_op jit(solution)/shard_map/squeeze | solution.py:540
  1.6 3.0 %collective-permute-start = (bf16[256,256]{1,0:T(8,128)(2,1)S(1)}, bf16[256,256]{1,0:T(8,128)(2,1)S(1)}, u32[]{:S(2)}, u32[]{:S(2)}) collective-permute-start(bf16[256,256]{1,0:T(8,128)(2,1)S(1)} %get-tuple-element.99), channel_id=1, source_target_pairs={{0,2},{2,4},{4,6},{6,8},{8,10},{10,12},{12,14},{14,16},{16,18},{18... | collective-permute-start | bytes 393224 | tf_op jit(solution)/shard_map/ppermute | solution.py:539
  4.6 1.5 %collective-permute-start.1 = (bf16[256,256]{1,0:T(8,128)(2,1)S(1)}, bf16[256,256]{1,0:T(8,128)(2,1)S(1)}, u32[]{:S(2)}, u32[]{:S(2)}) collective-permute-start(bf16[256,256]{1,0:T(8,128)(2,1)S(1)} %get-tuple-element.98), channel_id=1, source_target_pairs={{0,2},{2,4},{4,6},{6,8},{8,10},{10,12},{12,14},{14,16},{16,18},{18... | collective-permute-start | bytes 393224 | tf_op jit(solution)/shard_map/ppermute | solution.py:539
  6.1 0.7 %copy-done = f32[512]{0:T(512)S(1)} copy-done((f32[512]{0:T(512)S(1)}, f32[512]{0:T(512)}, u32[]{:S(2)}) %copy-start) | copy-done | bytes 2072
  6.8 3.3 %shard_map.109 = (bf16[1024,256]{1,0:T(8,128)(2,1)S(1)}, bf16[768,512]{1,0:T(8,128)(2,1)S(1)}, bf16[256,256]{1,0:T(8,128)(2,1)S(1)}, bf16[1024,256]{1,0:T(8,128)...) custom-call(bf16[1024,256]{1,0:T(8,128)(2,1)} %bitcast.14, ...), custom_call_target="tpu_custom_call" | custom-call | bytes 8 | tf_op jit(solution)/shard_map/pallas_call | solution.py:37
  10.1 2.8 %collective-permute-done.refs_0_ = bf16[256,256]{1,0:T(8,128)(2,1)S(1)} collective-permute-done((bf16[256,256]{1,0:T(8,128)(2,1)S(1)}, bf16[256,256]{1,0:T(8,128)(2,1)S(1)}, u32[]{:S(2)}, u32[]{:S(2)}) %collective-permute-start) | collective-permute-done | bytes 131104 | tf_op jit(solution)/shard_map/ppermute | solution.py:539
  12.9 0.7 %shard_map.110 = (bf16[256,256]{1,0:T(8,128)(2,1)S(1)}, bf16[256,512]{1,0:T(8,128)(2,1)S(1)}, f32[768,512]{1,0:T(8,128)S(1)}, f32[256,256]{1,0:T(8,128)S(1)}, f32[8,768]{1,0:T(8,128)S(1)}) custom-call(bf16[256,256]{1,0:T(8,128)(2,1)S(1)} %collective-permute-done.refs_0_, bf16[1024,256]{1,0:T(8,128)(2,1)S(1)} %get-tuple-element.52.refs_1_.refs_2_.refs_0_, ...), custom_call_target="tpu_custom_call" | custom-call | bytes 8 | tf_op jit(solution)/shard_map/pallas_call | solution.py:37
  13.7 1.2 %collective-permute-done.1.refs_1_ = bf16[256,256]{1,0:T(8,128)(2,1)S(1)} collective-permute-done((bf16[256,256]{1,0:T(8,128)(2,1)S(1)}, bf16[256,256]{1,0:T(8,128)(2,1)S(1)}, u32[]{:S(2)}, u32[]{:S(2)}) %collective-permute-start.1) | collective-permute-done | bytes 131104 | tf_op jit(solution)/shard_map/ppermute | solution.py:539
  14.9 1.0 %shard_map.111 = (bf16[256,256]{1,0:T(8,128)(2,1)S(1)}, bf16[256,512]{1,0:T(8,128)(2,1)S(1)}, f32[904,128]{1,0:T(8,128)S(1)}, f32[904,128]{1,0:T(8,128)S(1)}, f3...) custom-call(bf16[256,256]{1,0:T(8,128)(2,1)S(1)} %collective-permute, ...), custom_call_target="tpu_custom_call" | custom-call | bytes 8 | tf_op jit(solution)/shard_map/pallas_call | solution.py:37
  15.9 0.1 collective-permute-start.2
  16.0 0.5 %collective-permute-start.4 = (bf16[912,128]{1,0:T(8,128)(2,1)S(1)}, bf16[912,128]{1,0:T(8,128)(2,1)S(1)}, u32[]{:S(2)}, u32[]{:S(2)}) collective-permute-start(bf16[912,128]{1,0:T(8,128)(2,1)S(1)} %get-tuple-element.76), channel_id=1, source_target_pairs={{0,1},{1,0},{2,3},{3,2},{4,5},{5,4},{6,7},{7,6},{8,9},{9,8},{10,11... | collective-permute-start | bytes 700424 | tf_op jit(solution)/shard_map/ppermute | solution.py:413
  16.5 0.1 collective-permute-start.6
  16.6 0.4 shard_map.114.refs_3_.refs_0_
  17.0 0.5 %collective-permute-done.2.received = bf16[912,128]{1,0:T(8,128)(2,1)S(1)} collective-permute-done((bf16[912,128]{1,0:T(8,128)(2,1)S(1)}, bf16[912,128]{1,0:T(8,128)(2,1)S(1)}, u32[]{:S(2)}, u32[]{:S(2)}) %collective-permute-start.2) | collective-permute-done | bytes 233504 | tf_op jit(solution)/shard_map/ppermute | solution.py:413
  17.6 0.2 collective-permute-done.4.refs_2_
  17.8 0.1 shard_map.115
  18.0 0.2 collective-permute-done.6.received
  18.3 2.3 %collective-permute-start.3 = (bf16[512,256]{1,0:T(8,128)(2,1)S(1)}, bf16[512,256]{1,0:T(8,128)(2,1)S(1)}, u32[]{:S(2)}, u32[]{:S(2)}) collective-permute-start(bf16[512,256]{1,0:T(8,128)(2,1)S(1)} %shard_map.114.refs_3_.refs_0_), channel_id=1, source_target_pairs={{0,24},{1,25},{2,3},{3,2},{4,5},{5,4},{6,7},{7,6},{8,0},{9,1},{10,... | collective-permute-start | bytes 786440 | tf_op jit(solution)/shard_map/ppermute | solution.py:580
  20.6 1.6 %shard_map.113 = (bf16[1024,256]{1,0:T(8,128)(2,1)}, f32[1024,256]{1,0:T(8,128)S(1)}, f32[8,128]{1,0:T(8,128)S(1)}) custom-call(bf16[1024,256]{1,0:T(8,128)(2,1)S(1)} %get-tuple-element.52.refs_1_.refs_2_.refs_0_, bf16[768,512]{1,0:T(8,128)(2,1)S(1)} %get-tuple-element.53.refs_2_.refs_3_.refs_1_, bf16[256,256]{1,0:T(8,128)(2,1)S(1)} %get-tuple-element.54.refs_2_, ...), custom_call_target="tpu_custom_call" | custom-call | bytes 8 | tf_op jit(solution)/shard_map/pallas_call | solution.py:37
  22.2 1.3 %collective-permute-done.8.refs_3_ = bf16[912,128]{1,0:T(8,128)(2,1)S(1)} collective-permute-done((bf16[912,128]{1,0:T(8,128)(2,1)S(1)}, bf16[912,128]{1,0:T(8,128)(2,1)S(1)}, u32[]{:S(2)}, u32[]{:S(2)}) %collective-permute-start.8) | collective-permute-done | bytes 233504 | tf_op jit(solution)/shard_map/ppermute | solution.py:420
  23.5 0.5 %collective-permute-done.7.refs_2_ = bf16[912,128]{1,0:T(8,128)(2,1)S(1)} collective-permute-done((bf16[912,128]{1,0:T(8,128)(2,1)S(1)}, bf16[912,128]{1,0:T(8,128)(2,1)S(1)}, u32[]{:S(2)}, u32[]{:S(2)}) %collective-permute-start.7) | collective-permute-done | bytes 233504 | tf_op jit(solution)/shard_map/ppermute | solution.py:420
  24.1 0.1 shard_map.117
  24.2 2.0 %collective-permute-start.11 = (bf16[240,128]{1,0:T(8,128)(2,1)S(1)}, bf16[240,128]{1,0:T(8,128)(2,1)S(1)}, u32[]{:S(2)}, u32[]{:S(2)}) collective-permute-start(bf16[240,128]{1,0:T(8,128)(2,1)S(1)} %get-tuple-element.85), channel_id=1, source_target_pairs={{1,24},{3,26},{5,28},{7,30},{9,16},{11,18},{13,20},{15,22},{17,8},... | collective-permute-start | bytes 184328 | tf_op jit(solution)/shard_map/ppermute | solution.py:420
  26.2 0.4 collective-permute-start.13
  26.6 1.0 %collective-permute-start.12 = (bf16[240,128]{1,0:T(8,128)(2,1)S(1)}, bf16[240,128]{1,0:T(8,128)(2,1)S(1)}, u32[]{:S(2)}, u32[]{:S(2)}) collective-permute-start(bf16[240,128]{1,0:T(8,128)(2,1)S(1)} %get-tuple-element.82.refs_2_), channel_id=1, source_target_pairs={{1,8},{3,10},{5,12},{7,14},{9,0},{11,2},{13,4},{15,6},{17,24},{19,... | collective-permute-start | bytes 184328 | tf_op jit(solution)/shard_map/ppermute | solution.py:420
  27.7 1.3 %collective-permute-start.9 = (bf16[512,256]{1,0:T(8,128)(2,1)S(1)}, bf16[512,256]{1,0:T(8,128)(2,1)S(1)}, u32[]{:S(2)}, u32[]{:S(2)}) collective-permute-start(bf16[512,256]{1,0:T(8,128)(2,1)S(1)} %shard_map.118), channel_id=1, source_target_pairs={{0,6},{2,0},{4,2},{6,4},{8,14},{10,8},{12,10},{14,12},{16,22},{18,... | collective-permute-start | bytes 786440 | tf_op jit(solution)/shard_map/ppermute | solution.py:600
  29.0 1.0 %collective-permute-done.11.refs_0_ = bf16[240,128]{1,0:T(8,128)(2,1)S(1)} collective-permute-done((bf16[240,128]{1,0:T(8,128)(2,1)S(1)}, bf16[240,128]{1,0:T(8,128)(2,1)S(1)}, u32[]{:S(2)}, u32[]{:S(2)}) %collective-permute-start.11) | collective-permute-done | bytes 61472 | tf_op jit(solution)/shard_map/ppermute | solution.py:420
  30.0 1.3 %collective-permute-done.13.refs_2_ = bf16[240,128]{1,0:T(8,128)(2,1)S(1)} collective-permute-done((bf16[240,128]{1,0:T(8,128)(2,1)S(1)}, bf16[240,128]{1,0:T(8,128)(2,1)S(1)}, u32[]{:S(2)}, u32[]{:S(2)}) %collective-permute-start.13) | collective-permute-done | bytes 61472 | tf_op jit(solution)/shard_map/ppermute | solution.py:420
  31.5 0.8 %collective-permute-start.16 = (bf16[240,128]{1,0:T(8,128)(2,1)S(1)}, bf16[240,128]{1,0:T(8,128)(2,1)S(1)}, u32[]{:S(2)}, u32[]{:S(2)}) collective-permute-start(bf16[240,128]{1,0:T(8,128)(2,1)S(1)} %shard_map.121.refs_1_), channel_id=1, source_target_pairs={{0,17},{2,19},{4,21},{6,23},{8,25},{10,27},{12,29},{14,31},{16,1},... | collective-permute-start | bytes 184328 | tf_op jit(solution)/shard_map/ppermute | solution.py:420
  32.3 0.5 %collective-permute-start.14 = (bf16[240,128]{1,0:T(8,128)(2,1)S(1)}, bf16[240,128]{1,0:T(8,128)(2,1)S(1)}, u32[]{:S(2)}, u32[]{:S(2)}) collective-permute-start(bf16[240,128]{1,0:T(8,128)(2,1)S(1)} %shard_map.121.refs_1_), channel_id=1, source_target_pairs={{0,1},{1,0},{2,3},{3,2},{4,5},{5,4},{6,7},{7,6},{8,9},{9,8},{10,11... | collective-permute-start | bytes 184328 | tf_op jit(solution)/shard_map/ppermute | solution.py:413
  32.8 0.6 %collective-permute-done.17.refs_4_ = bf16[240,128]{1,0:T(8,128)(2,1)S(1)} collective-permute-done((bf16[240,128]{1,0:T(8,128)(2,1)S(1)}, bf16[240,128]{1,0:T(8,128)(2,1)S(1)}, u32[]{:S(2)}, u32[]{:S(2)}) %collective-permute-start.17) | collective-permute-done | bytes 61472 | tf_op jit(solution)/shard_map/ppermute | solution.py:420
  33.3 0.8 %collective-permute-done.16.refs_3_ = bf16[240,128]{1,0:T(8,128)(2,1)S(1)} collective-permute-done((bf16[240,128]{1,0:T(8,128)(2,1)S(1)}, bf16[240,128]{1,0:T(8,128)(2,1)S(1)}, u32[]{:S(2)}, u32[]{:S(2)}) %collective-permute-start.16) | collective-permute-done | bytes 61472 | tf_op jit(solution)/shard_map/ppermute | solution.py:420
  34.1 0.6 %collective-permute-done.15.refs_2_ = bf16[240,128]{1,0:T(8,128)(2,1)S(1)} collective-permute-done((bf16[240,128]{1,0:T(8,128)(2,1)S(1)}, bf16[240,128]{1,0:T(8,128)(2,1)S(1)}, u32[]{:S(2)}, u32[]{:S(2)}) %collective-permute-start.15) | collective-permute-done | bytes 61472 | tf_op jit(solution)/shard_map/ppermute | solution.py:420
  34.7 1.7 %collective-permute-done.9.incoming.refs_5_ = bf16[512,256]{1,0:T(8,128)(2,1)S(1)} collective-permute-done((bf16[512,256]{1,0:T(8,128)(2,1)S(1)}, bf16[512,256]{1,0:T(8,128)(2,1)S(1)}, u32[]{:S(2)}, u32[]{:S(2)}) %collective-permute-start.9) | collective-permute-done | bytes 262176 | tf_op jit(solution)/shard_map/ppermute | solution.py:600
  36.5 0.7 %collective-permute-start.20 = (bf16[912,128]{1,0:T(8,128)(2,1)S(1)}, bf16[912,128]{1,0:T(8,128)(2,1)S(1)}, u32[]{:S(2)}, u32[]{:S(2)}) collective-permute-start(bf16[912,128]{1,0:T(8,128)(2,1)S(1)} %shard_map.122.refs_0_), channel_id=1, source_target_pairs={{1,6},{3,4},{5,2},{7,0},{9,14},{11,12},{13,10},{15,8},{17,22},{19,... | collective-permute-start | bytes 700424 | tf_op jit(solution)/shard_map/ppermute | solution.py:420
  37.2 1.6 %collective-permute-start.23 = (bf16[912,128]{1,0:T(8,128)(2,1)S(1)}, bf16[912,128]{1,0:T(8,128)(2,1)S(1)}, u32[]{:S(2)}, u32[]{:S(2)}) collective-permute-start(bf16[912,128]{1,0:T(8,128)(2,1)S(1)} %shard_map.122.refs_0_), channel_id=1, source_target_pairs={{0,1},{1,0},{2,3},{3,2},{4,5},{5,4},{6,7},{7,6},{8,9},{9,8},{10,11... | collective-permute-start | bytes 700424 | tf_op jit(solution)/shard_map/ppermute | solution.py:413
  38.8 0.5 %collective-permute-start.18 = (bf16[912,128]{1,0:T(8,128)(2,1)S(1)}, bf16[912,128]{1,0:T(8,128)(2,1)S(1)}, u32[]{:S(2)}, u32[]{:S(2)}) collective-permute-start(bf16[912,128]{1,0:T(8,128)(2,1)S(1)} %shard_map.122.refs_0_), channel_id=1, source_target_pairs={{1,4},{3,6},{5,0},{7,2},{9,12},{11,14},{13,8},{15,10},{17,20},{19,... | collective-permute-start | bytes 700424 | tf_op jit(solution)/shard_map/ppermute | solution.py:420
  39.3 0.9 %shard_map.119 = (bf16[1024,256]{1,0:T(8,128)(2,1)}, f32[8,128]{1,0:T(8,128)S(1)}) custom-call(f32[1024,256]{1,0:T(8,128)S(1)} %get-tuple-element.73.partial, bf16[512,256]{1,0:T(8,128)(2,1)S(1)} %collective-permute-done.9.incoming.refs_5_), custom_call_target="tpu_custom_call" | custom-call | bytes 8 | tf_op jit(solution)/shard_map/pallas_call | solution.py:37
  40.2 2.8 %collective-permute-done.20.refs_0_ = bf16[912,128]{1,0:T(8,128)(2,1)S(1)} collective-permute-done((bf16[912,128]{1,0:T(8,128)(2,1)S(1)}, bf16[912,128]{1,0:T(8,128)(2,1)S(1)}, u32[]{:S(2)}, u32[]{:S(2)}) %collective-permute-start.20) | collective-permute-done | bytes 233504 | tf_op jit(solution)/shard_map/ppermute | solution.py:420
  43.1 0.1 collective-permute-start.22
  43.1 0.9 %shard_map.124 = (f32[768,512]{1,0:T(8,128)}, f32[256,256]{1,0:T(8,128)}, f32[8,128]{1,0:T(8,128)S(1)}) custom-call(bf16[912,128]{1,0:T(8,128)(2,1)S(1)} %shard_map.122.refs_0_, bf16[912,128]{1,0:T(8,128)(2,1)S(1)} %collective-permute-done.23.refs_1_), custom_call_target="tpu_custom_call" | custom-call | bytes 8 | tf_op jit(solution)/shard_map/pallas_call | solution.py:37
  44.0 1.1 %collective-permute-done.21.refs_0_.refs_1_ = bf16[912,128]{1,0:T(8,128)(2,1)S(1)} collective-permute-done((bf16[912,128]{1,0:T(8,128)(2,1)S(1)}, bf16[912,128]{1,0:T(8,128)(2,1)S(1)}, u32[]{:S(2)}, u32[]{:S(2)}) %collective-permute-start.21) | collective-permute-done | bytes 233504 | tf_op jit(solution)/shard_map/ppermute | solution.py:420
  45.1 0.1 collective-permute-start.24
  45.2 0.2 collective-permute-done.18.refs_0_
  45.4 0.2 collective-permute-start.19
  45.7 1.0 %collective-permute-done.24.refs_3_ = bf16[912,128]{1,0:T(8,128)(2,1)S(1)} collective-permute-done((bf16[912,128]{1,0:T(8,128)(2,1)S(1)}, bf16[912,128]{1,0:T(8,128)(2,1)S(1)}, u32[]{:S(2)}, u32[]{:S(2)}) %collective-permute-start.24) | collective-permute-done | bytes 233504 | tf_op jit(solution)/shard_map/ppermute | solution.py:413
  46.7 1.0 %shard_map.126 = (f32[768,512]{1,0:T(8,128)}, f32[256,256]{1,0:T(8,128)}, f32[8,128]{1,0:T(8,128)S(1)}) custom-call(bf16[912,128]{1,0:T(8,128)(2,1)S(1)} %collective-permute-done.20.refs_0_, bf16[912,128]{1,0:T(8,128)(2,1)S(1)} %collective-permute-done.21.refs_0_.refs_1_, ...), custom_call_target="tpu_custom_call", output_to_operand_aliasing={{0}: (5, {}), {1}: (6, {})} | custom-call | bytes 8 | tf_op jit(solution)/shard_map/pallas_call | solution.py:37
  47.7 0.9 %shard_map.127 = (f32[768,512]{1,0:T(8,128)}, f32[256,256]{1,0:T(8,128)}, f32[1,512]{1,0:T(1,128)}, f32[1,256]{1,0:T(1,128)}) custom-call(bf16[912,128]{1,0:T(8,128)(2,1)S(1)} %collective-permute-done.18.refs_0_, bf16[912,128]{1,0:T(8,128)(2,1)S(1)} %collective-permute-done.19.refs_1_, ...), custom_call_target="tpu_custom_call", output_to_operand_aliasing={{0}: (3, {}), {1}: (4, {})} | custom-call | bytes 8 | tf_op jit(solution)/shard_map/pallas_call | solution.py:37
  (26 shorter events, 0.6 us)
Async XLA Ops:
  1.6 11.3 %collective-permute-start = (bf16[256,256]{1,0:T(8,128)(2,1)S(1)}, bf16[256,256]{1,0:T(8,128)(2,1)S(1)}, u32[]{:S(2)}, u32[]{:S(2)}) collective-permute-start(bf16[256,256]{1,0:T(8,128)(2,1)S(1)} %get-tuple-element.99), channel_id=1, source_target_pairs={{0,2},{2,4},{4,6},{6,8},{8,10},{10,12},{12,14},{14,16},{16,18},{18... | collective-permute-start | bytes 393224 | tf_op jit(solution)/shard_map/ppermute | solution.py:539
  4.6 10.3 %collective-permute-start.1 = (bf16[256,256]{1,0:T(8,128)(2,1)S(1)}, bf16[256,256]{1,0:T(8,128)(2,1)S(1)}, u32[]{:S(2)}, u32[]{:S(2)}) collective-permute-start(bf16[256,256]{1,0:T(8,128)(2,1)S(1)} %get-tuple-element.98), channel_id=1, source_target_pairs={{0,2},{2,4},{4,6},{6,8},{8,10},{10,12},{12,14},{14,16},{16,18},{18... | collective-permute-start | bytes 393224 | tf_op jit(solution)/shard_map/ppermute | solution.py:539
  6.1 0.7 %copy-start = (f32[512]{0:T(512)S(1)}, f32[512]{0:T(512)}, u32[]{:S(2)}) copy-start(f32[512]{0:T(512)} %param.8) | copy-start | bytes 6148
  15.9 1.6 %collective-permute-start.2 = (bf16[912,128]{1,0:T(8,128)(2,1)S(1)}, bf16[912,128]{1,0:T(8,128)(2,1)S(1)}, u32[]{:S(2)}, u32[]{:S(2)}) collective-permute-start(bf16[912,128]{1,0:T(8,128)(2,1)S(1)} %get-tuple-element.71), channel_id=1, source_target_pairs={{0,1},{1,0},{2,3},{3,2},{4,5},{5,4},{6,7},{7,6},{8,9},{9,8},{10,11... | collective-permute-start | bytes 700424 | tf_op jit(solution)/shard_map/ppermute | solution.py:413
  16.0 1.8 %collective-permute-start.4 = (bf16[912,128]{1,0:T(8,128)(2,1)S(1)}, bf16[912,128]{1,0:T(8,128)(2,1)S(1)}, u32[]{:S(2)}, u32[]{:S(2)}) collective-permute-start(bf16[912,128]{1,0:T(8,128)(2,1)S(1)} %get-tuple-element.76), channel_id=1, source_target_pairs={{0,1},{1,0},{2,3},{3,2},{4,5},{5,4},{6,7},{7,6},{8,9},{9,8},{10,11... | collective-permute-start | bytes 700424 | tf_op jit(solution)/shard_map/ppermute | solution.py:413
  16.5 1.7 %collective-permute-start.6 = (bf16[912,128]{1,0:T(8,128)(2,1)S(1)}, bf16[912,128]{1,0:T(8,128)(2,1)S(1)}, u32[]{:S(2)}, u32[]{:S(2)}) collective-permute-start(bf16[912,128]{1,0:T(8,128)(2,1)S(1)} %get-tuple-element.80), channel_id=1, source_target_pairs={{0,1},{1,0},{2,3},{3,2},{4,5},{5,4},{6,7},{7,6},{8,9},{9,8},{10,11... | collective-permute-start | bytes 700424 | tf_op jit(solution)/shard_map/ppermute | solution.py:413
  17.5 3.1 %copy-start.1 = (f32[256]{0:T(256)S(1)}, f32[256]{0:T(256)}, u32[]{:S(2)}) copy-start(f32[256]{0:T(256)} %param.10) | copy-start | bytes 3076
  17.5 6.0 %collective-permute-start.8 = (bf16[912,128]{1,0:T(8,128)(2,1)S(1)}, bf16[912,128]{1,0:T(8,128)(2,1)S(1)}, u32[]{:S(2)}, u32[]{:S(2)}) collective-permute-start(bf16[912,128]{1,0:T(8,128)(2,1)S(1)} %shard_map.112.refs_11_), channel_id=1, source_target_pairs={{0,5},{2,7},{4,1},{6,3},{8,13},{10,15},{12,9},{14,11},{16,21},{18,... | collective-permute-start | bytes 700424 | tf_op jit(solution)/shard_map/ppermute | solution.py:420
  17.9 5.6 %collective-permute-start.5 = (bf16[912,128]{1,0:T(8,128)(2,1)S(1)}, bf16[912,128]{1,0:T(8,128)(2,1)S(1)}, u32[]{:S(2)}, u32[]{:S(2)}) collective-permute-start(bf16[912,128]{1,0:T(8,128)(2,1)S(1)} %get-tuple-element.78), channel_id=1, source_target_pairs={{0,7},{2,5},{4,3},{6,1},{8,15},{10,13},{12,11},{14,9},{16,23},{18,... | collective-permute-start | bytes 700424 | tf_op jit(solution)/shard_map/ppermute | solution.py:420
  18.2 5.9 %collective-permute-start.7 = (bf16[912,128]{1,0:T(8,128)(2,1)S(1)}, bf16[912,128]{1,0:T(8,128)(2,1)S(1)}, u32[]{:S(2)}, u32[]{:S(2)}) collective-permute-start(bf16[912,128]{1,0:T(8,128)(2,1)S(1)} %shard_map.116), channel_id=1, source_target_pairs={{0,3},{2,1},{4,7},{6,5},{8,11},{10,9},{12,15},{14,13},{16,19},{18,... | collective-permute-start | bytes 700424 | tf_op jit(solution)/shard_map/ppermute | solution.py:420
  18.3 9.3 %collective-permute-start.3 = (bf16[512,256]{1,0:T(8,128)(2,1)S(1)}, bf16[512,256]{1,0:T(8,128)(2,1)S(1)}, u32[]{:S(2)}, u32[]{:S(2)}) collective-permute-start(bf16[512,256]{1,0:T(8,128)(2,1)S(1)} %shard_map.114.refs_3_.refs_0_), channel_id=1, source_target_pairs={{0,24},{1,25},{2,3},{3,2},{4,5},{5,4},{6,7},{7,6},{8,0},{9,1},{10,... | collective-permute-start | bytes 786440 | tf_op jit(solution)/shard_map/ppermute | solution.py:580
  24.2 5.8 %collective-permute-start.11 = (bf16[240,128]{1,0:T(8,128)(2,1)S(1)}, bf16[240,128]{1,0:T(8,128)(2,1)S(1)}, u32[]{:S(2)}, u32[]{:S(2)}) collective-permute-start(bf16[240,128]{1,0:T(8,128)(2,1)S(1)} %get-tuple-element.85), channel_id=1, source_target_pairs={{1,24},{3,26},{5,28},{7,30},{9,16},{11,18},{13,20},{15,22},{17,8},... | collective-permute-start | bytes 184328 | tf_op jit(solution)/shard_map/ppermute | solution.py:420
  26.2 5.1 %collective-permute-start.13 = (bf16[240,128]{1,0:T(8,128)(2,1)S(1)}, bf16[240,128]{1,0:T(8,128)(2,1)S(1)}, u32[]{:S(2)}, u32[]{:S(2)}) collective-permute-start(bf16[240,128]{1,0:T(8,128)(2,1)S(1)} %get-tuple-element.86), channel_id=1, source_target_pairs={{1,16},{3,18},{5,20},{7,22},{9,24},{11,26},{13,28},{15,30},{17,0},... | collective-permute-start | bytes 184328 | tf_op jit(solution)/shard_map/ppermute | solution.py:420
  26.6 4.7 %collective-permute-start.12 = (bf16[240,128]{1,0:T(8,128)(2,1)S(1)}, bf16[240,128]{1,0:T(8,128)(2,1)S(1)}, u32[]{:S(2)}, u32[]{:S(2)}) collective-permute-start(bf16[240,128]{1,0:T(8,128)(2,1)S(1)} %get-tuple-element.82.refs_2_), channel_id=1, source_target_pairs={{1,8},{3,10},{5,12},{7,14},{9,0},{11,2},{13,4},{15,6},{17,24},{19,... | collective-permute-start | bytes 184328 | tf_op jit(solution)/shard_map/ppermute | solution.py:420
  27.6 3.8 %collective-permute-start.10 = (f32[232,128]{1,0:T(8,128)S(1)}, f32[232,128]{1,0:T(8,128)S(1)}, u32[]{:S(2)}, u32[]{:S(2)}) collective-permute-start(f32[232,128]{1,0:T(8,128)S(1)} %get-tuple-element.84), channel_id=1, source_target_pairs={{0,1},{1,0},{2,3},{3,2},{4,5},{5,4},{6,7},{7,6},{8,9},{9,8},{10,11... | collective-permute-start | bytes 356360 | tf_op jit(solution)/shard_map/ppermute | solution.py:413
  27.7 8.8 %collective-permute-start.9 = (bf16[512,256]{1,0:T(8,128)(2,1)S(1)}, bf16[512,256]{1,0:T(8,128)(2,1)S(1)}, u32[]{:S(2)}, u32[]{:S(2)}) collective-permute-start(bf16[512,256]{1,0:T(8,128)(2,1)S(1)} %shard_map.118), channel_id=1, source_target_pairs={{0,6},{2,0},{4,2},{6,4},{8,14},{10,8},{12,10},{14,12},{16,22},{18,... | collective-permute-start | bytes 786440 | tf_op jit(solution)/shard_map/ppermute | solution.py:600
  31.4 1.9 %collective-permute-start.17 = (bf16[240,128]{1,0:T(8,128)(2,1)S(1)}, bf16[240,128]{1,0:T(8,128)(2,1)S(1)}, u32[]{:S(2)}, u32[]{:S(2)}) collective-permute-start(bf16[240,128]{1,0:T(8,128)(2,1)S(1)} %shard_map.121.refs_1_), channel_id=1, source_target_pairs={{0,25},{2,27},{4,29},{6,31},{8,17},{10,19},{12,21},{14,23},{16,9},... | collective-permute-start | bytes 184328 | tf_op jit(solution)/shard_map/ppermute | solution.py:420
  31.5 2.7 %collective-permute-start.16 = (bf16[240,128]{1,0:T(8,128)(2,1)S(1)}, bf16[240,128]{1,0:T(8,128)(2,1)S(1)}, u32[]{:S(2)}, u32[]{:S(2)}) collective-permute-start(bf16[240,128]{1,0:T(8,128)(2,1)S(1)} %shard_map.121.refs_1_), channel_id=1, source_target_pairs={{0,17},{2,19},{4,21},{6,23},{8,25},{10,27},{12,29},{14,31},{16,1},... | collective-permute-start | bytes 184328 | tf_op jit(solution)/shard_map/ppermute | solution.py:420
  32.3 2.4 %collective-permute-start.15 = (bf16[240,128]{1,0:T(8,128)(2,1)S(1)}, bf16[240,128]{1,0:T(8,128)(2,1)S(1)}, u32[]{:S(2)}, u32[]{:S(2)}) collective-permute-start(bf16[240,128]{1,0:T(8,128)(2,1)S(1)} %shard_map.121.refs_1_), channel_id=1, source_target_pairs={{0,9},{2,11},{4,13},{6,15},{8,1},{10,3},{12,5},{14,7},{16,25},{18,... | collective-permute-start | bytes 184328 | tf_op jit(solution)/shard_map/ppermute | solution.py:420
  32.3 2.4 %collective-permute-start.14 = (bf16[240,128]{1,0:T(8,128)(2,1)S(1)}, bf16[240,128]{1,0:T(8,128)(2,1)S(1)}, u32[]{:S(2)}, u32[]{:S(2)}) collective-permute-start(bf16[240,128]{1,0:T(8,128)(2,1)S(1)} %shard_map.121.refs_1_), channel_id=1, source_target_pairs={{0,1},{1,0},{2,3},{3,2},{4,5},{5,4},{6,7},{7,6},{8,9},{9,8},{10,11... | collective-permute-start | bytes 184328 | tf_op jit(solution)/shard_map/ppermute | solution.py:413
  36.5 6.5 %collective-permute-start.20 = (bf16[912,128]{1,0:T(8,128)(2,1)S(1)}, bf16[912,128]{1,0:T(8,128)(2,1)S(1)}, u32[]{:S(2)}, u32[]{:S(2)}) collective-permute-start(bf16[912,128]{1,0:T(8,128)(2,1)S(1)} %shard_map.122.refs_0_), channel_id=1, source_target_pairs={{1,6},{3,4},{5,2},{7,0},{9,14},{11,12},{13,10},{15,8},{17,22},{19,... | collective-permute-start | bytes 700424 | tf_op jit(solution)/shard_map/ppermute | solution.py:420
  37.2 5.9 %collective-permute-start.23 = (bf16[912,128]{1,0:T(8,128)(2,1)S(1)}, bf16[912,128]{1,0:T(8,128)(2,1)S(1)}, u32[]{:S(2)}, u32[]{:S(2)}) collective-permute-start(bf16[912,128]{1,0:T(8,128)(2,1)S(1)} %shard_map.122.refs_0_), channel_id=1, source_target_pairs={{0,1},{1,0},{2,3},{3,2},{4,5},{5,4},{6,7},{7,6},{8,9},{9,8},{10,11... | collective-permute-start | bytes 700424 | tf_op jit(solution)/shard_map/ppermute | solution.py:413
  38.8 6.3 %collective-permute-start.21 = (bf16[912,128]{1,0:T(8,128)(2,1)S(1)}, bf16[912,128]{1,0:T(8,128)(2,1)S(1)}, u32[]{:S(2)}, u32[]{:S(2)}) collective-permute-start(bf16[912,128]{1,0:T(8,128)(2,1)S(1)} %shard_map.122.refs_0_), channel_id=1, source_target_pairs={{1,2},{3,0},{5,6},{7,4},{9,10},{11,8},{13,14},{15,12},{17,18},{19,... | collective-permute-start | bytes 700424 | tf_op jit(solution)/shard_map/ppermute | solution.py:420
  38.8 6.6 %collective-permute-start.18 = (bf16[912,128]{1,0:T(8,128)(2,1)S(1)}, bf16[912,128]{1,0:T(8,128)(2,1)S(1)}, u32[]{:S(2)}, u32[]{:S(2)}) collective-permute-start(bf16[912,128]{1,0:T(8,128)(2,1)S(1)} %shard_map.122.refs_0_), channel_id=1, source_target_pairs={{1,4},{3,6},{5,0},{7,2},{9,12},{11,14},{13,8},{15,10},{17,20},{19,... | collective-permute-start | bytes 700424 | tf_op jit(solution)/shard_map/ppermute | solution.py:420
  43.1 2.6 %collective-permute-start.22 = (bf16[912,128]{1,0:T(8,128)(2,1)S(1)}, bf16[912,128]{1,0:T(8,128)(2,1)S(1)}, u32[]{:S(2)}, u32[]{:S(2)}) collective-permute-start(bf16[912,128]{1,0:T(8,128)(2,1)S(1)} %shard_map.123), channel_id=1, source_target_pairs={{0,1},{1,0},{2,3},{3,2},{4,5},{5,4},{6,7},{7,6},{8,9},{9,8},{10,11... | collective-permute-start | bytes 700424 | tf_op jit(solution)/shard_map/ppermute | solution.py:413
  45.1 1.6 %collective-permute-start.24 = (bf16[912,128]{1,0:T(8,128)(2,1)S(1)}, bf16[912,128]{1,0:T(8,128)(2,1)S(1)}, u32[]{:S(2)}, u32[]{:S(2)}) collective-permute-start(bf16[912,128]{1,0:T(8,128)(2,1)S(1)} %shard_map.125), channel_id=1, source_target_pairs={{0,1},{1,0},{2,3},{3,2},{4,5},{5,4},{6,7},{7,6},{8,9},{9,8},{10,11... | collective-permute-start | bytes 700424 | tf_op jit(solution)/shard_map/ppermute | solution.py:413
  45.4 2.3 %collective-permute-start.19 = (bf16[912,128]{1,0:T(8,128)(2,1)S(1)}, bf16[912,128]{1,0:T(8,128)(2,1)S(1)}, u32[]{:S(2)}, u32[]{:S(2)}) collective-permute-start(bf16[912,128]{1,0:T(8,128)(2,1)S(1)} %collective-permute-done.18.refs_0_), channel_id=1, source_target_pairs={{0,1},{1,0},{2,3},{3,2},{4,5},{5,4},{6,7},{7,6},{8,9},{9,8},{10,11... | collective-permute-start | bytes 700424 | tf_op jit(solution)/shard_map/ppermute | solution.py:413

commit v6 on v5

--- a/solution.py
+++ b/solution.py
@@ -142,7 +142,7 @@
     grad_bias[:, 2 * channels :] = dot(ones, cot[...])[:SUBLANES]
 
 
-def chunk(begin, past, signal, weight, cot, preact_in, dmixed_in, conv_in, proj_in, bias_in, mixed_out, dpre_out, conv, proj):
+def chunk(begin, taps, past, signal, weight, cot, preact_in, dmixed_in, conv_in, proj_in, bias_in, mixed_out, dpre_out, conv, proj):
     channels = signal.shape[1]
     here = slice(begin, begin + STEP)
     own = begin // STEP + 1
@@ -150,7 +150,7 @@
         jnp.where(lax.axis_index("tm") == 0, jnp.zeros_like(block), block[...]) for block in past
     ]
     preact = preact_in[here, :]
-    for k in range(own, TAPS):
+    for k in taps:
         preact = preact + dot(past[k - own], weight[k * channels : (k + 1) * channels, :])
     mixed, dfiltered, dgated = gates(preact, dmixed_in[here, :])
     mixed_out[...] = mixed
@@ -167,8 +167,12 @@
 
 
 def middle_kernel(begin, *refs):
-    *ins, grad_bias = refs
-    grad_bias[...] = chunk(begin, ins[:1], *ins[1:])
+    *ins, grad_bias, ahead = refs
+    near, signal, weight, _, preact_in = ins[:5]
+    grad_bias[...] = chunk(begin, range(begin // STEP + 1, TAPS), ins[:1], *ins[1:])
+    channels = signal.shape[1]
+    block = jnp.where(lax.axis_index("tm") == 0, jnp.zeros_like(near), near[...])
+    ahead[...] = preact_in[:STEP, :] + dot(block, weight[channels : 2 * channels, :])
 
 
 def early_kernel(level, pieces, *refs):
@@ -177,7 +181,7 @@
     ins, (mixed_out, dpre_out), refs = refs[: TAPS + 7], refs[TAPS + 7 : TAPS + 9], refs[TAPS + 9 :]
     own, offered = refs[:radix], refs[radix : 2 * radix - 1]
     grad_conv, grad_proj = refs[2 * radix - 1 :]
-    bias = chunk(0, ins[: TAPS - 1], *ins[TAPS - 1 :], mixed_out, dpre_out, grad_conv, grad_proj)
+    bias = chunk(0, range(2, TAPS), ins[: TAPS - 1], *ins[TAPS - 1 :], mixed_out, dpre_out, grad_conv, grad_proj)
     conv_in, proj_in = ins[-3], ins[-2]
     for grad, filled in ((grad_conv, conv_in.shape[0]), (grad_proj, proj_in.shape[0])):
         if filled < grad.shape[0]:
@@ -185,7 +189,8 @@
     lines = [bias[:1, c : c + LANES] for c in range(0, bias.shape[1], LANES)]
     lines += [jnp.zeros((1, LANES), F32)] * (SUBLANES - len(lines))
     bias = jnp.concatenate(lines, 0)
-    for k in range(radix):
+
+    def pack(k, target, kind):
         at = 0
         for piece in range(pieces // radix):
             index = (digit ^ k) * (pieces // radix) + piece
@@ -193,20 +198,23 @@
                 height = grad.shape[0] // pieces
                 begin = pl.multiple_of(index * height, 16)
                 for column in range(0, grad.shape[1], LANES):
-                    block = grad[pl.ds(begin, height), column : column + LANES]
-                    own[k][at : at + height, :] = block
-                    if k in turn[1:]:
-                        offered[turn.index(k)][at : at + height, :] = block.astype(BF16)
+                    target[at : at + height, :] = grad[
+                        pl.ds(begin, height), column : column + LANES
+                    ].astype(kind)
                     at += height
-        own[k][at:, :] = bias
-        if k in turn[1:]:
-            offered[turn.index(k)][at:, :] = narrowed(bias)
-    offered[0][at:, :] = narrowed(bias)
-    for mine, k in ((0, 0), (1, turn[0])):
-
-        @pl.when(core == mine)
-        def _():
-            offered[0][:at, :] = own[k][:at, :].astype(BF16)
+        target[at:, :] = bias if kind == F32 else narrowed(bias)
+
+    @pl.when(core == 0)
+    def _():
+        pack(0, offered[0], BF16)
+        for k in turn:
+            pack(k, own[k], F32)
+
+    @pl.when(core == 1)
+    def _():
+        for k, target in zip(turn, offered):
+            pack(k, target, BF16)
+        pack(0, own[0], F32)
 
 
 def back_kernel(*refs):
@@ -557,9 +565,9 @@
         far=(0, 1, 3, 4),
     )
     grads = [held(F32, TAPS * channels, wide), held(F32, channels, channels)]
-    mixed_middle, dpre_middle, conv, proj, bias = call(
+    mixed_middle, dpre_middle, conv, proj, bias, ahead = call(
         functools.partial(middle_kernel, STEP),
-        [held(BF16, STEP, channels), held(BF16, STEP, wide), *grads, held(F32, SUBLANES, wide + channels)],
+        [held(BF16, STEP, channels), held(BF16, STEP, wide), *grads, held(F32, SUBLANES, wide + channels), held(F32, STEP, wide)],
         (history[0], x, weight, cot, preact, dmixed, conv, proj, bias),
     )
     mixed_early, dpre_early, *pieces = call(
@@ -567,7 +575,7 @@
         [held(BF16, STEP, channels), held(BF16, STEP, wide)]
         + [held(F32, piece + SUBLANES, LANES)] * radix
         + [held(BF16, piece + BIAS_ROWS, LANES)] * (radix - 1),
-        (*history, x, weight, cot, preact, dmixed, conv, proj, bias),
+        (*history, x, weight, cot, ahead, dmixed, conv, proj, bias),
         scratch=[pltpu.VMEM((chips * h, w), F32) for h, w in zip(heights, widths)],
     )
     results = {}

time: 48.8 us -> 48.6 us (level)
  no operation moved by 1% of the time
where the time goes in v6:
time: 48.6 us; the launch traced here: 48.4 us
  waiting for transfers between devices  17.9 us (37%)
  starting transfers between devices  17 us (35%)
  Pallas kernels  11.1 us (23%)
  local copies, waits for them, and re-layouts  1.67 us (3%)
  between operations  0.82 us (2%)
    pallas_call x19, Pallas kernels, call(): pl.pallas_call(inner, out_shape=out_shape, in_specs=ins + [ANY] * len(aft...  11.1 us
    ppermute x12, waiting for transfers between devices, crossed(): return lax.ppermute(array, BOTH, pairs)  10.3 us
    ppermute x12, starting transfers between devices, crossed(): return lax.ppermute(array, BOTH, pairs)  5.7 us
    ppermute x2, starting transfers between devices, local(): lax.ppermute(signal[0, rows - n * STEP:rows - n * STEP + STEP], 'tm', [(i...  4.48 us
    ppermute x2, waiting for transfers between devices, local(): lax.ppermute(signal[0, rows - n * STEP:rows - n * STEP + STEP], 'tm', [(i...  4.01 us
    ppermute x9, starting transfers between devices, swapped(): return lax.ppermute(array, BOTH, [(i, i ^ 1) for i in range(2 * chips)])  3.16 us
    ppermute x1, starting transfers between devices, fill(): results['relayed'] = lax.ppermute(results['back'], BOTH, relay_pairs())  2.32 us
    ppermute x9, waiting for transfers between devices, swapped(): return lax.ppermute(array, BOTH, [(i, i ^ 1) for i in range(2 * chips)])  1.86 us
  transfers between devices with their start and end apart: 25, of which 17 were waited for; matrix products, arithmetic and copies ran while one was open for 0% of the time, Pallas kernels for 19%

profile of v6, /device:TPU:0, one launch (start us, length us, event | category | flops | bytes accessed | tf_op | source)
XLA Modules:
  0.0 48.4 jit_solution(17433039408225915924)
XLA Ops:
  0.6 1.0 %slice_bitcast_fusion = (bf16[256,256]{1,0:T(8,128)(2,1)S(1)}, bf16[256,256]{1,0:T(8,128)(2,1)S(1)}) fusion(bf16[1,1024,256]{2,1,0:T(8,128)(2,1)} %param.6), kind=kLoop, calls=%fused_computation | loop fusion | bytes 524288 | tf_op jit(solution)/shard_map/squeeze | solution.py:548
  1.6 3.0 %collective-permute-start = (bf16[256,256]{1,0:T(8,128)(2,1)S(1)}, bf16[256,256]{1,0:T(8,128)(2,1)S(1)}, u32[]{:S(2)}, u32[]{:S(2)}) collective-permute-start(bf16[256,256]{1,0:T(8,128)(2,1)S(1)} %get-tuple-element.101), channel_id=1, source_target_pairs={{0,2},{2,4},{4,6},{6,8},{8,10},{10,12},{12,14},{14,16},{16,18},{18... | collective-permute-start | bytes 393224 | tf_op jit(solution)/shard_map/ppermute | solution.py:547
  4.6 1.5 %collective-permute-start.1 = (bf16[256,256]{1,0:T(8,128)(2,1)S(1)}, bf16[256,256]{1,0:T(8,128)(2,1)S(1)}, u32[]{:S(2)}, u32[]{:S(2)}) collective-permute-start(bf16[256,256]{1,0:T(8,128)(2,1)S(1)} %get-tuple-element.100), channel_id=1, source_target_pairs={{0,2},{2,4},{4,6},{6,8},{8,10},{10,12},{12,14},{14,16},{16,18},{18... | collective-permute-start | bytes 393224 | tf_op jit(solution)/shard_map/ppermute | solution.py:547
  6.1 0.7 %copy-done = f32[512]{0:T(512)S(1)} copy-done((f32[512]{0:T(512)S(1)}, f32[512]{0:T(512)}, u32[]{:S(2)}) %copy-start) | copy-done | bytes 2072
  6.8 3.3 %shard_map.109 = (bf16[1024,256]{1,0:T(8,128)(2,1)S(1)}, bf16[768,512]{1,0:T(8,128)(2,1)S(1)}, bf16[256,256]{1,0:T(8,128)(2,1)S(1)}, bf16[1024,256]{1,0:T(8,128)...) custom-call(bf16[1024,256]{1,0:T(8,128)(2,1)} %bitcast.14, ...), custom_call_target="tpu_custom_call" | custom-call | bytes 8 | tf_op jit(solution)/shard_map/pallas_call | solution.py:37
  10.1 2.8 %collective-permute-done.refs_0_ = bf16[256,256]{1,0:T(8,128)(2,1)S(1)} collective-permute-done((bf16[256,256]{1,0:T(8,128)(2,1)S(1)}, bf16[256,256]{1,0:T(8,128)(2,1)S(1)}, u32[]{:S(2)}, u32[]{:S(2)}) %collective-permute-start) | collective-permute-done | bytes 131104 | tf_op jit(solution)/shard_map/ppermute | solution.py:547
  12.9 0.8 %shard_map.110 = (bf16[256,256]{1,0:T(8,128)(2,1)S(1)}, bf16[256,512]{1,0:T(8,128)(2,1)S(1)}, f32[768,512]{1,0:T(8,128)S(1)}, f32[256,256]{1,0:T(8,128)S(1)}, f3...) custom-call(bf16[256,256]{1,0:T(8,128)(2,1)S(1)} %collective-permute-done.refs_0_, ...), custom_call_target="tpu_custom_call" | custom-call | bytes 8 | tf_op jit(solution)/shard_map/pallas_call | solution.py:37
  13.7 1.2 %collective-permute-done.1.refs_1_ = bf16[256,256]{1,0:T(8,128)(2,1)S(1)} collective-permute-done((bf16[256,256]{1,0:T(8,128)(2,1)S(1)}, bf16[256,256]{1,0:T(8,128)(2,1)S(1)}, u32[]{:S(2)}, u32[]{:S(2)}) %collective-permute-start.1) | collective-permute-done | bytes 131104 | tf_op jit(solution)/shard_map/ppermute | solution.py:547
  14.9 0.8 %shard_map.111 = (bf16[256,256]{1,0:T(8,128)(2,1)S(1)}, bf16[256,512]{1,0:T(8,128)(2,1)S(1)}, f32[904,128]{1,0:T(8,128)S(1)}, f32[904,128]{1,0:T(8,128)S(1)}, f3...) custom-call(bf16[256,256]{1,0:T(8,128)(2,1)S(1)} %collective-permute, ...), custom_call_target="tpu_custom_call" | custom-call | bytes 8 | tf_op jit(solution)/shard_map/pallas_call | solution.py:37
  15.8 0.1 collective-permute-start.2
  15.8 0.5 %collective-permute-start.4 = (bf16[912,128]{1,0:T(8,128)(2,1)S(1)}, bf16[912,128]{1,0:T(8,128)(2,1)S(1)}, u32[]{:S(2)}, u32[]{:S(2)}) collective-permute-start(bf16[912,128]{1,0:T(8,128)(2,1)S(1)} %get-tuple-element.78), channel_id=1, source_target_pairs={{0,1},{1,0},{2,3},{3,2},{4,5},{5,4},{6,7},{7,6},{8,9},{9,8},{10,11... | collective-permute-start | bytes 700424 | tf_op jit(solution)/shard_map/ppermute | solution.py:421
  16.3 0.1 collective-permute-start.6
  16.4 0.4 shard_map.114.refs_3_.refs_0_
  16.8 0.5 %collective-permute-done.2.received = bf16[912,128]{1,0:T(8,128)(2,1)S(1)} collective-permute-done((bf16[912,128]{1,0:T(8,128)(2,1)S(1)}, bf16[912,128]{1,0:T(8,128)(2,1)S(1)}, u32[]{:S(2)}, u32[]{:S(2)}) %collective-permute-start.2) | collective-permute-done | bytes 233504 | tf_op jit(solution)/shard_map/ppermute | solution.py:421
  17.4 0.2 collective-permute-done.4.refs_2_
  17.7 0.1 shard_map.115
  17.8 0.2 collective-permute-done.6.received
  18.1 2.3 %collective-permute-start.3 = (bf16[512,256]{1,0:T(8,128)(2,1)S(1)}, bf16[512,256]{1,0:T(8,128)(2,1)S(1)}, u32[]{:S(2)}, u32[]{:S(2)}) collective-permute-start(bf16[512,256]{1,0:T(8,128)(2,1)S(1)} %shard_map.114.refs_3_.refs_0_), channel_id=1, source_target_pairs={{0,24},{1,25},{2,3},{3,2},{4,5},{5,4},{6,7},{7,6},{8,0},{9,1},{10,... | collective-permute-start | bytes 786440 | tf_op jit(solution)/shard_map/ppermute | solution.py:588
  20.4 1.6 %shard_map.113 = (bf16[1024,256]{1,0:T(8,128)(2,1)}, f32[1024,256]{1,0:T(8,128)S(1)}, f32[8,128]{1,0:T(8,128)S(1)}) custom-call(bf16[1024,256]{1,0:T(8,128)(2,1)S(1)} %get-tuple-element.53.refs_1_.refs_2_.refs_0_, bf16[768,512]{1,0:T(8,128)(2,1)S(1)} %get-tuple-element.54.refs_2_.refs_3_.refs_1_, bf16[256,256]{1,0:T(8,128)(2,1)S(1)} %get-tuple-element.55.refs_2_, ...), custom_call_target="tpu_custom_call" | custom-call | bytes 8 | tf_op jit(solution)/shard_map/pallas_call | solution.py:37
  22.0 1.4 %collective-permute-done.8.refs_3_ = bf16[912,128]{1,0:T(8,128)(2,1)S(1)} collective-permute-done((bf16[912,128]{1,0:T(8,128)(2,1)S(1)}, bf16[912,128]{1,0:T(8,128)(2,1)S(1)}, u32[]{:S(2)}, u32[]{:S(2)}) %collective-permute-start.8) | collective-permute-done | bytes 233504 | tf_op jit(solution)/shard_map/ppermute | solution.py:428
  23.4 0.5 %collective-permute-done.7.refs_2_ = bf16[912,128]{1,0:T(8,128)(2,1)S(1)} collective-permute-done((bf16[912,128]{1,0:T(8,128)(2,1)S(1)}, bf16[912,128]{1,0:T(8,128)(2,1)S(1)}, u32[]{:S(2)}, u32[]{:S(2)}) %collective-permute-start.7) | collective-permute-done | bytes 233504 | tf_op jit(solution)/shard_map/ppermute | solution.py:428
  23.9 0.1 shard_map.117
  24.0 2.0 %collective-permute-start.11 = (bf16[240,128]{1,0:T(8,128)(2,1)S(1)}, bf16[240,128]{1,0:T(8,128)(2,1)S(1)}, u32[]{:S(2)}, u32[]{:S(2)}) collective-permute-start(bf16[240,128]{1,0:T(8,128)(2,1)S(1)} %get-tuple-element.87), channel_id=1, source_target_pairs={{1,24},{3,26},{5,28},{7,30},{9,16},{11,18},{13,20},{15,22},{17,8},... | collective-permute-start | bytes 184328 | tf_op jit(solution)/shard_map/ppermute | solution.py:428
  26.1 0.4 collective-permute-start.13
  26.4 1.0 %collective-permute-start.12 = (bf16[240,128]{1,0:T(8,128)(2,1)S(1)}, bf16[240,128]{1,0:T(8,128)(2,1)S(1)}, u32[]{:S(2)}, u32[]{:S(2)}) collective-permute-start(bf16[240,128]{1,0:T(8,128)(2,1)S(1)} %get-tuple-element.84.refs_2_), channel_id=1, source_target_pairs={{1,8},{3,10},{5,12},{7,14},{9,0},{11,2},{13,4},{15,6},{17,24},{19,... | collective-permute-start | bytes 184328 | tf_op jit(solution)/shard_map/ppermute | solution.py:428
  27.5 1.3 %collective-permute-start.9 = (bf16[512,256]{1,0:T(8,128)(2,1)S(1)}, bf16[512,256]{1,0:T(8,128)(2,1)S(1)}, u32[]{:S(2)}, u32[]{:S(2)}) collective-permute-start(bf16[512,256]{1,0:T(8,128)(2,1)S(1)} %shard_map.118), channel_id=1, source_target_pairs={{0,6},{2,0},{4,2},{6,4},{8,14},{10,8},{12,10},{14,12},{16,22},{18,... | collective-permute-start | bytes 786440 | tf_op jit(solution)/shard_map/ppermute | solution.py:608
  28.8 1.0 %collective-permute-done.11.refs_0_ = bf16[240,128]{1,0:T(8,128)(2,1)S(1)} collective-permute-done((bf16[240,128]{1,0:T(8,128)(2,1)S(1)}, bf16[240,128]{1,0:T(8,128)(2,1)S(1)}, u32[]{:S(2)}, u32[]{:S(2)}) %collective-permute-start.11) | collective-permute-done | bytes 61472 | tf_op jit(solution)/shard_map/ppermute | solution.py:428
  29.8 1.3 %collective-permute-done.13.refs_2_ = bf16[240,128]{1,0:T(8,128)(2,1)S(1)} collective-permute-done((bf16[240,128]{1,0:T(8,128)(2,1)S(1)}, bf16[240,128]{1,0:T(8,128)(2,1)S(1)}, u32[]{:S(2)}, u32[]{:S(2)}) %collective-permute-start.13) | collective-permute-done | bytes 61472 | tf_op jit(solution)/shard_map/ppermute | solution.py:428
  31.3 0.8 %collective-permute-start.16 = (bf16[240,128]{1,0:T(8,128)(2,1)S(1)}, bf16[240,128]{1,0:T(8,128)(2,1)S(1)}, u32[]{:S(2)}, u32[]{:S(2)}) collective-permute-start(bf16[240,128]{1,0:T(8,128)(2,1)S(1)} %shard_map.121.refs_1_), channel_id=1, source_target_pairs={{0,17},{2,19},{4,21},{6,23},{8,25},{10,27},{12,29},{14,31},{16,1},... | collective-permute-start | bytes 184328 | tf_op jit(solution)/shard_map/ppermute | solution.py:428
  32.1 0.5 %collective-permute-start.14 = (bf16[240,128]{1,0:T(8,128)(2,1)S(1)}, bf16[240,128]{1,0:T(8,128)(2,1)S(1)}, u32[]{:S(2)}, u32[]{:S(2)}) collective-permute-start(bf16[240,128]{1,0:T(8,128)(2,1)S(1)} %shard_map.121.refs_1_), channel_id=1, source_target_pairs={{0,1},{1,0},{2,3},{3,2},{4,5},{5,4},{6,7},{7,6},{8,9},{9,8},{10,11... | collective-permute-start | bytes 184328 | tf_op jit(solution)/shard_map/ppermute | solution.py:421
  32.6 0.5 %collective-permute-done.17.refs_4_ = bf16[240,128]{1,0:T(8,128)(2,1)S(1)} collective-permute-done((bf16[240,128]{1,0:T(8,128)(2,1)S(1)}, bf16[240,128]{1,0:T(8,128)(2,1)S(1)}, u32[]{:S(2)}, u32[]{:S(2)}) %collective-permute-start.17) | collective-permute-done | bytes 61472 | tf_op jit(solution)/shard_map/ppermute | solution.py:428
  33.2 0.8 %collective-permute-done.16.refs_3_ = bf16[240,128]{1,0:T(8,128)(2,1)S(1)} collective-permute-done((bf16[240,128]{1,0:T(8,128)(2,1)S(1)}, bf16[240,128]{1,0:T(8,128)(2,1)S(1)}, u32[]{:S(2)}, u32[]{:S(2)}) %collective-permute-start.16) | collective-permute-done | bytes 61472 | tf_op jit(solution)/shard_map/ppermute | solution.py:428
  34.0 0.6 %collective-permute-done.15.refs_2_ = bf16[240,128]{1,0:T(8,128)(2,1)S(1)} collective-permute-done((bf16[240,128]{1,0:T(8,128)(2,1)S(1)}, bf16[240,128]{1,0:T(8,128)(2,1)S(1)}, u32[]{:S(2)}, u32[]{:S(2)}) %collective-permute-start.15) | collective-permute-done | bytes 61472 | tf_op jit(solution)/shard_map/ppermute | solution.py:428
  34.6 1.7 %collective-permute-done.9.incoming.refs_5_ = bf16[512,256]{1,0:T(8,128)(2,1)S(1)} collective-permute-done((bf16[512,256]{1,0:T(8,128)(2,1)S(1)}, bf16[512,256]{1,0:T(8,128)(2,1)S(1)}, u32[]{:S(2)}, u32[]{:S(2)}) %collective-permute-start.9) | collective-permute-done | bytes 262176 | tf_op jit(solution)/shard_map/ppermute | solution.py:608
  36.3 0.7 %collective-permute-start.20 = (bf16[912,128]{1,0:T(8,128)(2,1)S(1)}, bf16[912,128]{1,0:T(8,128)(2,1)S(1)}, u32[]{:S(2)}, u32[]{:S(2)}) collective-permute-start(bf16[912,128]{1,0:T(8,128)(2,1)S(1)} %shard_map.122.refs_0_), channel_id=1, source_target_pairs={{1,6},{3,4},{5,2},{7,0},{9,14},{11,12},{13,10},{15,8},{17,22},{19,... | collective-permute-start | bytes 700424 | tf_op jit(solution)/shard_map/ppermute | solution.py:428
  37.1 1.6 %collective-permute-start.23 = (bf16[912,128]{1,0:T(8,128)(2,1)S(1)}, bf16[912,128]{1,0:T(8,128)(2,1)S(1)}, u32[]{:S(2)}, u32[]{:S(2)}) collective-permute-start(bf16[912,128]{1,0:T(8,128)(2,1)S(1)} %shard_map.122.refs_0_), channel_id=1, source_target_pairs={{0,1},{1,0},{2,3},{3,2},{4,5},{5,4},{6,7},{7,6},{8,9},{9,8},{10,11... | collective-permute-start | bytes 700424 | tf_op jit(solution)/shard_map/ppermute | solution.py:421
  38.7 0.5 %collective-permute-start.18 = (bf16[912,128]{1,0:T(8,128)(2,1)S(1)}, bf16[912,128]{1,0:T(8,128)(2,1)S(1)}, u32[]{:S(2)}, u32[]{:S(2)}) collective-permute-start(bf16[912,128]{1,0:T(8,128)(2,1)S(1)} %shard_map.122.refs_0_), channel_id=1, source_target_pairs={{1,4},{3,6},{5,0},{7,2},{9,12},{11,14},{13,8},{15,10},{17,20},{19,... | collective-permute-start | bytes 700424 | tf_op jit(solution)/shard_map/ppermute | solution.py:428
  39.2 0.9 %shard_map.119 = (bf16[1024,256]{1,0:T(8,128)(2,1)}, f32[8,128]{1,0:T(8,128)S(1)}) custom-call(f32[1024,256]{1,0:T(8,128)S(1)} %get-tuple-element.75.partial, bf16[512,256]{1,0:T(8,128)(2,1)S(1)} %collective-permute-done.9.incoming.refs_5_), custom_call_target="tpu_custom_call" | custom-call | bytes 8 | tf_op jit(solution)/shard_map/pallas_call | solution.py:37
  40.1 2.8 %collective-permute-done.20.refs_0_ = bf16[912,128]{1,0:T(8,128)(2,1)S(1)} collective-permute-done((bf16[912,128]{1,0:T(8,128)(2,1)S(1)}, bf16[912,128]{1,0:T(8,128)(2,1)S(1)}, u32[]{:S(2)}, u32[]{:S(2)}) %collective-permute-start.20) | collective-permute-done | bytes 233504 | tf_op jit(solution)/shard_map/ppermute | solution.py:428
  42.9 0.1 collective-permute-start.22
  43.0 0.9 %shard_map.124 = (f32[768,512]{1,0:T(8,128)}, f32[256,256]{1,0:T(8,128)}, f32[8,128]{1,0:T(8,128)S(1)}) custom-call(bf16[912,128]{1,0:T(8,128)(2,1)S(1)} %shard_map.122.refs_0_, bf16[912,128]{1,0:T(8,128)(2,1)S(1)} %collective-permute-done.23.refs_1_), custom_call_target="tpu_custom_call" | custom-call | bytes 8 | tf_op jit(solution)/shard_map/pallas_call | solution.py:37
  43.9 1.1 %collective-permute-done.21.refs_0_.refs_1_ = bf16[912,128]{1,0:T(8,128)(2,1)S(1)} collective-permute-done((bf16[912,128]{1,0:T(8,128)(2,1)S(1)}, bf16[912,128]{1,0:T(8,128)(2,1)S(1)}, u32[]{:S(2)}, u32[]{:S(2)}) %collective-permute-start.21) | collective-permute-done | bytes 233504 | tf_op jit(solution)/shard_map/ppermute | solution.py:428
  44.9 0.1 collective-permute-start.24
  45.0 0.2 collective-permute-done.18.refs_0_
  45.3 0.2 collective-permute-start.19
  45.5 1.0 %collective-permute-done.24.refs_3_ = bf16[912,128]{1,0:T(8,128)(2,1)S(1)} collective-permute-done((bf16[912,128]{1,0:T(8,128)(2,1)S(1)}, bf16[912,128]{1,0:T(8,128)(2,1)S(1)}, u32[]{:S(2)}, u32[]{:S(2)}) %collective-permute-start.24) | collective-permute-done | bytes 233504 | tf_op jit(solution)/shard_map/ppermute | solution.py:421
  46.5 1.0 %shard_map.126 = (f32[768,512]{1,0:T(8,128)}, f32[256,256]{1,0:T(8,128)}, f32[8,128]{1,0:T(8,128)S(1)}) custom-call(bf16[912,128]{1,0:T(8,128)(2,1)S(1)} %collective-permute-done.20.refs_0_, bf16[912,128]{1,0:T(8,128)(2,1)S(1)} %collective-permute-done.21.refs_0_.refs_1_, ...), custom_call_target="tpu_custom_call", output_to_operand_aliasing={{0}: (5, {}), {1}: (6, {})} | custom-call | bytes 8 | tf_op jit(solution)/shard_map/pallas_call | solution.py:37
  47.6 0.9 %shard_map.127 = (f32[768,512]{1,0:T(8,128)}, f32[256,256]{1,0:T(8,128)}, f32[1,512]{1,0:T(1,128)}, f32[1,256]{1,0:T(1,128)}) custom-call(bf16[912,128]{1,0:T(8,128)(2,1)S(1)} %collective-permute-done.18.refs_0_, bf16[912,128]{1,0:T(8,128)(2,1)S(1)} %collective-permute-done.19.refs_1_, ...), custom_call_target="tpu_custom_call", output_to_operand_aliasing={{0}: (3, {}), {1}: (4, {})} | custom-call | bytes 8 | tf_op jit(solution)/shard_map/pallas_call | solution.py:37
  (26 shorter events, 0.6 us)
Async XLA Ops:
  1.6 11.3 %collective-permute-start = (bf16[256,256]{1,0:T(8,128)(2,1)S(1)}, bf16[256,256]{1,0:T(8,128)(2,1)S(1)}, u32[]{:S(2)}, u32[]{:S(2)}) collective-permute-start(bf16[256,256]{1,0:T(8,128)(2,1)S(1)} %get-tuple-element.101), channel_id=1, source_target_pairs={{0,2},{2,4},{4,6},{6,8},{8,10},{10,12},{12,14},{14,16},{16,18},{18... | collective-permute-start | bytes 393224 | tf_op jit(solution)/shard_map/ppermute | solution.py:547
  4.6 10.3 %collective-permute-start.1 = (bf16[256,256]{1,0:T(8,128)(2,1)S(1)}, bf16[256,256]{1,0:T(8,128)(2,1)S(1)}, u32[]{:S(2)}, u32[]{:S(2)}) collective-permute-start(bf16[256,256]{1,0:T(8,128)(2,1)S(1)} %get-tuple-element.100), channel_id=1, source_target_pairs={{0,2},{2,4},{4,6},{6,8},{8,10},{10,12},{12,14},{14,16},{16,18},{18... | collective-permute-start | bytes 393224 | tf_op jit(solution)/shard_map/ppermute | solution.py:547
  6.1 0.7 %copy-start = (f32[512]{0:T(512)S(1)}, f32[512]{0:T(512)}, u32[]{:S(2)}) copy-start(f32[512]{0:T(512)} %param.8) | copy-start | bytes 6148
  15.8 1.6 %collective-permute-start.2 = (bf16[912,128]{1,0:T(8,128)(2,1)S(1)}, bf16[912,128]{1,0:T(8,128)(2,1)S(1)}, u32[]{:S(2)}, u32[]{:S(2)}) collective-permute-start(bf16[912,128]{1,0:T(8,128)(2,1)S(1)} %get-tuple-element.73), channel_id=1, source_target_pairs={{0,1},{1,0},{2,3},{3,2},{4,5},{5,4},{6,7},{7,6},{8,9},{9,8},{10,11... | collective-permute-start | bytes 700424 | tf_op jit(solution)/shard_map/ppermute | solution.py:421
  15.8 1.8 %collective-permute-start.4 = (bf16[912,128]{1,0:T(8,128)(2,1)S(1)}, bf16[912,128]{1,0:T(8,128)(2,1)S(1)}, u32[]{:S(2)}, u32[]{:S(2)}) collective-permute-start(bf16[912,128]{1,0:T(8,128)(2,1)S(1)} %get-tuple-element.78), channel_id=1, source_target_pairs={{0,1},{1,0},{2,3},{3,2},{4,5},{5,4},{6,7},{7,6},{8,9},{9,8},{10,11... | collective-permute-start | bytes 700424 | tf_op jit(solution)/shard_map/ppermute | solution.py:421
  16.3 1.7 %collective-permute-start.6 = (bf16[912,128]{1,0:T(8,128)(2,1)S(1)}, bf16[912,128]{1,0:T(8,128)(2,1)S(1)}, u32[]{:S(2)}, u32[]{:S(2)}) collective-permute-start(bf16[912,128]{1,0:T(8,128)(2,1)S(1)} %get-tuple-element.82), channel_id=1, source_target_pairs={{0,1},{1,0},{2,3},{3,2},{4,5},{5,4},{6,7},{7,6},{8,9},{9,8},{10,11... | collective-permute-start | bytes 700424 | tf_op jit(solution)/shard_map/ppermute | solution.py:421
  17.3 3.1 %copy-start.1 = (f32[256]{0:T(256)S(1)}, f32[256]{0:T(256)}, u32[]{:S(2)}) copy-start(f32[256]{0:T(256)} %param.10) | copy-start | bytes 3076
  17.4 6.0 %collective-permute-start.8 = (bf16[912,128]{1,0:T(8,128)(2,1)S(1)}, bf16[912,128]{1,0:T(8,128)(2,1)S(1)}, u32[]{:S(2)}, u32[]{:S(2)}) collective-permute-start(bf16[912,128]{1,0:T(8,128)(2,1)S(1)} %shard_map.112.refs_11_), channel_id=1, source_target_pairs={{0,5},{2,7},{4,1},{6,3},{8,13},{10,15},{12,9},{14,11},{16,21},{18,... | collective-permute-start | bytes 700424 | tf_op jit(solution)/shard_map/ppermute | solution.py:428
  17.7 5.6 %collective-permute-start.5 = (bf16[912,128]{1,0:T(8,128)(2,1)S(1)}, bf16[912,128]{1,0:T(8,128)(2,1)S(1)}, u32[]{:S(2)}, u32[]{:S(2)}) collective-permute-start(bf16[912,128]{1,0:T(8,128)(2,1)S(1)} %get-tuple-element.80), channel_id=1, source_target_pairs={{0,7},{2,5},{4,3},{6,1},{8,15},{10,13},{12,11},{14,9},{16,23},{18,... | collective-permute-start | bytes 700424 | tf_op jit(solution)/shard_map/ppermute | solution.py:428
  18.0 5.8 %collective-permute-start.7 = (bf16[912,128]{1,0:T(8,128)(2,1)S(1)}, bf16[912,128]{1,0:T(8,128)(2,1)S(1)}, u32[]{:S(2)}, u32[]{:S(2)}) collective-permute-start(bf16[912,128]{1,0:T(8,128)(2,1)S(1)} %shard_map.116), channel_id=1, source_target_pairs={{0,3},{2,1},{4,7},{6,5},{8,11},{10,9},{12,15},{14,13},{16,19},{18,... | collective-permute-start | bytes 700424 | tf_op jit(solution)/shard_map/ppermute | solution.py:428
  18.1 9.3 %collective-permute-start.3 = (bf16[512,256]{1,0:T(8,128)(2,1)S(1)}, bf16[512,256]{1,0:T(8,128)(2,1)S(1)}, u32[]{:S(2)}, u32[]{:S(2)}) collective-permute-start(bf16[512,256]{1,0:T(8,128)(2,1)S(1)} %shard_map.114.refs_3_.refs_0_), channel_id=1, source_target_pairs={{0,24},{1,25},{2,3},{3,2},{4,5},{5,4},{6,7},{7,6},{8,0},{9,1},{10,... | collective-permute-start | bytes 786440 | tf_op jit(solution)/shard_map/ppermute | solution.py:588
  24.0 5.8 %collective-permute-start.11 = (bf16[240,128]{1,0:T(8,128)(2,1)S(1)}, bf16[240,128]{1,0:T(8,128)(2,1)S(1)}, u32[]{:S(2)}, u32[]{:S(2)}) collective-permute-start(bf16[240,128]{1,0:T(8,128)(2,1)S(1)} %get-tuple-element.87), channel_id=1, source_target_pairs={{1,24},{3,26},{5,28},{7,30},{9,16},{11,18},{13,20},{15,22},{17,8},... | collective-permute-start | bytes 184328 | tf_op jit(solution)/shard_map/ppermute | solution.py:428
  26.1 5.1 %collective-permute-start.13 = (bf16[240,128]{1,0:T(8,128)(2,1)S(1)}, bf16[240,128]{1,0:T(8,128)(2,1)S(1)}, u32[]{:S(2)}, u32[]{:S(2)}) collective-permute-start(bf16[240,128]{1,0:T(8,128)(2,1)S(1)} %get-tuple-element.88), channel_id=1, source_target_pairs={{1,16},{3,18},{5,20},{7,22},{9,24},{11,26},{13,28},{15,30},{17,0},... | collective-permute-start | bytes 184328 | tf_op jit(solution)/shard_map/ppermute | solution.py:428
  26.4 4.7 %collective-permute-start.12 = (bf16[240,128]{1,0:T(8,128)(2,1)S(1)}, bf16[240,128]{1,0:T(8,128)(2,1)S(1)}, u32[]{:S(2)}, u32[]{:S(2)}) collective-permute-start(bf16[240,128]{1,0:T(8,128)(2,1)S(1)} %get-tuple-element.84.refs_2_), channel_id=1, source_target_pairs={{1,8},{3,10},{5,12},{7,14},{9,0},{11,2},{13,4},{15,6},{17,24},{19,... | collective-permute-start | bytes 184328 | tf_op jit(solution)/shard_map/ppermute | solution.py:428
  27.4 3.8 %collective-permute-start.10 = (f32[232,128]{1,0:T(8,128)S(1)}, f32[232,128]{1,0:T(8,128)S(1)}, u32[]{:S(2)}, u32[]{:S(2)}) collective-permute-start(f32[232,128]{1,0:T(8,128)S(1)} %get-tuple-element.86), channel_id=1, source_target_pairs={{0,1},{1,0},{2,3},{3,2},{4,5},{5,4},{6,7},{7,6},{8,9},{9,8},{10,11... | collective-permute-start | bytes 356360 | tf_op jit(solution)/shard_map/ppermute | solution.py:421
  27.5 8.8 %collective-permute-start.9 = (bf16[512,256]{1,0:T(8,128)(2,1)S(1)}, bf16[512,256]{1,0:T(8,128)(2,1)S(1)}, u32[]{:S(2)}, u32[]{:S(2)}) collective-permute-start(bf16[512,256]{1,0:T(8,128)(2,1)S(1)} %shard_map.118), channel_id=1, source_target_pairs={{0,6},{2,0},{4,2},{6,4},{8,14},{10,8},{12,10},{14,12},{16,22},{18,... | collective-permute-start | bytes 786440 | tf_op jit(solution)/shard_map/ppermute | solution.py:608
  31.2 1.9 %collective-permute-start.17 = (bf16[240,128]{1,0:T(8,128)(2,1)S(1)}, bf16[240,128]{1,0:T(8,128)(2,1)S(1)}, u32[]{:S(2)}, u32[]{:S(2)}) collective-permute-start(bf16[240,128]{1,0:T(8,128)(2,1)S(1)} %shard_map.121.refs_1_), channel_id=1, source_target_pairs={{0,25},{2,27},{4,29},{6,31},{8,17},{10,19},{12,21},{14,23},{16,9},... | collective-permute-start | bytes 184328 | tf_op jit(solution)/shard_map/ppermute | solution.py:428
  31.3 2.7 %collective-permute-start.16 = (bf16[240,128]{1,0:T(8,128)(2,1)S(1)}, bf16[240,128]{1,0:T(8,128)(2,1)S(1)}, u32[]{:S(2)}, u32[]{:S(2)}) collective-permute-start(bf16[240,128]{1,0:T(8,128)(2,1)S(1)} %shard_map.121.refs_1_), channel_id=1, source_target_pairs={{0,17},{2,19},{4,21},{6,23},{8,25},{10,27},{12,29},{14,31},{16,1},... | collective-permute-start | bytes 184328 | tf_op jit(solution)/shard_map/ppermute | solution.py:428
  32.1 2.4 %collective-permute-start.15 = (bf16[240,128]{1,0:T(8,128)(2,1)S(1)}, bf16[240,128]{1,0:T(8,128)(2,1)S(1)}, u32[]{:S(2)}, u32[]{:S(2)}) collective-permute-start(bf16[240,128]{1,0:T(8,128)(2,1)S(1)} %shard_map.121.refs_1_), channel_id=1, source_target_pairs={{0,9},{2,11},{4,13},{6,15},{8,1},{10,3},{12,5},{14,7},{16,25},{18,... | collective-permute-start | bytes 184328 | tf_op jit(solution)/shard_map/ppermute | solution.py:428
  32.1 2.4 %collective-permute-start.14 = (bf16[240,128]{1,0:T(8,128)(2,1)S(1)}, bf16[240,128]{1,0:T(8,128)(2,1)S(1)}, u32[]{:S(2)}, u32[]{:S(2)}) collective-permute-start(bf16[240,128]{1,0:T(8,128)(2,1)S(1)} %shard_map.121.refs_1_), channel_id=1, source_target_pairs={{0,1},{1,0},{2,3},{3,2},{4,5},{5,4},{6,7},{7,6},{8,9},{9,8},{10,11... | collective-permute-start | bytes 184328 | tf_op jit(solution)/shard_map/ppermute | solution.py:421
  36.3 6.5 %collective-permute-start.20 = (bf16[912,128]{1,0:T(8,128)(2,1)S(1)}, bf16[912,128]{1,0:T(8,128)(2,1)S(1)}, u32[]{:S(2)}, u32[]{:S(2)}) collective-permute-start(bf16[912,128]{1,0:T(8,128)(2,1)S(1)} %shard_map.122.refs_0_), channel_id=1, source_target_pairs={{1,6},{3,4},{5,2},{7,0},{9,14},{11,12},{13,10},{15,8},{17,22},{19,... | collective-permute-start | bytes 700424 | tf_op jit(solution)/shard_map/ppermute | solution.py:428
  37.1 5.9 %collective-permute-start.23 = (bf16[912,128]{1,0:T(8,128)(2,1)S(1)}, bf16[912,128]{1,0:T(8,128)(2,1)S(1)}, u32[]{:S(2)}, u32[]{:S(2)}) collective-permute-start(bf16[912,128]{1,0:T(8,128)(2,1)S(1)} %shard_map.122.refs_0_), channel_id=1, source_target_pairs={{0,1},{1,0},{2,3},{3,2},{4,5},{5,4},{6,7},{7,6},{8,9},{9,8},{10,11... | collective-permute-start | bytes 700424 | tf_op jit(solution)/shard_map/ppermute | solution.py:421
  38.7 6.3 %collective-permute-start.21 = (bf16[912,128]{1,0:T(8,128)(2,1)S(1)}, bf16[912,128]{1,0:T(8,128)(2,1)S(1)}, u32[]{:S(2)}, u32[]{:S(2)}) collective-permute-start(bf16[912,128]{1,0:T(8,128)(2,1)S(1)} %shard_map.122.refs_0_), channel_id=1, source_target_pairs={{1,2},{3,0},{5,6},{7,4},{9,10},{11,8},{13,14},{15,12},{17,18},{19,... | collective-permute-start | bytes 700424 | tf_op jit(solution)/shard_map/ppermute | solution.py:428
  38.7 6.6 %collective-permute-start.18 = (bf16[912,128]{1,0:T(8,128)(2,1)S(1)}, bf16[912,128]{1,0:T(8,128)(2,1)S(1)}, u32[]{:S(2)}, u32[]{:S(2)}) collective-permute-start(bf16[912,128]{1,0:T(8,128)(2,1)S(1)} %shard_map.122.refs_0_), channel_id=1, source_target_pairs={{1,4},{3,6},{5,0},{7,2},{9,12},{11,14},{13,8},{15,10},{17,20},{19,... | collective-permute-start | bytes 700424 | tf_op jit(solution)/shard_map/ppermute | solution.py:428
  42.9 2.6 %collective-permute-start.22 = (bf16[912,128]{1,0:T(8,128)(2,1)S(1)}, bf16[912,128]{1,0:T(8,128)(2,1)S(1)}, u32[]{:S(2)}, u32[]{:S(2)}) collective-permute-start(bf16[912,128]{1,0:T(8,128)(2,1)S(1)} %shard_map.123), channel_id=1, source_target_pairs={{0,1},{1,0},{2,3},{3,2},{4,5},{5,4},{6,7},{7,6},{8,9},{9,8},{10,11... | collective-permute-start | bytes 700424 | tf_op jit(solution)/shard_map/ppermute | solution.py:421
  44.9 1.6 %collective-permute-start.24 = (bf16[912,128]{1,0:T(8,128)(2,1)S(1)}, bf16[912,128]{1,0:T(8,128)(2,1)S(1)}, u32[]{:S(2)}, u32[]{:S(2)}) collective-permute-start(bf16[912,128]{1,0:T(8,128)(2,1)S(1)} %shard_map.125), channel_id=1, source_target_pairs={{0,1},{1,0},{2,3},{3,2},{4,5},{5,4},{6,7},{7,6},{8,9},{9,8},{10,11... | collective-permute-start | bytes 700424 | tf_op jit(solution)/shard_map/ppermute | solution.py:421
  45.3 2.3 %collective-permute-start.19 = (bf16[912,128]{1,0:T(8,128)(2,1)S(1)}, bf16[912,128]{1,0:T(8,128)(2,1)S(1)}, u32[]{:S(2)}, u32[]{:S(2)}) collective-permute-start(bf16[912,128]{1,0:T(8,128)(2,1)S(1)} %collective-permute-done.18.refs_0_), channel_id=1, source_target_pairs={{0,1},{1,0},{2,3},{3,2},{4,5},{5,4},{6,7},{7,6},{8,9},{9,8},{10,11... | collective-permute-start | bytes 700424 | tf_op jit(solution)/shard_map/ppermute | solution.py:421
